TPU v7x, 256 devices: a whole 4x4x8 slice. The times are simulated.
256 devices in a mesh: dp: 4 (over y_lo, core), pipe: 64 (over z, x, y_hi).
Axes of the slice: x: 4, y: 4 (y_hi: 2, y_lo: 2; y = y_hi * 2 + y_lo), z: 8, core: 2. Of those that a mesh axis runs over, the one named last changes fastest.
Arguments:
- acts_in: bfloat16 [4, 64, 2, 1536, 32], P('dp', 'pipe'), may hold values from -6 to 6
- cot_in: bfloat16 [4, 64, 2, 1536, 32], P('dp', 'pipe'), may hold values from -6 to 6
- stash: bfloat16 [4, 64, 2, 2, 1536, 32], P('dp', 'pipe'), may hold values from -6 to 6
- entering: bfloat16 [4, 2, 1536, 32], P('dp'), may hold values from -6 to 6
- pattern: int32 [64, 2, 72], replicated, may hold values from 0 to 2303, as said below
- weights: bfloat16 [64, 2, 2, 72, 4096], P('pipe'), may hold values from -0.5 to 0.5
- momentum: float32 [64, 2, 2, 72, 4096], P('pipe', None, None, 'dp'), may hold values from -0.6 to 0.6
Outputs:
- forward_out: bfloat16 [4, 64, 2, 1536, 32], P('dp', 'pipe')
- backward_out: bfloat16 [4, 64, 2, 1536, 32], P('dp', 'pipe')
- weights_next: bfloat16 [64, 2, 2, 72, 4096], P('pipe', None, None, 'dp')
- momentum_next: float32 [64, 2, 2, 72, 4096], P('pipe', None, None, 'dp')
Inputs may be any that keep to these rules, and one draw needn't show every extreme that they name: pattern[s, 0] lists 72 different blocks of section s's up projection, pattern[s, 1] 72 different blocks of its down projection, in no particular order.
All inputs are finite; a program needn't handle non-finite values.
Results may differ from a plain program's by a relative error of at most 0.012.
Values may be sent and summed in bfloat16 or wider, within the bound.
A program may use at most 128 MiB of HBM per device.

v0:
```python
import jax
import jax.numpy as jnp
from jax import lax
from jax.sharding import PartitionSpec as P

FF = 6144
BLOCK = 64


beta_coef = 0.9
step_size = 0.2


def shifted(value, axis, steps):
    count = lax.axis_size(axis)
    first, last = (max(0, -steps), min(count, count - steps))
    return lax.ppermute(value, axis, [(source, source + steps) for source in range(first, last)])


def from_partner(value, axis, distance):
    mask = 2**distance
    pairs = [(source, source ^ mask) for source in range(lax.axis_size(axis))]
    return lax.ppermute(value, axis, pairs)


def gelu_exact(values):
    return jax.nn.gelu(values, approximate=False)


def block_product(spec, left, right):
    return jnp.einsum(spec, left, right, preferred_element_type=jnp.float32)


def select_table(indices, count):
    return indices[:, None] == jnp.arange(count, dtype=jnp.int32)[None, :]


def pick_blocks(table, source):
    return jnp.einsum(
        "nb,bir->nir", table.astype(jnp.bfloat16), source, preferred_element_type=jnp.float32
    ).astype(jnp.bfloat16)


def add_blocks(table, terms):
    return jnp.einsum(
        "nb,njr->bjr",
        table.astype(jnp.float32),
        terms,
        precision=lax.Precision.HIGHEST,
        preferred_element_type=jnp.float32,
    )


def split_pattern(inputs, section_pattern):
    blocks_d = inputs.shape[0] // BLOCK
    blocks_f = FF // BLOCK
    return (
        blocks_d,
        blocks_f,
        select_table(section_pattern[0] // blocks_f, blocks_d),
        select_table(section_pattern[0] % blocks_f, blocks_f),
        select_table(section_pattern[1] // blocks_d, blocks_f),
        select_table(section_pattern[1] % blocks_d, blocks_d),
    )


def hidden_state(inputs, section_weights, tables):
    blocks_d, blocks_f, up_rows, up_cols, down_rows, down_cols = tables
    count = section_weights.shape[1]
    up_blocks = section_weights[0].reshape(count, BLOCK, BLOCK)
    input_blocks = pick_blocks(up_rows, inputs.reshape(blocks_d, BLOCK, -1))
    preact = add_blocks(up_cols, block_product("nij,nir->njr", up_blocks, input_blocks))
    hidden_act = gelu_exact(preact).astype(jnp.bfloat16)
    return (preact, hidden_act, input_blocks)


def section_forward(inputs, section_weights, section_pattern):
    tables = split_pattern(inputs, section_pattern)
    blocks_d, blocks_f, up_rows, up_cols, down_rows, down_cols = tables
    count = section_weights.shape[1]
    preact, hidden_act, input_blocks = hidden_state(inputs, section_weights, tables)
    down_blocks = section_weights[1].reshape(count, BLOCK, BLOCK)
    act_blocks = pick_blocks(down_rows, hidden_act)
    output = add_blocks(down_cols, block_product("nij,nir->njr", down_blocks, act_blocks))
    return (inputs.astype(jnp.float32) + output.reshape(inputs.shape)).astype(jnp.bfloat16)


def section_backward(inputs, grad_out, section_weights, section_pattern):
    tables = split_pattern(inputs, section_pattern)
    blocks_d, blocks_f, up_rows, up_cols, down_rows, down_cols = tables
    count = section_weights.shape[1]
    preact, hidden_act, input_blocks = hidden_state(inputs, section_weights, tables)
    up_blocks = section_weights[0].reshape(count, BLOCK, BLOCK)
    down_blocks = section_weights[1].reshape(count, BLOCK, BLOCK)
    act_blocks = pick_blocks(down_rows, hidden_act)
    grad_blocks = pick_blocks(down_cols, grad_out.reshape(blocks_d, BLOCK, -1))
    grad_act = add_blocks(down_rows, block_product("nij,njr->nir", down_blocks, grad_blocks))
    pullback = jax.vjp(gelu_exact, preact)[1]
    grad_pre = pullback(grad_act)[0].astype(jnp.bfloat16)
    pre_blocks = pick_blocks(up_cols, grad_pre)
    back = add_blocks(up_rows, block_product("nij,njr->nir", up_blocks, pre_blocks))
    grad_in = (grad_out.astype(jnp.float32) + back.reshape(grad_out.shape)).astype(jnp.bfloat16)
    grad_up = block_product("nir,njr->nij", input_blocks, pre_blocks).reshape(count, -1)
    grad_down = block_product("nir,njr->nij", act_blocks, grad_blocks).reshape(count, -1)
    return (grad_in, jnp.stack([grad_up, grad_down]))


def shards(acts_in, cot_in, stash, entering, pattern, weights, momentum):
    device_pos = lax.axis_index("pipe")
    section_count = lax.axis_size("pipe")
    patterns_here = jnp.stack(
        [
            lax.dynamic_index_in_dim(pattern, device_pos, 0, keepdims=False),
            lax.dynamic_index_in_dim(pattern, section_count - 1 - device_pos, 0, keepdims=False),
        ]
    )
    section_weights = weights[0]
    first_inputs = acts_in[0, 0]
    first_cots = cot_in[0, 0]
    saved_inputs = stash[0, 0]
    fresh_inputs = entering[0]
    outputs_first = [
        section_forward(first_inputs[copy_idx], section_weights[copy_idx], patterns_here[copy_idx])
        for copy_idx in range(2)
    ]
    backs_first = [
        section_backward(
            saved_inputs[copy_idx, 0],
            first_cots[copy_idx],
            section_weights[copy_idx],
            patterns_here[copy_idx],
        )
        for copy_idx in range(2)
    ]
    recv_copy0 = shifted(outputs_first[0], "pipe", 1)
    recv_copy1 = shifted(outputs_first[1], "pipe", -1)
    back_copy0 = shifted(backs_first[0][0], "pipe", -1)
    back_copy1 = shifted(backs_first[1][0], "pipe", 1)
    at_entry = device_pos == 0
    at_exit = device_pos == section_count - 1
    second_inputs = [
        jnp.where(at_entry, fresh_inputs[0], recv_copy0),
        jnp.where(at_exit, fresh_inputs[1], recv_copy1),
    ]
    second_cots = [
        jnp.where(at_exit, outputs_first[0], back_copy0),
        jnp.where(at_entry, outputs_first[1], back_copy1),
    ]
    second_saved = [
        jnp.where(at_exit, first_inputs[0], saved_inputs[0, 1]),
        jnp.where(at_entry, first_inputs[1], saved_inputs[1, 1]),
    ]
    outputs_second = []
    backs_second = []
    grads_local = []
    for copy_idx in range(2):
        outputs_second.append(
            section_forward(
                second_inputs[copy_idx], section_weights[copy_idx], patterns_here[copy_idx]
            )
        )
        grad_in, late_grads = section_backward(
            second_saved[copy_idx],
            second_cots[copy_idx],
            section_weights[copy_idx],
            patterns_here[copy_idx],
        )
        backs_second.append(grad_in)
        grads_local.append(backs_first[copy_idx][1] + late_grads)
    grad_share = lax.psum_scatter(
        jnp.stack(grads_local).astype(jnp.bfloat16), "dp", scatter_dimension=2, tiled=True
    ).astype(jnp.float32)
    bit_count = section_count.bit_length() - 1
    mirrored = grad_share
    for which_bit in range(bit_count):
        mirrored = from_partner(mirrored.astype(jnp.bfloat16), "pipe", which_bit).astype(
            mirrored.dtype
        )
    total = grad_share + mirrored[::-1]
    tokens_slot = first_inputs.shape[-1]
    momentum_next = beta_coef * momentum[0] + total / (2 * tokens_slot)
    quarter = grad_share.shape[2]
    weight_share = lax.dynamic_slice_in_dim(
        section_weights, lax.axis_index("dp") * quarter, quarter, axis=2
    )
    weights_next = (weight_share.astype(jnp.float32) - step_size * momentum_next).astype(
        jnp.bfloat16
    )
    forward_out = jnp.stack(outputs_second)[None, None]
    backward_out = jnp.stack(backs_second)[None, None]
    return (forward_out, backward_out, weights_next[None], momentum_next[None])


def solution(mesh):
    placed = (
        P("dp", "pipe", None, None, None),
        P("dp", "pipe", None, None, None),
        P("dp", "pipe", None, None, None, None),
        P("dp", None, None, None),
        P(),
        P("pipe", None, None, None, None),
        P("pipe", None, None, "dp", None),
    )
    return jax.shard_map(
        shards,
        mesh=mesh,
        in_specs=placed,
        out_specs=(
            P("dp", "pipe", None, None, None),
            P("dp", "pipe", None, None, None),
            P("pipe", None, None, "dp", None),
            P("pipe", None, None, "dp", None),
        ),
        check_vma=False,
    )
```

profile of v0, /device:TPU:1, one launch (start us, length us, event | category | flops | bytes accessed | tf_op | source)
XLA Modules:
  0.0 481.6 jit_solution(16412283592790329007)
XLA Ops:
  16.5 2.7 reshape_squeeze.22
  34.4 2.4 reshape_squeeze.24
  40.5 2.7 copy.77
  43.2 2.9 reshape_squeeze.25
  55.2 2.7 copy.79
  66.5 7.3 %collective-permute-start.3 = (bf16[1536,32]{0,1:T(8,128)(2,1)}, bf16[1536,32]{0,1:T(8,128)(2,1)}, u32[]{:S(2)}, u32[]{:S(2)}) collective-permute-start(bf16[1536,32]{0,1:T(8,128)(2,1)} %get-tuple-element.49), channel_id=1, source_target_pairs={{0,1},{1,2},{2,3},{3,4},{4,5},{5,6},{6,7},{7,8},{8,9},{9,10},{10,1... | collective-permute-start | bytes 294920 | tf_op jit(solution)/shard_map/ppermute | solution.py:17
  73.8 2.8 convolution_convert_fusion.13
  86.4 2.6 copy.47
  92.3 3.3 convolution_convert_fusion.23
  95.6 2.6 copy.49
  105.5 2.6 copy.55
  111.4 3.5 convolution_convert_fusion.21
  114.9 2.6 copy.57
  117.5 2.9 convolution_bitcast_fusion.14
  124.3 2.6 copy.81
  128.4 3.3 convert_reduce_fusion.1
  135.6 2.7 copy.69
  139.7 3.4 convert_reduce_fusion.5
  143.1 2.4 constant_dynamic-slice_fusion
  145.4 2.7 copy.99
  148.1 3.2 fusion.371
  155.8 2.9 copy.91
  158.7 3.2 fusion.367
  171.5 3.0 stack.65
  174.5 3.0 stack.64
  177.5 2.7 copy.103
  180.2 3.0 stack.59
  183.2 3.4 stack.58
  186.5 2.7 copy.95
  197.0 2.6 copy.83
  199.7 2.3 convolution_bitcast_fusion.1
  204.9 2.7 copy.85
  207.6 2.9 convolution_bitcast_fusion
  216.3 2.6 copy.71
  223.8 2.6 copy.73
  226.4 2.9 convolution_bitcast_fusion.6
  231.3 5.8 %collective-permute-start = (bf16[1536,32]{0,1:T(8,128)(2,1)}, bf16[1536,32]{0,1:T(8,128)(2,1)}, u32[]{:S(2)}, u32[]{:S(2)}) collective-permute-start(bf16[1536,32]{0,1:T(8,128)(2,1)} %get-tuple-element.31), channel_id=1, source_target_pairs={{0,1},{1,2},{2,3},{3,4},{4,5},{5,6},{6,7},{7,8},{8,9},{9,10},{10,1... | collective-permute-start | bytes 294920 | tf_op jit(solution)/shard_map/ppermute | solution.py:17
  242.1 3.1 fusion.15
  247.1 3.1 fusion.373
  250.2 3.1 stack.68
  253.4 3.0 stack.67
  256.3 3.3 fusion.369
  259.6 3.0 stack.62
  262.7 3.0 stack.61
  265.6 2.7 fusion.1
  269.9 3.9 copy.105
  282.0 2.6 copy.59
  287.9 3.3 convert_reduce_fusion.9
  291.2 55.9 %all-reduce.3.cloned.1.call-done = bf16[2,2,72,4096]{3,1,0,2:T(2,128)(2,1)} async-done(((bf16[2,2,72,4096]{3,1,0,2:T(2,128)(2,1)}), bf16[2,2,72,4096]{3,1,0,2:T(2,128)(2,1)}) %all-reduce.3.cloned.1.call-update) | async-done | bytes 2359312
  349.3 2.7 collective-permute-start.4
  352.1 3.3 convolution_convert_fusion.20
  355.4 10.4 %collective-permute-done.4 = bf16[2,2,18,4096]{3,1,2,0:T(2,128)(2,1)} collective-permute-done((bf16[2,2,18,4096]{3,1,2,0:T(2,128)(2,1)S(1)}, bf16[2,2,18,4096]{3,1,2,0:T(2,128)(2,1)}, u32[]{:S(2)}, u32[]{:S(2)}) %collective-permute-start.4) | collective-permute-done | bytes 589856 | tf_op jit(solution)/shard_map/ppermute | solution.py:23
  367.4 2.6 copy.61
  373.2 6.6 %collective-permute-done.5 = bf16[2,2,18,4096]{3,1,2,0:T(2,128)(2,1)} collective-permute-done((bf16[2,2,18,4096]{3,1,2,0:T(2,128)(2,1)}, bf16[2,2,18,4096]{3,1,2,0:T(2,128)(2,1)}, u32[]{:S(2)}, u32[]{:S(2)}) %collective-permute-start.5) | collective-permute-done | bytes 589856 | tf_op jit(solution)/shard_map/ppermute | solution.py:23
  379.8 2.7 collective-permute-start.6
  382.5 3.3 convolution_convert_fusion.22
  385.8 8.5 %collective-permute-done.6 = bf16[2,2,18,4096]{3,1,2,0:T(2,128)(2,1)} collective-permute-done((bf16[2,2,18,4096]{3,1,2,0:T(2,128)(2,1)}, bf16[2,2,18,4096]{3,1,2,0:T(2,128)(2,1)}, u32[]{:S(2)}, u32[]{:S(2)}) %collective-permute-start.6) | collective-permute-done | bytes 589856 | tf_op jit(solution)/shard_map/ppermute | solution.py:23
  396.1 2.6 copy.53
  401.1 5.4 %collective-permute-done.7 = bf16[2,2,18,4096]{3,1,2,0:T(2,128)(2,1)} collective-permute-done((bf16[2,2,18,4096]{3,1,2,0:T(2,128)(2,1)}, bf16[2,2,18,4096]{3,1,2,0:T(2,128)(2,1)}, u32[]{:S(2)}, u32[]{:S(2)}) %collective-permute-start.7) | collective-permute-done | bytes 589856 | tf_op jit(solution)/shard_map/ppermute | solution.py:23
  406.5 2.5 collective-permute-start.8
  410.5 23.9 %collective-permute-done.8 = bf16[2,2,18,4096]{3,1,2,0:T(2,128)(2,1)} collective-permute-done((bf16[2,2,18,4096]{3,1,2,0:T(2,128)(2,1)}, bf16[2,2,18,4096]{3,1,2,0:T(2,128)(2,1)}, u32[]{:S(2)}, u32[]{:S(2)}) %collective-permute-start.8) | collective-permute-done | bytes 589856 | tf_op jit(solution)/shard_map/ppermute | solution.py:23
  434.4 6.8 %collective-permute-start.9 = (bf16[2,2,18,4096]{3,1,2,0:T(2,128)(2,1)}, bf16[2,2,18,4096]{3,1,2,0:T(2,128)(2,1)S(1)}, u32[]{:S(2)}, u32[]{:S(2)}) collective-permute-start(bf16[2,2,18,4096]{3,1,2,0:T(2,128)(2,1)} %collective-permute-done.8), channel_id=1, source_target_pairs={{0,32},{1,33},{2,34},{3,35},{4,36},{5,37},{6,38},{7,39},{8,40},{9,... | collective-permute-start | bytes 1769480 | tf_op jit(solution)/shard_map/ppermute | solution.py:23
  442.0 25.2 %collective-permute-done.9 = bf16[2,2,18,4096]{3,1,2,0:T(2,128)(2,1)S(1)} collective-permute-done((bf16[2,2,18,4096]{3,1,2,0:T(2,128)(2,1)}, bf16[2,2,18,4096]{3,1,2,0:T(2,128)(2,1)S(1)}, u32[]{:S(2)}, u32[]{:S(2)}) %collective-permute-start.9) | collective-permute-done | bytes 589856 | tf_op jit(solution)/shard_map/ppermute | solution.py:23
  467.7 4.3 fusion.111
  (268 shorter events, 152.1 us)
Async XLA Ops:
  7.2 339.9 %all-reduce.3.cloned.1.call-start = ((), (), s32[]{:S(2)}) async-start(), calls=%async_computation | async-start | bytes 4718592
  7.2 4.6 copy-start.20
  11.8 7.4 %copy-start.6 = (bf16[72,64,32]{1,2,0:T(8,128)(2,1)}, bf16[72,64,32]{1,2,0:T(8,128)(2,1)S(1)}, u32[]{:S(2)}) copy-start(bf16[72,64,32]{1,2,0:T(8,128)(2,1)S(1)} %copy.63) | copy-start | bytes 884740
  16.5 5.1 %copy-start.2 = (bf16[72,64,32]{1,2,0:T(8,128)(2,1)}, bf16[72,64,32]{1,2,0:T(8,128)(2,1)S(1)}, u32[]{:S(2)}) copy-start(bf16[72,64,32]{1,2,0:T(8,128)(2,1)S(1)} %copy.65) | copy-start | bytes 884740
  21.7 3.0 copy-start.25
  22.4 2.2 copy-start.61
  30.2 2.0 copy-start.45
  49.4 3.0 copy-start.33
  50.1 2.2 copy-start.67
  65.2 126.0 %collective-permute-start.2 = (bf16[1536,32]{0,1:T(8,128)(2,1)}, bf16[1536,32]{0,1:T(8,128)(2,1)}, u32[]{:S(2)}, u32[]{:S(2)}) collective-permute-start(bf16[1536,32]{0,1:T(8,128)(2,1)} %get-tuple-element.48), channel_id=1, source_target_pairs={{1,0},{2,1},{3,2},{4,3},{5,4},{6,5},{7,6},{8,7},{9,8},{10,9},{11,1... | collective-permute-start | bytes 294920 | tf_op jit(solution)/shard_map/ppermute | solution.py:17
  66.5 124.7 %collective-permute-start.3 = (bf16[1536,32]{0,1:T(8,128)(2,1)}, bf16[1536,32]{0,1:T(8,128)(2,1)}, u32[]{:S(2)}, u32[]{:S(2)}) collective-permute-start(bf16[1536,32]{0,1:T(8,128)(2,1)} %get-tuple-element.49), channel_id=1, source_target_pairs={{0,1},{1,2},{2,3},{3,4},{4,5},{5,6},{6,7},{7,8},{8,9},{9,10},{10,1... | collective-permute-start | bytes 294920 | tf_op jit(solution)/shard_map/ppermute | solution.py:17
  73.8 2.8 copy-start.10
  73.8 2.8 copy-start.11
  76.7 2.0 copy-start.26
  76.7 2.0 copy-start.28
  76.7 2.0 copy-start.62
  79.9 2.0 copy-start.44
  148.1 3.3 copy-start.23
  148.1 3.3 copy-start.47
  148.1 3.3 copy-start.48
  151.4 3.2 copy-start.69
  158.7 3.3 copy-start.21
  158.7 3.3 copy-start.49
  158.7 3.3 copy-start.50
  161.9 2.2 copy-start.64
  164.2 1.8 copy-start.18
  199.7 2.3 copy-start.24
  199.7 2.3 copy-start.32
  199.7 2.3 copy-start.70
  207.6 2.9 copy-start.5
  207.6 2.9 copy-start.12
  218.9 1.9 copy-start.22
  218.9 1.9 copy-start.30
  218.9 1.9 copy-start.65
  226.4 2.9 copy-start.4
  226.4 2.9 copy-start.13
  229.4 9.0 %copy-start.19 = (f32[72,64,32]{1,2,0:T(8,128)S(1)}, f32[72,64,32]{1,2,0:T(8,128)}, u32[]{:S(2)}) copy-start(f32[72,64,32]{1,2,0:T(8,128)} %convolution_bitcast_fusion) | copy-start | bytes 1769476
  231.3 45.3 %collective-permute-start = (bf16[1536,32]{0,1:T(8,128)(2,1)}, bf16[1536,32]{0,1:T(8,128)(2,1)}, u32[]{:S(2)}, u32[]{:S(2)}) collective-permute-start(bf16[1536,32]{0,1:T(8,128)(2,1)} %get-tuple-element.31), channel_id=1, source_target_pairs={{0,1},{1,2},{2,3},{3,4},{4,5},{5,6},{6,7},{7,8},{8,9},{9,10},{10,1... | collective-permute-start | bytes 294920 | tf_op jit(solution)/shard_map/ppermute | solution.py:17
  237.1 39.5 %collective-permute-start.1 = (bf16[1536,32]{0,1:T(8,128)(2,1)}, bf16[1536,32]{0,1:T(8,128)(2,1)}, u32[]{:S(2)}, u32[]{:S(2)}) collective-permute-start(bf16[1536,32]{0,1:T(8,128)(2,1)} %get-tuple-element.45), channel_id=1, source_target_pairs={{1,0},{2,1},{3,2},{4,3},{5,4},{6,5},{7,6},{8,7},{9,8},{10,9},{11,1... | collective-permute-start | bytes 294920 | tf_op jit(solution)/shard_map/ppermute | solution.py:17
  265.6 2.8 copy-start.14
  265.6 3.0 copy-start.15
  265.6 3.4 copy-start.16
  265.6 3.7 copy-start.17
  273.8 2.8 copy-start.46
  291.2 60.9 %copy-start.71 = (s32[72]{0:T(128)S(1)}, s32[72]{0:T(128)}, u32[]{:S(2)}) copy-start(s32[72]{0:T(128)} %get-tuple-element.58) | copy-start | bytes 868
  347.1 5.0 %copy-start.72 = (f32[96,64,32]{0,1,2:T(8,128)S(1)}, f32[96,64,32]{0,1,2:T(8,128)}, u32[]{:S(2)}) copy-start(f32[96,64,32]{0,1,2:T(8,128)} %get-tuple-element.66) | copy-start | bytes 2359300
  347.1 5.0 %copy-start.73 = (u32[96,64]{0,1:T(8,128)S(1)}, u32[96,64]{0,1:T(8,128)}, u32[]{:S(2)}) copy-start(u32[96,64]{0,1:T(8,128)} %get-tuple-element.24) | copy-start | bytes 73732
  347.1 5.0 %copy-start.74 = (u32[96,64]{0,1:T(8,128)S(1)}, u32[96,64]{0,1:T(8,128)}, u32[]{:S(2)}) copy-start(u32[96,64]{0,1:T(8,128)} %get-tuple-element.25) | copy-start | bytes 73732
  349.3 16.5 %collective-permute-start.4 = (bf16[2,2,18,4096]{3,1,2,0:T(2,128)(2,1)S(1)}, bf16[2,2,18,4096]{3,1,2,0:T(2,128)(2,1)}, u32[]{:S(2)}, u32[]{:S(2)}) collective-permute-start(bf16[2,2,18,4096]{3,1,2,0:T(2,128)(2,1)S(1)} %copy.106), channel_id=1, source_target_pairs={{0,1},{1,0},{2,3},{3,2},{4,5},{5,4},{6,7},{7,6},{8,9},{9,8},{10,11... | collective-permute-start | bytes 1769480 | tf_op jit(solution)/shard_map/ppermute | solution.py:23
  352.1 14.9 %copy-start.43 = (bf16[24,64,32]{1,0,2:T(8,128)(2,1)S(1)}, bf16[24,64,32]{1,0,2:T(8,128)(2,1)}, u32[]{:S(2)}) copy-start(bf16[24,64,32]{1,0,2:T(8,128)(2,1)} %reshape.346) | copy-start | bytes 294916
  365.8 14.0 %collective-permute-start.5 = (bf16[2,2,18,4096]{3,1,2,0:T(2,128)(2,1)}, bf16[2,2,18,4096]{3,1,2,0:T(2,128)(2,1)}, u32[]{:S(2)}, u32[]{:S(2)}) collective-permute-start(bf16[2,2,18,4096]{3,1,2,0:T(2,128)(2,1)} %collective-permute-done.4), channel_id=1, source_target_pairs={{0,2},{1,3},{2,0},{3,1},{4,6},{5,7},{6,4},{7,5},{8,10},{9,11},{10,... | collective-permute-start | bytes 1769480 | tf_op jit(solution)/shard_map/ppermute | solution.py:23
  371.5 11.0 %copy-start.66 = (s32[72]{0:T(128)S(1)}, s32[72]{0:T(128)}, u32[]{:S(2)}) copy-start(s32[72]{0:T(128)} %get-tuple-element.73) | copy-start | bytes 868
  379.8 14.6 %collective-permute-start.6 = (bf16[2,2,18,4096]{3,1,2,0:T(2,128)(2,1)}, bf16[2,2,18,4096]{3,1,2,0:T(2,128)(2,1)}, u32[]{:S(2)}, u32[]{:S(2)}) collective-permute-start(bf16[2,2,18,4096]{3,1,2,0:T(2,128)(2,1)} %collective-permute-done.5), channel_id=1, source_target_pairs={{0,4},{1,5},{2,6},{3,7},{4,0},{5,1},{6,2},{7,3},{8,12},{9,13},{10,... | collective-permute-start | bytes 1769480 | tf_op jit(solution)/shard_map/ppermute | solution.py:23
  382.5 13.1 %copy-start.1 = (bf16[72,64,64]{2,1,0:T(8,128)(2,1)S(1)}, bf16[72,64,64]{2,1,0:T(8,128)(2,1)}, u32[]{:S(2)}) copy-start(bf16[72,64,64]{2,1,0:T(8,128)(2,1)} %reshape_squeeze.25) | copy-start | bytes 1769476
  382.5 13.1 %copy-start.36 = (bf16[72,64,32]{1,2,0:T(8,128)(2,1)S(1)}, bf16[72,64,32]{1,2,0:T(8,128)(2,1)}, u32[]{:S(2)}) copy-start(bf16[72,64,32]{1,2,0:T(8,128)(2,1)} %copy.61) | copy-start | bytes 884740
  394.4 12.1 %collective-permute-start.7 = (bf16[2,2,18,4096]{3,1,2,0:T(2,128)(2,1)}, bf16[2,2,18,4096]{3,1,2,0:T(2,128)(2,1)}, u32[]{:S(2)}, u32[]{:S(2)}) collective-permute-start(bf16[2,2,18,4096]{3,1,2,0:T(2,128)(2,1)} %collective-permute-done.6), channel_id=1, source_target_pairs={{0,8},{1,9},{2,10},{3,11},{4,12},{5,13},{6,14},{7,15},{8,0},{9,1},... | collective-permute-start | bytes 1769480 | tf_op jit(solution)/shard_map/ppermute | solution.py:23
  398.7 1.9 copy-start.37
  401.1 9.1 %copy-start.38 = (f32[24,64,32]{1,0,2:T(8,128)S(1)}, f32[24,64,32]{1,0,2:T(8,128)}, u32[]{:S(2)}) copy-start(f32[24,64,32]{1,0,2:T(8,128)} %fusion.27) | copy-start | bytes 589828
  401.1 9.4 %copy-start.41 = (bf16[1536,32]{0,1:T(8,128)(2,1)S(1)}, bf16[1536,32]{0,1:T(8,128)(2,1)}, u32[]{:S(2)}) copy-start(bf16[1536,32]{0,1:T(8,128)(2,1)} %get-tuple-element.43) | copy-start | bytes 294916
  406.5 27.9 %collective-permute-start.8 = (bf16[2,2,18,4096]{3,1,2,0:T(2,128)(2,1)}, bf16[2,2,18,4096]{3,1,2,0:T(2,128)(2,1)}, u32[]{:S(2)}, u32[]{:S(2)}) collective-permute-start(bf16[2,2,18,4096]{3,1,2,0:T(2,128)(2,1)} %collective-permute-done.7), channel_id=1, source_target_pairs={{0,16},{1,17},{2,18},{3,19},{4,20},{5,21},{6,22},{7,23},{8,24},{9,... | collective-permute-start | bytes 1769480 | tf_op jit(solution)/shard_map/ppermute | solution.py:23
  410.2 31.0 %copy-start.40 = (bf16[1536,32]{0,1:T(8,128)(2,1)S(1)}, bf16[1536,32]{0,1:T(8,128)(2,1)}, u32[]{:S(2)}) copy-start(bf16[1536,32]{0,1:T(8,128)(2,1)} %get-tuple-element.42) | copy-start | bytes 294916
  434.4 32.8 %collective-permute-start.9 = (bf16[2,2,18,4096]{3,1,2,0:T(2,128)(2,1)}, bf16[2,2,18,4096]{3,1,2,0:T(2,128)(2,1)S(1)}, u32[]{:S(2)}, u32[]{:S(2)}) collective-permute-start(bf16[2,2,18,4096]{3,1,2,0:T(2,128)(2,1)} %collective-permute-done.8), channel_id=1, source_target_pairs={{0,32},{1,33},{2,34},{3,35},{4,36},{5,37},{6,38},{7,39},{8,40},{9,... | collective-permute-start | bytes 1769480 | tf_op jit(solution)/shard_map/ppermute | solution.py:23
  441.2 26.4 %copy-start.35 = (bf16[1,2,2,18,4096]{4,3,2,1,0:T(8,128)(2,1)S(1)}, bf16[1,2,2,18,4096]{4,3,2,1,0:T(8,128)(2,1)}, u32[]{:S(2)}) copy-start(bf16[1,2,2,18,4096]{4,3,2,1,0:T(8,128)(2,1)} %constant_dynamic-slice_fusion) | copy-start | bytes 1769476
  441.3 26.4 %copy-start.39 = (f32[1,2,2,18,4096]{4,2,3,1,0:T(2,128)S(1)}, f32[1,2,2,18,4096]{4,2,3,1,0:T(2,128)}, u32[]{:S(2)}) copy-start(f32[1,2,2,18,4096]{4,2,3,1,0:T(2,128)} %param.13) | copy-start | bytes 3538948
  (22 other events, 31.0 us)
Sparse Core Ops, SparseCore 0:
  273.9 73.1 all-reduce.2
where the time goes:
time: 488 us; the launch traced here: 482 us
  local copies, waits for them, and re-layouts  138 us (28%)
  waiting for transfers between devices  136 us (28%)
  matrix products  133 us (27%)
  starting transfers between devices  32.9 us (7%)
  other arithmetic  26.3 us (5%)
  between operations  15.9 us (3%)
    ppermute x6, waiting for transfers between devices, from_partner(): return lax.ppermute(value, axis, pairs)  80.1 us
    convert_element_type x24, local copies, waits for them, and re-layouts, pick_blocks(): return jnp.einsum('nb,bir->nir', table.astype(jnp.bfloat16), source, pref...  56.7 us
    unnamed x2, waiting for transfers between devices  55.9 us
    dot_general x28, matrix products, block_product(): return jnp.einsum(spec, left, right, preferred_element_type=jnp.float32)  49.7 us
    dot_general x24, matrix products, pick_blocks(): jnp.einsum('nb,bir->nir', table.astype(jnp.bfloat16), source, preferred_e...  42.4 us
    dot_general x20, matrix products, add_blocks(): jnp.einsum('nb,njr->bjr', table.astype(jnp.float32), terms, precision=lax...  40.5 us
    another operation x8, local copies, waits for them, and re-layouts, section_backward(): return (grad_in, jnp.stack([grad_up, grad_down]))  24.4 us
    ppermute x6, starting transfers between devices, from_partner(): return lax.ppermute(value, axis, pairs)  17.2 us
  transfers between devices with their start and end apart: 11, of which 7 were waited for; matrix products, arithmetic and copies ran while one was open for 39% of the time, Pallas kernels for 0%

commit v1 on v0

v1 whole, which is shorter than its diff:
```python
import jax
import jax.numpy as jnp
from jax import lax
from jax.experimental import pallas as pl
from jax.experimental.pallas import tpu as pltpu
from jax.sharding import PartitionSpec as P

FF = 6144
BLOCK = 64
BETA = 0.9
STEP = 0.2
UNROLL = 8
VMEM_BYTES = 56 * 2**20


def dot(left, right, dims):
    return lax.dot_general(left, right, (dims, ((), ())), preferred_element_type=jnp.float32)


def mul(left, right):
    return dot(left, right, ((1,), (0,)))


def mul_nt(left, right):
    return dot(left, right, ((1,), (1,)))


def gelu_parts(values):
    cdf = 0.5 + 0.5 * lax.erf(values * 0.7071067811865476)
    slope = cdf + values * (0.3989422804014327 * jnp.exp(-0.5 * values * values))
    return values * cdf, slope


def lanes(parts):
    zero = jnp.zeros((BLOCK, 32), jnp.bfloat16)
    return jnp.concatenate([zero if part is None else part for part in parts], axis=1)


def place(pat, copy, proj, n, blocks_d, blocks_f):
    value = pat[(copy * 2 + proj) * 72 + n]
    if proj == 0:
        r = value // blocks_f
        return r, value - r * blocks_f
    r = value // blocks_d
    return value - r * blocks_d, r


def each_block(count, body):
    def step(i, carry):
        body([i * UNROLL + u for u in range(UNROLL)])
        return carry

    lax.fori_loop(0, count // UNROLL, step, 0)


def section_pass(pat, w, wt, x, gy, pre, gh, out, copy):
    blocks_d, blocks_f, count = x.shape[1], pre.shape[0], w.shape[2]

    def up(ns):
        terms = []
        for n in ns:
            d, f = place(pat, copy, 0, n, blocks_d, blocks_f)
            terms.append((f, mul(wt[copy, 0, n], x[copy, d])))
        for f, term in terms:
            pre[f] += term

    def down(ns):
        terms = []
        for n in ns:
            d, f = place(pat, copy, 1, n, blocks_d, blocks_f)
            terms.append((f, mul(w[copy, 1, n], gy[copy, d])))
        for f, term in terms:
            gh[f] += term

    each_block(count, up)
    each_block(count, down)


def section_close(pat, w, wt, hid, gp, out, copy, fwd_lanes):
    blocks_d, blocks_f, count = out.shape[0], hid.shape[0], w.shape[2]
    lane = lax.broadcasted_iota(jnp.int32, (BLOCK, 128), 1) // 32
    fwd = (lane == fwd_lanes + copy).astype(jnp.float32).astype(jnp.bfloat16)
    own = (lane % 2 == copy).astype(jnp.float32).astype(jnp.bfloat16)

    def down(ns):
        terms = []
        for n in ns:
            d, f = place(pat, copy, 1, n, blocks_d, blocks_f)
            terms.append((d, mul(wt[copy, 1, n], hid[f] * fwd)))
        for d, term in terms:
            out[d] += term

    def up(ns):
        terms = []
        for n in ns:
            d, f = place(pat, copy, 0, n, blocks_d, blocks_f)
            terms.append((d, mul(w[copy, 0, n], gp[f] * own)))
        for d, term in terms:
            out[d] += term

    each_block(count, down)
    each_block(count, up)


def clear(ref):
    def step(i, carry):
        ref[i] = jnp.zeros(ref.shape[1:], ref.dtype)
        return carry

    lax.fori_loop(0, ref.shape[0], step, 0)


def first_kernel(pat, acts, cot, stash, w, wt, y_out, send_up, send_down, hid, gp, x, gy, pre, gh, out):
    blocks_d, blocks_f = out.shape[0], pre.shape[0]
    clear(pre)
    clear(gh)

    def load(r, carry):
        rows = pl.ds(r * BLOCK, BLOCK)
        a0, a1, c0, c1 = acts[0, rows], acts[1, rows], cot[0, rows], cot[1, rows]
        x[0, r] = lanes([a0, None, stash[0, 0, rows], None])
        x[1, r] = lanes([None, a1, None, stash[1, 0, rows]])
        gy[0, r] = lanes([None, None, c0, None])
        gy[1, r] = lanes([None, None, None, c1])
        out[r] = lanes([a0, a1, c0, c1]).astype(jnp.float32)
        return carry

    lax.fori_loop(0, blocks_d, load, 0)
    for copy in range(2):
        section_pass(pat, w, wt, x, gy, pre, gh, out, copy)

    def act(f, carry):
        hidden, slope = gelu_parts(pre[f])
        hid[f] = hidden.astype(jnp.bfloat16)
        gp[f] = (slope * gh[f]).astype(jnp.bfloat16)
        return carry

    lax.fori_loop(0, blocks_f, act, 0)
    for copy in range(2):
        section_close(pat, w, wt, hid, gp, out, copy, 0)

    half = blocks_d // 2

    def store(r, carry):
        rows = pl.ds(r * BLOCK, BLOCK)
        lo, hi = out[r].astype(jnp.bfloat16), out[r + half].astype(jnp.bfloat16)
        send_up[rows, :] = jnp.concatenate([lo[:, 0:32], lo[:, 96:128], hi[:, 0:32], hi[:, 96:128]], axis=1)
        send_down[rows, :] = jnp.concatenate([lo[:, 32:96], hi[:, 32:96]], axis=1)
        return carry

    lax.fori_loop(0, half, store, 0)

    def keep(r, carry):
        rows = pl.ds(r * BLOCK, BLOCK)
        value = out[r].astype(jnp.bfloat16)
        y_out[0, rows, :] = value[:, 0:32]
        y_out[1, rows, :] = value[:, 32:64]
        return carry

    lax.fori_loop(0, blocks_d, keep, 0)


def second_kernel(
    sections, pat, acts, cot, stash, entering, y_first, got_up, got_down, hid1, gp1, w, wt,
    forward, backward, grads, x, gy, xs, gys, hid, gp, pre, gh, out,
):
    blocks_d, blocks_f, count = out.shape[0], pre.shape[0], w.shape[2]
    me = lax.axis_index("pipe")
    at_entry, at_exit = me == 0, me == sections - 1
    clear(pre)
    clear(gh)
    half = blocks_d // 2
    row = lax.broadcasted_iota(jnp.int32, (BLOCK, BLOCK), 0)
    col = lax.broadcasted_iota(jnp.int32, (BLOCK, BLOCK), 1)
    source = jnp.where(row < BLOCK // 2, 2 * row, 2 * row - BLOCK + 1)
    evens_first = (col == source).astype(jnp.float32).astype(jnp.bfloat16)

    def rearranged(value):
        return mul(evens_first, value).astype(jnp.bfloat16)

    def load(r, part):
        rows = pl.ds(r * BLOCK, BLOCK)
        sent = pl.ds((r - part * half) * BLOCK, BLOCK)
        up, down = got_up[sent, :], got_down[sent, :]
        base = part * 64
        y0, d1 = up[:, base : base + 32], up[:, base + 32 : base + 64]
        y1, d0 = down[:, base : base + 32], down[:, base + 32 : base + 64]
        x0 = jnp.where(at_entry, entering[0, rows], y0)
        x1 = jnp.where(at_exit, entering[1, rows], y1)
        g0 = jnp.where(at_exit, y_first[0, rows], d0)
        g1 = jnp.where(at_entry, y_first[1, rows], d1)
        s0 = jnp.where(at_exit, acts[0, rows], stash[0, 1, rows])
        s1 = jnp.where(at_entry, acts[1, rows], stash[1, 1, rows])
        x[0, r] = lanes([s0, None, x0, None])
        x[1, r] = lanes([None, s1, None, x1])
        gy[0, r] = lanes([g0, None, None, None])
        gy[1, r] = lanes([None, g1, None, None])
        gys[0, r] = lanes([g0, None, cot[0, rows], None])
        gys[1, r] = lanes([None, g1, None, cot[1, rows]])
        xs[0, r] = rearranged(lanes([s0, None, stash[0, 0, rows], None]))
        xs[1, r] = rearranged(lanes([None, s1, None, stash[1, 0, rows]]))
        out[r] = lanes([g0, g1, x0, x1]).astype(jnp.float32)

    for part in range(2):
        lax.fori_loop(part * half, (part + 1) * half, lambda r, carry: (load(r, part), carry)[1], 0)
    for copy in range(2):
        section_pass(pat, w, wt, x, gy, pre, gh, out, copy)

    early = lax.broadcasted_iota(jnp.int32, (BLOCK, 128), 1) >= 64

    def act(f, carry):
        hidden, slope = gelu_parts(pre[f])
        hid[f] = hidden.astype(jnp.bfloat16)
        gp[f] = (slope * gh[f]).astype(jnp.bfloat16)
        return carry

    lax.fori_loop(0, blocks_f, act, 0)
    for copy in range(2):
        section_close(pat, w, wt, hid, gp, out, copy, 2)

    def store(r, carry):
        rows = pl.ds(r * BLOCK, BLOCK)
        value = out[r].astype(jnp.bfloat16)
        for copy in range(2):
            backward[copy, rows, :] = value[:, 32 * copy : 32 * copy + 32]
            forward[copy, rows, :] = value[:, 64 + 32 * copy : 96 + 32 * copy]
        return carry

    lax.fori_loop(0, blocks_d, store, 0)

    def join(f, carry):
        gp[f] = jnp.where(early, gp1[f].astype(jnp.float32), gp[f].astype(jnp.float32)).astype(jnp.bfloat16)
        both = jnp.where(early, hid1[f].astype(jnp.float32), hid[f].astype(jnp.float32)).astype(jnp.bfloat16)
        hid[f] = rearranged(both)
        return carry

    lax.fori_loop(0, blocks_f, join, 0)

    def two_wide(value):
        return jnp.concatenate([value[: BLOCK // 2], value[BLOCK // 2 :]], axis=1).astype(jnp.bfloat16)

    for copy in range(2):

        def outer(ns, copy=copy):
            for n in ns:
                d, f = place(pat, copy, 0, n, blocks_d, blocks_f)
                grads[copy, 0, n] = two_wide(mul_nt(xs[copy, d], gp[f]))
            for n in ns:
                d, f = place(pat, copy, 1, n, blocks_d, blocks_f)
                grads[copy, 1, n] = two_wide(mul_nt(hid[f], gys[copy, d]))

        each_block(count, outer)


def call(kernel, args, outs, scratch):
    smem, vmem = pl.BlockSpec(memory_space=pltpu.SMEM), pl.BlockSpec(memory_space=pltpu.VMEM)
    return pl.pallas_call(
        kernel,
        out_shape=[jax.ShapeDtypeStruct(*out) for out in outs],
        in_specs=[smem] + [vmem] * (len(args) - 1),
        out_specs=[vmem] * len(outs),
        scratch_shapes=[pltpu.VMEM(*one) for one in scratch],
        compiler_params=pltpu.CompilerParams(vmem_limit_bytes=VMEM_BYTES),
    )(*args)


def shards(acts_in, cot_in, stash, entering, pattern, weights, momentum):
    bf16, f32 = jnp.bfloat16, jnp.float32
    me, sections = lax.axis_index("pipe"), lax.axis_size("pipe")
    group = lax.axis_index("dp")
    acts, cot, saved, fresh = acts_in[0, 0], cot_in[0, 0], stash[0, 0], entering[0]
    pat = jnp.stack(
        [
            lax.dynamic_index_in_dim(pattern, me, 0, keepdims=False),
            lax.dynamic_index_in_dim(pattern, sections - 1 - me, 0, keepdims=False),
        ]
    ).reshape(-1)
    width, tokens = acts.shape[1:]
    count = weights.shape[3]
    blocks_d, blocks_f = width // BLOCK, FF // BLOCK
    w = weights[0].reshape(2, 2, count, BLOCK, BLOCK)
    wt = jnp.swapaxes(w, 3, 4)
    d_block, f_block = (blocks_d, BLOCK, 128), (blocks_f, BLOCK, 128)
    y_first, send_up, send_down, hid, gp = call(
        first_kernel,
        (pat, acts, cot, saved, w, wt),
        [
            (acts.shape, bf16),
            ((width // 2, 128), bf16),
            ((width // 2, 128), bf16),
            (f_block, bf16),
            (f_block, bf16),
        ],
        [((2, *d_block), bf16), ((2, *d_block), bf16), (f_block, f32), (f_block, f32), (d_block, f32)],
    )
    got_up = lax.ppermute(send_up, "pipe", [(i, i + 1) for i in range(sections - 1)])
    got_down = lax.ppermute(send_down, "pipe", [(i + 1, i) for i in range(sections - 1)])
    forward, backward, grads = call(
        lambda *refs: second_kernel(sections, *refs),
        (pat, acts, cot, saved, fresh, y_first, got_up, got_down, hid, gp, w, wt),
        [(acts.shape, bf16), (acts.shape, bf16), ((2, 2, count, BLOCK // 2, 128), bf16)],
        [((2, *d_block), bf16)] * 4 + [(f_block, bf16)] * 2 + [(f_block, f32)] * 2 + [(d_block, f32)],
    )
    quarter = count // 4
    core, side = group % 2, group // 2
    grads = grads.reshape(2, 2, 2, 2, quarter, BLOCK // 2, 128)
    given = lax.dynamic_index_in_dim(grads, 1 - core, 3, keepdims=False)
    kept = lax.dynamic_index_in_dim(grads, core, 3, keepdims=False)
    got = lax.ppermute(given, "dp", [(i, i ^ 1) for i in range(4)])
    summed = (kept.astype(f32) + got.astype(f32)).astype(bf16)
    given = lax.dynamic_index_in_dim(summed, 1 - side, 2, keepdims=False)
    kept = lax.dynamic_index_in_dim(summed, side, 2, keepdims=False)
    got = lax.ppermute(given, "dp", [(i, i ^ 2) for i in range(4)])
    share = (kept.astype(f32) + got.astype(f32)).astype(bf16)
    mirrored = lax.ppermute(share, "pipe", [(i, sections - 1 - i) for i in range(sections)])
    total = share.astype(f32) + mirrored[::-1].astype(f32)
    total = total.reshape(2, 2, quarter, -1)
    momentum_next = BETA * momentum[0] + total / (2 * tokens)
    own = lax.dynamic_slice_in_dim(weights[0], group * quarter, quarter, axis=2)
    weights_next = (own.astype(f32) - STEP * momentum_next).astype(bf16)
    return forward[None, None], backward[None, None], weights_next[None], momentum_next[None]


def solution(mesh):
    placed = (
        P("dp", "pipe"),
        P("dp", "pipe"),
        P("dp", "pipe"),
        P("dp"),
        P(),
        P("pipe"),
        P("pipe", None, None, "dp"),
    )
    return jax.shard_map(
        shards,
        mesh=mesh,
        in_specs=placed,
        out_specs=(P("dp", "pipe"), P("dp", "pipe"), P("pipe", None, None, "dp"), P("pipe", None, None, "dp")),
        check_vma=False,
    )
```

time: 488 us -> 181 us (0.37)
  matrix products: 133 us -> 0 us
  local copies, waits for them, and re-layouts: 138 us -> 28.4 us
  waiting for transfers between devices: 136 us -> 44.3 us
  Pallas kernels: 0 us -> 80.9 us
  other arithmetic: 26.3 us -> 6.08 us
  starting transfers between devices: 32.9 us -> 17.3 us
  between operations: 15.9 us -> 0.75 us
    dot_general x72 -> x0, matrix products: 133 us -> none  [the longest x28 49.7 us: block_product(): return jnp.einsum(spec, left, right, preferred_element_type=jnp.float32)]
    pallas_call x0 -> x2, Pallas kernels: none -> 80.9 us  [call(): pl.pallas_call(kernel, out_shape=[jax.ShapeDtypeStruct(*out) for out in o...]
    convert_element_type x24 -> x0, local copies, waits for them, and re-layouts: 56.7 us -> none  [pick_blocks(): return jnp.einsum('nb,bir->nir', table.astype(jnp.bfloat16), source, pref...]
    unnamed x2 -> x0, waiting for transfers between devices: 55.9 us -> none
    ppermute x10 -> x5, waiting for transfers between devices: 80.1 us -> 44.3 us  [the longest x1 21 us: shards(): lax.ppermute(share, 'pipe', [(i, sections - 1 - i) for i in range(section...]
    another operation x19 -> x2, local copies, waits for them, and re-layouts: 43.3 us -> 14.3 us  [shards(): w = weights[0].reshape(2, 2, count, BLOCK, BLOCK)]
    reshape x12 -> x1, local copies, waits for them, and re-layouts: 17.1 us -> 0.66 us  [shards(): pat = jnp.stack([lax.dynamic_index_in_dim(pattern, me, 0, keepdims=False)...]
    ppermute x10 -> x5, starting transfers between devices: 32.9 us -> 17.3 us  [the longest x1 7.97 us: shards(): lax.ppermute(share, 'pipe', [(i, sections - 1 - i) for i in range(section...]
  transfers between devices with their start and end apart: 11 -> 5, of which waited for: 7 -> 5; matrix products, arithmetic and copies ran while one was open for 39% -> 3% of each run, Pallas kernels for 0% -> 0%
where the time goes in v1:
time: 181 us; the launch traced here: 178 us
  Pallas kernels  80.9 us (45%)
  waiting for transfers between devices  44.3 us (24%)
  local copies, waits for them, and re-layouts  28.4 us (16%)
  starting transfers between devices  17.3 us (10%)
  other arithmetic  6.08 us (3%)
    pallas_call x2, Pallas kernels, call(): pl.pallas_call(kernel, out_shape=[jax.ShapeDtypeStruct(*out) for out in o...  80.9 us
    ppermute x1, waiting for transfers between devices, shards(): lax.ppermute(share, 'pipe', [(i, sections - 1 - i) for i in range(section...  21 us
    another operation x2, local copies, waits for them, and re-layouts, shards(): w = weights[0].reshape(2, 2, count, BLOCK, BLOCK)  14.3 us
    ppermute x1, waiting for transfers between devices, shards(): got = lax.ppermute(given, 'dp', [(i, i ^ 2) for i in range(4)])  14.2 us
    unnamed x22, local copies, waits for them, and re-layouts  8.76 us
    ppermute x1, starting transfers between devices, shards(): lax.ppermute(share, 'pipe', [(i, sections - 1 - i) for i in range(section...  7.97 us
    ppermute x1, starting transfers between devices, shards(): lax.ppermute(send_up, 'pipe', [(i, i + 1) for i in range(sections - 1)])  5.64 us
    ppermute x1, waiting for transfers between devices, shards(): lax.ppermute(send_down, 'pipe', [(i + 1, i) for i in range(sections - 1)])  5.2 us
  transfers between devices with their start and end apart: 5, of which 5 were waited for; matrix products, arithmetic and copies ran while one was open for 3% of the time, Pallas kernels for 0%

profile of v1, /device:TPU:1, one launch (start us, length us, event | category | flops | bytes accessed | tf_op | source)
XLA Modules:
  0.0 177.8 jit_solution(11636387252417026395)
XLA Ops:
  0.6 0.7 constant_dynamic-slice_fusion.2
  1.3 0.7 reshape.33.pat.refs_0_
  2.0 7.6 %reshape_squeeze.3.w.refs_10_ = bf16[2,2,72,64,64]{4,3,2,1,0:T(8,128)(2,1)} reshape(bf16[1,2,2,72,4096]{4,3,2,1,0:T(8,128)(2,1)} %param.12) | data formatting | bytes 4718592 | tf_op jit(solution)/shard_map/reshape;squeeze | solution.py:281
  9.6 0.0 copy-start.2
  9.6 6.7 %copy.25 = bf16[2,2,72,64,64]{3,4,2,1,0:T(8,128)(2,1)} copy(bf16[2,2,72,64,64]{4,3,2,1,0:T(8,128)(2,1)} %reshape_squeeze.3.w.refs_10_) | data formatting | bytes 4718592 | tf_op jit(solution)/shard_map/reshape;squeeze | solution.py:281
  16.3 0.0 copy-done.2
  16.3 0.0 copy-start.5
  16.3 0.0 copy-start.6
  16.3 1.6 copy.23
  17.9 0.0 copy-done.5
  17.9 1.2 copy.21
  19.1 0.0 copy-done.6
  19.1 1.2 copy.22
  20.2 0.0 copy-start.7
  20.2 29.4 %shard_map.102 = (bf16[2,1536,32]{2,1,0:T(8,128)(2,1)}, bf16[768,128]{1,0:T(8,128)(2,1)}, bf16[768,128]{1,0:T(8,128)(2,1)}, bf16[96,64,128]{2,1,0:T(8,128)(2,1)}, bf16[96,64,128]{2,1,0:T(8,128)(2,1)}) custom-call(s32[288]{0:T(512)} %reshape.33.pat.refs_0_, bf16[2,1536,32]{2,1,0:T(8,128)(2,1)} %bitcast.28, bf16[2,1536,32]{2,1,0:T(8,128)(2,1)} %bitcast.30, ...), custom_call_target="tpu_custom_call" | custom-call | tf_op jit(solution)/shard_map/pallas_call | solution.py:257
  49.6 5.6 %collective-permute-start = (bf16[768,128]{1,0:T(8,128)(2,1)}, bf16[768,128]{1,0:T(8,128)(2,1)S(1)}, u32[]{:S(2)}, u32[]{:S(2)}) collective-permute-start(bf16[768,128]{1,0:T(8,128)(2,1)} %get-tuple-element.13), channel_id=1, source_target_pairs={{0,1},{1,2},{2,3},{3,4},{4,5},{5,6},{6,7},{7,8},{8,9},{9,10},{10,1... | collective-permute-start | bytes 589832 | tf_op jit(solution)/shard_map/ppermute | solution.py:296
  55.3 1.3 collective-permute-start.1
  56.6 0.0 copy-done.7
  56.6 1.2 copy.24
  57.8 1.4 collective-permute-done.refs_6_
  59.1 0.0 copy-start.3
  59.2 5.2 %collective-permute-done.1.refs_7_ = bf16[768,128]{1,0:T(8,128)(2,1)S(1)} collective-permute-done((bf16[768,128]{1,0:T(8,128)(2,1)}, bf16[768,128]{1,0:T(8,128)(2,1)S(1)}, u32[]{:S(2)}, u32[]{:S(2)}) %collective-permute-start.1) | collective-permute-done | bytes 196640 | tf_op jit(solution)/shard_map/ppermute | solution.py:297
  64.4 0.0 copy-start.4
  64.4 0.0 copy-done.3
  64.4 0.7 copy-done.4
  65.0 51.5 %shard_map.103 = (bf16[2,1536,32]{2,1,0:T(8,128)(2,1)}, bf16[2,1536,32]{2,1,0:T(8,128)(2,1)}, bf16[2,2,72,32,128]{4,3,2,1,0:T(8,128)(2,1)}) custom-call(s32[288]{0:T(512)} %reshape.33.pat.refs_0_, bf16[2,1536,32]{2,1,0:T(8,128)(2,1)} %bitcast.29, bf16[2,1536,32]{2,1,0:T(8,128)(2,1)} %bitcast.31, bf16[2,2,1536,32]{3,2,1,0:T(8,128)(2,1)} %bitcast.27, ...), custom_call_target="tpu_custom_call" | custom-call | tf_op jit(solution)/shard_map/pallas_call | solution.py:257
  116.5 0.0 copy-start
  116.5 1.7 dynamic-slice_bitcast_fusion
  118.2 2.0 %collective-permute-start.2 = (bf16[2,2,2,18,32,128]{5,4,3,2,1,0:T(8,128)(2,1)S(1)}, bf16[2,2,2,18,32,128]{5,4,3,2,1,0:T(8,128)(2,1)}, u32[]{:S(2)}, u32[]{:S(2)}) collective-permute-start(bf16[2,2,2,18,32,128]{5,4,3,2,1,0:T(8,128)(2,1)S(1)} %dynamic-slice_bitcast_fusion), channel_id=1, source_target_pairs={{0,64},{64,0},{128,192},{192,128},{1,65},{65,1},{129,193},{193,129... | collective-permute-start | bytes 3538952 | tf_op jit(solution)/shard_map/ppermute | solution.py:309
  120.1 2.6 %collective-permute-done.2 = bf16[2,2,2,18,32,128]{5,4,3,2,1,0:T(8,128)(2,1)} collective-permute-done((bf16[2,2,2,18,32,128]{5,4,3,2,1,0:T(8,128)(2,1)S(1)}, bf16[2,2,2,18,32,128]{5,4,3,2,1,0:T(8,128)(2,1)}, u32[]{:S(2)}, u32[]{:S(2)}) %collective-permute-start.2) | collective-permute-done | bytes 1179680 | tf_op jit(solution)/shard_map/ppermute | solution.py:309
  122.7 0.0 copy-done
  122.7 1.6 fusion
  124.4 0.5 collective-permute-start.3
  124.9 14.2 %collective-permute-done.3 = bf16[2,2,18,32,128]{4,3,2,1,0:T(8,128)(2,1)S(1)} collective-permute-done((bf16[2,2,18,32,128]{4,3,2,1,0:T(8,128)(2,1)S(1)}, bf16[2,2,18,32,128]{4,3,2,1,0:T(8,128)(2,1)S(1)}, u32[]{:S(2)}, u32[]{:S(2)}) %collective-permute-start.3) | collective-permute-done | bytes 589856 | tf_op jit(solution)/shard_map/ppermute | solution.py:313
  139.1 0.2 fusion.1
  139.3 8.0 %collective-permute-start.4 = (bf16[2,2,18,32,128]{4,3,2,1,0:T(8,128)(2,1)S(1)}, bf16[2,2,18,32,128]{4,3,2,1,0:T(8,128)(2,1)S(1)}, u32[]{:S(2)}, u32[]{:S(2)}) collective-permute-start(bf16[2,2,18,32,128]{4,3,2,1,0:T(8,128)(2,1)S(1)} %fusion.1), channel_id=1, source_target_pairs={{0,63},{1,62},{2,61},{3,60},{4,59},{5,58},{6,57},{7,56},{8,55},{9,... | collective-permute-start | bytes 1769480 | tf_op jit(solution)/shard_map/ppermute | solution.py:315
  147.2 0.0 copy-start.1
  147.2 1.5 constant_dynamic-slice_fusion
  148.7 2.1 %copy.28 = bf16[1,1,2,1536,32]{3,4,2,1,0:T(8,128)(2,1)} copy(bf16[1,1,2,1536,32]{4,3,2,1,0:T(8,128)(2,1)} %bitcast.36) | data formatting | bytes 393216
  150.8 0.0 copy-done.1
  150.8 0.9 copy.29
  151.7 21.0 %collective-permute-done.4 = bf16[2,2,18,32,128]{4,3,2,1,0:T(8,128)(2,1)S(1)} collective-permute-done((bf16[2,2,18,32,128]{4,3,2,1,0:T(8,128)(2,1)S(1)}, bf16[2,2,18,32,128]{4,3,2,1,0:T(8,128)(2,1)S(1)}, u32[]{:S(2)}, u32[]{:S(2)}) %collective-permute-start.4) | collective-permute-done | bytes 589856 | tf_op jit(solution)/shard_map/ppermute | solution.py:315
  172.7 0.2 add_multiply_fusion
  172.9 0.1 copy.27
  173.0 0.6 div.21
  173.7 4.1 %subtract_convert_fusion = (bf16[1,2,2,18,4096]{4,2,3,1,0:T(2,128)(2,1)}, f32[1,2,2,18,4096]{4,2,3,1,0:T(2,128)}) fusion(bf16[1,2,2,18,4096]{4,3,2,1,0:T(8,128)(2,1)S(1)} %constant_dynamic-slice_fusion, f32[1,2,2,18,4096]{4,2,3,1,0:T(2,128)S(1)} %div.21, f32[1,2,2,18,4096]{4,2,3,1,0:T(2,128)} %param.13), kind=kLoop, calls=%fused_computation.4 | loop fusion | flops 1769472 | bytes 4718592 | tf_op jit(solution)/shard_map/convert_element_type | solution.py:320
  (2 shorter events, 0.1 us)
Async XLA Ops:
  9.6 6.7 %copy-start.2 = (bf16[1,1,2,2,1536,32]{4,5,3,2,1,0:T(8,128)(2,1)S(1)}, bf16[1,1,2,2,1536,32]{4,5,3,2,1,0:T(8,128)(2,1)}, u32[]{:S(2)}) copy-start(bf16[1,1,2,2,1536,32]{4,5,3,2,1,0:T(8,128)(2,1)} %param.9) | copy-start | bytes 1179652
  16.3 1.6 copy-start.5
  16.3 2.7 %copy-start.6 = (bf16[1,1,2,1536,32]{3,4,2,1,0:T(8,128)(2,1)S(1)}, bf16[1,1,2,1536,32]{3,4,2,1,0:T(8,128)(2,1)}, u32[]{:S(2)}) copy-start(bf16[1,1,2,1536,32]{3,4,2,1,0:T(8,128)(2,1)} %param.8) | copy-start | bytes 589828
  20.2 36.4 %copy-start.7 = (bf16[1,2,1536,32]{2,3,1,0:T(8,128)(2,1)S(1)}, bf16[1,2,1536,32]{2,3,1,0:T(8,128)(2,1)}, u32[]{:S(2)}) copy-start(bf16[1,2,1536,32]{2,3,1,0:T(8,128)(2,1)} %param.10) | copy-start | bytes 589828
  49.6 9.5 %collective-permute-start = (bf16[768,128]{1,0:T(8,128)(2,1)}, bf16[768,128]{1,0:T(8,128)(2,1)S(1)}, u32[]{:S(2)}, u32[]{:S(2)}) collective-permute-start(bf16[768,128]{1,0:T(8,128)(2,1)} %get-tuple-element.13), channel_id=1, source_target_pairs={{0,1},{1,2},{2,3},{3,4},{4,5},{5,6},{6,7},{7,8},{8,9},{9,10},{10,1... | collective-permute-start | bytes 589832 | tf_op jit(solution)/shard_map/ppermute | solution.py:296
  55.3 9.1 %collective-permute-start.1 = (bf16[768,128]{1,0:T(8,128)(2,1)}, bf16[768,128]{1,0:T(8,128)(2,1)S(1)}, u32[]{:S(2)}, u32[]{:S(2)}) collective-permute-start(bf16[768,128]{1,0:T(8,128)(2,1)} %get-tuple-element.14), channel_id=1, source_target_pairs={{1,0},{2,1},{3,2},{4,3},{5,4},{6,5},{7,6},{8,7},{9,8},{10,9},{11,1... | collective-permute-start | bytes 589832 | tf_op jit(solution)/shard_map/ppermute | solution.py:297
  59.1 5.2 %copy-start.3 = (bf16[768,128]{1,0:T(8,128)(2,1)}, bf16[768,128]{1,0:T(8,128)(2,1)S(1)}, u32[]{:S(2)}) copy-start(bf16[768,128]{1,0:T(8,128)(2,1)S(1)} %collective-permute-done.refs_6_) | copy-start | bytes 589828
  64.4 0.7 copy-start.4
  116.5 6.3 %copy-start = (bf16[2,2,72,32,128]{4,3,2,1,0:T(8,128)(2,1)S(1)}, bf16[2,2,72,32,128]{4,3,2,1,0:T(8,128)(2,1)}, u32[]{:S(2)}) copy-start(bf16[2,2,72,32,128]{4,3,2,1,0:T(8,128)(2,1)} %get-tuple-element.19) | copy-start | bytes 7077892
  118.2 4.6 %collective-permute-start.2 = (bf16[2,2,2,18,32,128]{5,4,3,2,1,0:T(8,128)(2,1)S(1)}, bf16[2,2,2,18,32,128]{5,4,3,2,1,0:T(8,128)(2,1)}, u32[]{:S(2)}, u32[]{:S(2)}) collective-permute-start(bf16[2,2,2,18,32,128]{5,4,3,2,1,0:T(8,128)(2,1)S(1)} %dynamic-slice_bitcast_fusion), channel_id=1, source_target_pairs={{0,64},{64,0},{128,192},{192,128},{1,65},{65,1},{129,193},{193,129... | collective-permute-start | bytes 3538952 | tf_op jit(solution)/shard_map/ppermute | solution.py:309
  124.4 14.7 %collective-permute-start.3 = (bf16[2,2,18,32,128]{4,3,2,1,0:T(8,128)(2,1)S(1)}, bf16[2,2,18,32,128]{4,3,2,1,0:T(8,128)(2,1)S(1)}, u32[]{:S(2)}, u32[]{:S(2)}) collective-permute-start(bf16[2,2,18,32,128]{4,3,2,1,0:T(8,128)(2,1)S(1)} %dynamic-slice_bitcast_fusion.1), channel_id=1, source_target_pairs={{0,128},{64,192},{128,0},{192,64},{1,129},{65,193},{129,1},{193,65... | collective-permute-start | bytes 1769480 | tf_op jit(solution)/shard_map/ppermute | solution.py:313
  139.3 33.5 %collective-permute-start.4 = (bf16[2,2,18,32,128]{4,3,2,1,0:T(8,128)(2,1)S(1)}, bf16[2,2,18,32,128]{4,3,2,1,0:T(8,128)(2,1)S(1)}, u32[]{:S(2)}, u32[]{:S(2)}) collective-permute-start(bf16[2,2,18,32,128]{4,3,2,1,0:T(8,128)(2,1)S(1)} %fusion.1), channel_id=1, source_target_pairs={{0,63},{1,62},{2,61},{3,60},{4,59},{5,58},{6,57},{7,56},{8,55},{9,... | collective-permute-start | bytes 1769480 | tf_op jit(solution)/shard_map/ppermute | solution.py:315
  147.2 3.6 %copy-start.1 = (bf16[2,1536,32]{2,1,0:T(8,128)(2,1)S(1)}, bf16[2,1536,32]{2,1,0:T(8,128)(2,1)}, u32[]{:S(2)}) copy-start(bf16[2,1536,32]{2,1,0:T(8,128)(2,1)} %get-tuple-element.18) | copy-start | bytes 589828

commit v2 on v1

--- a/solution.py
+++ b/solution.py
@@ -162,9 +162,9 @@
 
 def second_kernel(
     sections, pat, acts, cot, stash, entering, y_first, got_up, got_down, hid1, gp1, w, wt,
-    forward, backward, grads, x, gy, xs, gys, hid, gp, pre, gh, out,
+    forward, backward, xs, gys, hid, gp, x, gy, pre, gh, out,
 ):
-    blocks_d, blocks_f, count = out.shape[0], pre.shape[0], w.shape[2]
+    blocks_d, blocks_f = out.shape[0], pre.shape[0]
     me = lax.axis_index("pipe")
     at_entry, at_exit = me == 0, me == sections - 1
     clear(pre)
@@ -236,20 +236,109 @@
 
     lax.fori_loop(0, blocks_f, join, 0)
 
-    def two_wide(value):
-        return jnp.concatenate([value[: BLOCK // 2], value[BLOCK // 2 :]], axis=1).astype(jnp.bfloat16)
-
-    for copy in range(2):
-
-        def outer(ns, copy=copy):
-            for n in ns:
-                d, f = place(pat, copy, 0, n, blocks_d, blocks_f)
-                grads[copy, 0, n] = two_wide(mul_nt(xs[copy, d], gp[f]))
-            for n in ns:
-                d, f = place(pat, copy, 1, n, blocks_d, blocks_f)
-                grads[copy, 1, n] = two_wide(mul_nt(hid[f], gys[copy, d]))
-
-        each_block(count, outer)
+
+def two_wide(value):
+    return jnp.concatenate([value[: BLOCK // 2], value[BLOCK // 2 :]], axis=1).astype(jnp.bfloat16)
+
+
+def sum_kernel(
+    sections, quarter, pat, xs, gys, hid, gp, total, grads, got_core, to_side, got_side, share, got_far, wide, *sems
+):
+    core_sent, core_got, side_sent, side_got, far_sent, far_got = sems
+    blocks_d, blocks_f = xs.shape[1], gp.shape[0]
+    me, group = lax.axis_index("pipe"), lax.axis_index("dp")
+    core, side = lax.rem(group, 2), group // 2
+    near, over, far = group + 1 - 2 * core, group + 2 - 4 * side, sections - 1 - me
+    barrier = pltpu.get_barrier_semaphore()
+    for other in ((near, me), (over, me), (group, far)):
+        pl.semaphore_signal(barrier, inc=1, device_id=other, device_id_type=pl.DeviceIdType.MESH)
+    pl.semaphore_wait(barrier, 3)
+    half = BLOCK // 2
+
+    def compute(j):
+        copy, proj = divmod(j, 2)
+        for q in range(4):
+
+            def step(i, carry, q=q):
+                for u in range(6):
+                    n = i * 6 + u
+                    d, f = place(pat, copy, proj, q * quarter + n, blocks_d, blocks_f)
+                    if proj == 0:
+                        value = mul_nt(xs[copy, d], gp[f])
+                    else:
+                        value = mul_nt(hid[f], gys[copy, d])
+                    grads[j, q // 2, q % 2, pl.ds(pl.multiple_of(n * half, half), half)] = two_wide(value)
+                return carry
+
+            lax.fori_loop(0, quarter // 6, step, 0)
+
+    def copies(j):
+        def remote(source, target, sent, got, to):
+            return pltpu.make_async_remote_copy(
+                src_ref=source, dst_ref=target, send_sem=sent.at[j], recv_sem=got.at[j],
+                device_id=to, device_id_type=pl.DeviceIdType.MESH,
+            )
+
+        return (
+            remote(grads.at[j, :, 1 - core], got_core.at[j], core_sent, core_got, (near, me)),
+            remote(to_side.at[j], got_side.at[j], side_sent, side_got, (over, me)),
+            remote(share.at[j], got_far.at[j], far_sent, far_got, (group, far)),
+        )
+
+    wires = [copies(j) for j in range(4)]
+
+    def pieces(body):
+        def step(i, carry):
+            body(pl.ds(pl.multiple_of(i * 64, 64), 64))
+            return carry
+
+        lax.fori_loop(0, quarter * half // 64, step, 0)
+
+    def after_core(j):
+        wires[j][0].wait_recv()
+
+        def body(rows):
+            value = grads[j, 1 - side, core, rows].astype(jnp.float32) + got_core[j, 1 - side, rows].astype(jnp.float32)
+            to_side[j, rows] = value.astype(jnp.bfloat16)
+
+        pieces(body)
+        wires[j][1].start()
+
+    def after_side(j):
+        wires[j][1].wait_recv()
+
+        def body(rows):
+            value = grads[j, side, core, rows].astype(jnp.float32) + got_core[j, side, rows].astype(jnp.float32)
+            share[j, rows] = (value + got_side[j, rows].astype(jnp.float32)).astype(jnp.bfloat16)
+
+        pieces(body)
+        wires[j][2].start()
+
+    def after_far(j):
+        wires[j][2].wait_recv()
+        mine = (j + 2) % 4
+        copy, proj = divmod(mine, 2)
+
+        def body(rows):
+            wide[rows, :] = share[mine, rows].astype(jnp.float32) + got_far[j, rows].astype(jnp.float32)
+
+        pieces(body)
+        for t in range(half):
+            total[copy, proj, :, t * 128 : (t + 1) * 128] = wide[pl.ds(t, quarter, stride=half), :]
+
+    for step in range(6):
+        if step < 4:
+            compute(step)
+            wires[step][0].start()
+        if 1 <= step < 5:
+            after_core(step - 1)
+        if 2 <= step:
+            after_side(step - 2)
+    for j in range(4):
+        after_far(j)
+    for j in range(4):
+        for wire in wires[j]:
+            wire.wait_send()
 
 
 def call(kernel, args, outs, scratch):
@@ -295,26 +384,32 @@
     )
     got_up = lax.ppermute(send_up, "pipe", [(i, i + 1) for i in range(sections - 1)])
     got_down = lax.ppermute(send_down, "pipe", [(i + 1, i) for i in range(sections - 1)])
-    forward, backward, grads = call(
+    forward, backward, xs, gys, hid, gp = call(
         lambda *refs: second_kernel(sections, *refs),
         (pat, acts, cot, saved, fresh, y_first, got_up, got_down, hid, gp, w, wt),
-        [(acts.shape, bf16), (acts.shape, bf16), ((2, 2, count, BLOCK // 2, 128), bf16)],
-        [((2, *d_block), bf16)] * 4 + [(f_block, bf16)] * 2 + [(f_block, f32)] * 2 + [(d_block, f32)],
+        [(acts.shape, bf16)] * 2 + [((2, *d_block), bf16)] * 2 + [(f_block, bf16)] * 2,
+        [((2, *d_block), bf16)] * 2 + [(f_block, f32)] * 2 + [(d_block, f32)],
     )
     quarter = count // 4
-    core, side = group % 2, group // 2
-    grads = grads.reshape(2, 2, 2, 2, quarter, BLOCK // 2, 128)
-    given = lax.dynamic_index_in_dim(grads, 1 - core, 3, keepdims=False)
-    kept = lax.dynamic_index_in_dim(grads, core, 3, keepdims=False)
-    got = lax.ppermute(given, "dp", [(i, i ^ 1) for i in range(4)])
-    summed = (kept.astype(f32) + got.astype(f32)).astype(bf16)
-    given = lax.dynamic_index_in_dim(summed, 1 - side, 2, keepdims=False)
-    kept = lax.dynamic_index_in_dim(summed, side, 2, keepdims=False)
-    got = lax.ppermute(given, "dp", [(i, i ^ 2) for i in range(4)])
-    share = (kept.astype(f32) + got.astype(f32)).astype(bf16)
-    mirrored = lax.ppermute(share, "pipe", [(i, sections - 1 - i) for i in range(sections)])
-    total = share.astype(f32) + mirrored[::-1].astype(f32)
-    total = total.reshape(2, 2, quarter, -1)
+    chunk = (4, quarter * BLOCK // 2, 128)
+    smem, vmem = pl.BlockSpec(memory_space=pltpu.SMEM), pl.BlockSpec(memory_space=pltpu.VMEM)
+    total = pl.pallas_call(
+        lambda *refs: sum_kernel(sections, quarter, *refs),
+        out_shape=jax.ShapeDtypeStruct((2, 2, quarter, weights.shape[4]), f32),
+        in_specs=[smem] + [vmem] * 4,
+        out_specs=vmem,
+        scratch_shapes=[
+            pltpu.VMEM((4, 2, 2, *chunk[1:]), bf16),
+            pltpu.VMEM((4, 2, *chunk[1:]), bf16),
+            pltpu.VMEM(chunk, bf16),
+            pltpu.VMEM(chunk, bf16),
+            pltpu.VMEM(chunk, bf16),
+            pltpu.VMEM(chunk, bf16),
+            pltpu.VMEM(chunk[1:], f32),
+        ]
+        + [pltpu.SemaphoreType.DMA((4,))] * 6,
+        compiler_params=pltpu.CompilerParams(collective_id=0, has_side_effects=True, vmem_limit_bytes=VMEM_BYTES),
+    )(pat, xs, gys, hid, gp)
     momentum_next = BETA * momentum[0] + total / (2 * tokens)
     own = lax.dynamic_slice_in_dim(weights[0], group * quarter, quarter, axis=2)
     weights_next = (own.astype(f32) - STEP * momentum_next).astype(bf16)

time: 181 us -> 177 us (0.978)
  Pallas kernels: 80.9 us -> 127 us
  waiting for transfers between devices: 44.3 us -> 6.56 us
  starting transfers between devices: 17.3 us -> 6.94 us
  other arithmetic: 6.08 us -> 2.41 us
    pallas_call x0 -> x1, Pallas kernels: none -> 51.8 us  [shards(): pl.pallas_call(lambda *refs: sum_kernel(sections, quarter, *refs), out_sh...]
    ppermute x3 -> x0, waiting for transfers between devices: 37.7 us -> none  [the longest x1 21 us: shards(): lax.ppermute(share, 'pipe', [(i, sections - 1 - i) for i in range(section...]
    ppermute x3 -> x0, starting transfers between devices: 10.4 us -> none  [the longest x1 7.97 us: shards(): lax.ppermute(share, 'pipe', [(i, sections - 1 - i) for i in range(section...]
    unnamed x22 -> x20, local copies, waits for them, and re-layouts: 8.76 us -> 15.2 us
    convert_element_type x3 -> x0, other arithmetic: 5.88 us -> none  [the longest x1 4.1 us: shards(): weights_next = (own.astype(f32) - STEP * momentum_next).astype(bf16)]
    pallas_call x2, Pallas kernels: 80.9 us -> 75.5 us  [call(): pl.pallas_call(kernel, out_shape=[jax.ShapeDtypeStruct(*out) for out in o...]
    broadcast_in_dim x0 -> x1, other arithmetic: none -> 2.4 us  [shards(): momentum_next[None]]
  transfers between devices with their start and end apart: 5 -> 2, of which waited for: 5 -> 2; matrix products, arithmetic and copies ran while one was open for 3% -> 1% of each run, Pallas kernels for 0% -> 0%
where the time goes in v2:
time: 177 us; the launch traced here: 173 us
  Pallas kernels  127 us (72%)
  local copies, waits for them, and re-layouts  29.3 us (17%)
  starting transfers between devices  6.94 us (4%)
  waiting for transfers between devices  6.56 us (4%)
  other arithmetic  2.41 us (1%)
    pallas_call x2, Pallas kernels, call(): pl.pallas_call(kernel, out_shape=[jax.ShapeDtypeStruct(*out) for out in o...  75.5 us
    pallas_call x1, Pallas kernels, shards(): pl.pallas_call(lambda *refs: sum_kernel(sections, quarter, *refs), out_sh...  51.8 us
    unnamed x20, local copies, waits for them, and re-layouts  15.2 us
    another operation x2, local copies, waits for them, and re-layouts, shards(): w = weights[0].reshape(2, 2, count, BLOCK, BLOCK)  12.8 us
    ppermute x1, starting transfers between devices, shards(): lax.ppermute(send_up, 'pipe', [(i, i + 1) for i in range(sections - 1)])  5.65 us
    ppermute x1, waiting for transfers between devices, shards(): lax.ppermute(send_down, 'pipe', [(i + 1, i) for i in range(sections - 1)])  5.2 us
  transfers between devices with their start and end apart: 2, of which 2 were waited for; matrix products, arithmetic and copies ran while one was open for 1% of the time, Pallas kernels for 0%

profile of v2, /device:TPU:1, one launch (start us, length us, event | category | flops | bytes accessed | tf_op | source)
XLA Modules:
  0.0 173.2 jit_solution(10020072065740848745)
XLA Ops:
  0.6 0.0 copy-start.2
  0.6 0.7 constant_dynamic-slice_fusion.1
  1.4 0.7 reshape.16.pat.refs_0_
  2.1 2.1 %copy.22 = bf16[1,1,2,1536,32]{4,3,2,1,0:T(8,128)(2,1)} copy(bf16[1,1,2,1536,32]{3,4,2,1,0:T(8,128)(2,1)} %param.7) | data formatting | bytes 393216 | tf_op args[0]
  4.1 0.0 copy-start
  4.2 2.2 %copy.23 = bf16[1,1,2,1536,32]{4,3,2,1,0:T(8,128)(2,1)} copy(bf16[1,1,2,1536,32]{3,4,2,1,0:T(8,128)(2,1)} %param.8) | data formatting | bytes 393216 | tf_op args[1]
  6.4 0.0 copy-done.2
  6.4 1.5 copy.24
  7.9 0.0 copy-done
  7.9 6.1 %reshape_squeeze.3.w.refs_10_ = bf16[2,2,72,64,64]{4,3,2,1,0:T(8,128)(2,1)} reshape(bf16[1,2,2,72,4096]{4,3,2,1,0:T(8,128)(2,1)S(1)} %copy-done) | data formatting | bytes 4718592 | tf_op jit(solution)/shard_map/reshape;squeeze | solution.py:370
  14.0 6.7 %copy.26 = bf16[2,2,72,64,64]{3,4,2,1,0:T(8,128)(2,1)} copy(bf16[2,2,72,64,64]{4,3,2,1,0:T(8,128)(2,1)} %reshape_squeeze.3.w.refs_10_) | data formatting | bytes 4718592 | tf_op jit(solution)/shard_map/reshape;squeeze | solution.py:370
  20.7 0.0 copy-start.5
  20.7 29.4 %shard_map.102 = (bf16[2,1536,32]{2,1,0:T(8,128)(2,1)}, bf16[768,128]{1,0:T(8,128)(2,1)}, bf16[768,128]{1,0:T(8,128)(2,1)}, bf16[96,64,128]{2,1,0:T(8,128)(2,1)}, bf16[96,64,128]{2,1,0:T(8,128)(2,1)}) custom-call(s32[288]{0:T(512)} %reshape.16.pat.refs_0_, bf16[2,1536,32]{2,1,0:T(8,128)(2,1)} %bitcast.26, bf16[2,1536,32]{2,1,0:T(8,128)(2,1)} %bitcast.28, ...), custom_call_target="tpu_custom_call" | custom-call | tf_op jit(solution)/shard_map/pallas_call | solution.py:346
  50.1 5.6 %collective-permute-start = (bf16[768,128]{1,0:T(8,128)(2,1)}, bf16[768,128]{1,0:T(8,128)(2,1)S(1)}, u32[]{:S(2)}, u32[]{:S(2)}) collective-permute-start(bf16[768,128]{1,0:T(8,128)(2,1)} %get-tuple-element.16), channel_id=1, source_target_pairs={{0,1},{1,2},{2,3},{3,4},{4,5},{5,6},{6,7},{7,8},{8,9},{9,10},{10,1... | collective-permute-start | bytes 589832 | tf_op jit(solution)/shard_map/ppermute | solution.py:385
  55.7 1.3 collective-permute-start.1
  57.0 0.0 copy-done.5
  57.0 1.2 copy.25
  58.2 1.4 collective-permute-done.refs_6_
  59.6 0.0 copy-start.3
  59.6 5.2 %collective-permute-done.1.refs_7_ = bf16[768,128]{1,0:T(8,128)(2,1)S(1)} collective-permute-done((bf16[768,128]{1,0:T(8,128)(2,1)}, bf16[768,128]{1,0:T(8,128)(2,1)S(1)}, u32[]{:S(2)}, u32[]{:S(2)}) %collective-permute-start.1) | collective-permute-done | bytes 196640 | tf_op jit(solution)/shard_map/ppermute | solution.py:386
  64.8 0.0 copy-start.4
  64.8 0.0 copy-done.3
  64.8 0.7 copy-done.4
  65.4 46.1 %shard_map.103 = (bf16[2,1536,32]{2,1,0:T(8,128)(2,1)}, bf16[2,1536,32]{2,1,0:T(8,128)(2,1)}, bf16[2,24,64,128]{3,2,1,0:T(8,128)(2,1)}, bf16[2,24,64,128]{3,2,1,...) custom-call(s32[288]{0:T(512)} %reshape.16.pat.refs_0_, bf16[2,1536,32]{2,1,0:T(8,128)(2,1)} %bitcast.27, ...), custom_call_target="tpu_custom_call" | custom-call | tf_op jit(solution)/shard_map/pallas_call | solution.py:346
  111.5 2.1 %copy.28 = bf16[1,1,2,1536,32]{3,4,2,1,0:T(8,128)(2,1)} copy(bf16[1,1,2,1536,32]{4,3,2,1,0:T(8,128)(2,1)} %bitcast.32) | data formatting | bytes 393216
  113.6 2.1 %copy.29 = bf16[1,1,2,1536,32]{3,4,2,1,0:T(8,128)(2,1)} copy(bf16[1,1,2,1536,32]{4,3,2,1,0:T(8,128)(2,1)} %bitcast.31) | data formatting | bytes 393216
  115.7 0.0 copy-start.1
  115.7 51.8 %shard_map.104 = f32[2,2,18,4096]{3,2,1,0:T(8,128)} custom-call(s32[288]{0:T(512)} %reshape.16.pat.refs_0_, bf16[2,24,64,128]{3,2,1,0:T(8,128)(2,1)} %get-tuple-element.22.refs_1_, bf16[2,24,64,128]{3,2,1,0:T(8,128)(2,1)} %get-tuple-element.23.refs_2_, bf16[96,64,128]{2,1,0:T(8,128)(2,1)} %get-tuple-element.24.refs_3_, ...), custom_call_target="tpu_custom_call" | custom-call | tf_op jit(solution)/shard_map/pallas_call | solution.py:396
  167.5 0.0 copy-done.1
  167.5 2.4 %fusion.2 = (f32[1,2,2,18,4096]{4,3,2,1,0:T(8,128)S(1)}, bf16[1,2,2,18,4096]{4,3,2,1,0:T(8,128)(2,1)S(1)}) fusion(f32[2,2,18,4096]{3,2,1,0:T(8,128)} %shard_map.104, f32[1,2,2,18,4096]{4,2,3,1,0:T(2,128)S(1)} %copy-done.1, bf16[1,2,2,72,4096]{4,3,2,1,0:T(8,128)(2,1)S(1)} %copy-done, s32[]{:T(128)S(6)} %select_n.12), kind=kLoop, calls=%fused_computation.5 | loop fusion | flops 2064384 | bytes 4718596 | tf_op jit(solution)/shard_map/broadcast_in_dim | solution.py:416
  169.9 1.9 %copy.31 = f32[1,2,2,18,4096]{4,2,3,1,0:T(2,128)} copy(f32[1,2,2,18,4096]{4,3,2,1,0:T(8,128)S(1)} %get-tuple-element.34) | data formatting | bytes 2359296
  171.8 1.4 copy.30
  (1 shorter events, 0.0 us)
Async XLA Ops:
  0.6 5.8 %copy-start.2 = (bf16[1,1,2,2,1536,32]{4,5,3,2,1,0:T(8,128)(2,1)S(1)}, bf16[1,1,2,2,1536,32]{4,5,3,2,1,0:T(8,128)(2,1)}, u32[]{:S(2)}) copy-start(bf16[1,1,2,2,1536,32]{4,5,3,2,1,0:T(8,128)(2,1)} %param.9) | copy-start | bytes 1179652
  4.1 3.7 %copy-start = (bf16[1,2,2,72,4096]{4,3,2,1,0:T(8,128)(2,1)S(1)}, bf16[1,2,2,72,4096]{4,3,2,1,0:T(8,128)(2,1)}, u32[]{:S(2)}) copy-start(bf16[1,2,2,72,4096]{4,3,2,1,0:T(8,128)(2,1)} %param.12) | copy-start | bytes 7077892
  20.7 36.4 %copy-start.5 = (bf16[1,2,1536,32]{2,3,1,0:T(8,128)(2,1)S(1)}, bf16[1,2,1536,32]{2,3,1,0:T(8,128)(2,1)}, u32[]{:S(2)}) copy-start(bf16[1,2,1536,32]{2,3,1,0:T(8,128)(2,1)} %param.10) | copy-start | bytes 589828
  50.1 9.5 %collective-permute-start = (bf16[768,128]{1,0:T(8,128)(2,1)}, bf16[768,128]{1,0:T(8,128)(2,1)S(1)}, u32[]{:S(2)}, u32[]{:S(2)}) collective-permute-start(bf16[768,128]{1,0:T(8,128)(2,1)} %get-tuple-element.16), channel_id=1, source_target_pairs={{0,1},{1,2},{2,3},{3,4},{4,5},{5,6},{6,7},{7,8},{8,9},{9,10},{10,1... | collective-permute-start | bytes 589832 | tf_op jit(solution)/shard_map/ppermute | solution.py:385
  55.7 9.1 %collective-permute-start.1 = (bf16[768,128]{1,0:T(8,128)(2,1)}, bf16[768,128]{1,0:T(8,128)(2,1)S(1)}, u32[]{:S(2)}, u32[]{:S(2)}) collective-permute-start(bf16[768,128]{1,0:T(8,128)(2,1)} %get-tuple-element.17), channel_id=1, source_target_pairs={{1,0},{2,1},{3,2},{4,3},{5,4},{6,5},{7,6},{8,7},{9,8},{10,9},{11,1... | collective-permute-start | bytes 589832 | tf_op jit(solution)/shard_map/ppermute | solution.py:386
  59.6 5.2 %copy-start.3 = (bf16[768,128]{1,0:T(8,128)(2,1)}, bf16[768,128]{1,0:T(8,128)(2,1)S(1)}, u32[]{:S(2)}) copy-start(bf16[768,128]{1,0:T(8,128)(2,1)S(1)} %collective-permute-done.refs_6_) | copy-start | bytes 589828
  64.8 0.7 copy-start.4
  115.7 51.8 %copy-start.1 = (f32[1,2,2,18,4096]{4,2,3,1,0:T(2,128)S(1)}, f32[1,2,2,18,4096]{4,2,3,1,0:T(2,128)}, u32[]{:S(2)}) copy-start(f32[1,2,2,18,4096]{4,2,3,1,0:T(2,128)} %param.13) | copy-start | bytes 3538948

commit v3 on v2

v3 whole, which is shorter than its diff:
```python
import jax
import jax.numpy as jnp
from jax import lax
from jax.experimental import pallas as pl
from jax.experimental.pallas import tpu as pltpu
from jax.sharding import PartitionSpec as P

FF = 6144
BLOCK = 64
BETA = 0.9
STEP = 0.2
UNROLL = 8
VMEM_BYTES = 56 * 2**20


def dot(left, right, dims):
    return lax.dot_general(left, right, (dims, ((), ())), preferred_element_type=jnp.float32)


def mul(left, right):
    return dot(left, right, ((1,), (0,)))


def mul_nt(left, right):
    return dot(left, right, ((1,), (1,)))


def gelu_parts(values):
    cdf = 0.5 + 0.5 * lax.erf(values * 0.7071067811865476)
    slope = cdf + values * (0.3989422804014327 * jnp.exp(-0.5 * values * values))
    return values * cdf, slope


def stack_tokens(parts):
    return jnp.concatenate(parts, axis=0).T


def copy_mask(copy, rows):
    lane = lax.broadcasted_iota(jnp.int32, (rows, 128), 1) // 32
    return (lane % 2 == copy).astype(jnp.float32).astype(jnp.bfloat16)


def wide_columns(i):
    return pl.ds(pl.multiple_of(i * 128, 128), 128)


def put(ref, i, value, *lead):
    ref[(*lead, 2 * i)] = value[:BLOCK]
    ref[(*lead, 2 * i + 1)] = value[BLOCK:]


def place(pat, copy, proj, n, blocks_d, blocks_f):
    value = pat[(copy * 2 + proj) * 72 + n]
    if proj == 0:
        r = value // blocks_f
        return r, value - r * blocks_f
    r = value // blocks_d
    return value - r * blocks_d, r


def each_block(count, body):
    def step(i, carry):
        body([i * UNROLL + u for u in range(UNROLL)])
        return carry

    lax.fori_loop(0, count // UNROLL, step, 0)


def section_pass(pat, w, wt, x, gy, pre, gh, out, copy):
    blocks_d, blocks_f, count = x.shape[1], pre.shape[0], w.shape[2]

    def up(ns):
        terms = []
        for n in ns:
            d, f = place(pat, copy, 0, n, blocks_d, blocks_f)
            terms.append((f, mul(wt[copy, 0, n], x[copy, d])))
        for f, term in terms:
            pre[f] += term

    def down(ns):
        terms = []
        for n in ns:
            d, f = place(pat, copy, 1, n, blocks_d, blocks_f)
            terms.append((f, mul(w[copy, 1, n], gy[copy, d])))
        for f, term in terms:
            gh[f] += term

    each_block(count, up)
    each_block(count, down)


def section_close(pat, w, wt, hid, gp, out, copy, fwd_lanes):
    blocks_d, blocks_f, count = out.shape[0], hid.shape[0], w.shape[2]
    lane = lax.broadcasted_iota(jnp.int32, (BLOCK, 128), 1) // 32
    fwd = (lane == fwd_lanes + copy).astype(jnp.float32).astype(jnp.bfloat16)
    own = (lane % 2 == copy).astype(jnp.float32).astype(jnp.bfloat16)

    def down(ns):
        terms = []
        for n in ns:
            d, f = place(pat, copy, 1, n, blocks_d, blocks_f)
            terms.append((d, mul(wt[copy, 1, n], hid[f] * fwd)))
        for d, term in terms:
            out[d] += term

    def up(ns):
        terms = []
        for n in ns:
            d, f = place(pat, copy, 0, n, blocks_d, blocks_f)
            terms.append((d, mul(w[copy, 0, n], gp[f] * own)))
        for d, term in terms:
            out[d] += term

    each_block(count, down)
    each_block(count, up)


def clear(ref):
    def step(i, carry):
        ref[i] = jnp.zeros(ref.shape[1:], ref.dtype)
        return carry

    lax.fori_loop(0, ref.shape[0], step, 0)


def first_kernel(pat, acts, cot, stash, w, wt, send_up, send_down, hid, gp, x, gy, pre, gh, out):
    blocks_d, blocks_f = out.shape[0], pre.shape[0]
    clear(pre)
    clear(gh)
    masks = [copy_mask(copy, 128) for copy in range(2)]
    backward = lax.broadcasted_iota(jnp.int32, (128, 128), 1) >= 64

    def load(i, carry):
        cols = wide_columns(i)
        zero = jnp.zeros((64, 128), jnp.bfloat16)
        inputs = stack_tokens([acts[0, :, cols], acts[1, :, cols], stash[0, 0, :, cols], stash[1, 0, :, cols]])
        cots = stack_tokens([zero, cot[0, :, cols], cot[1, :, cols]])
        for copy in range(2):
            put(x, i, inputs * masks[copy], copy)
            put(gy, i, cots * masks[copy], copy)
        put(out, i, jnp.where(backward, cots.astype(jnp.float32), inputs.astype(jnp.float32)))
        return carry

    lax.fori_loop(0, blocks_d // 2, load, 0)
    for copy in range(2):
        section_pass(pat, w, wt, x, gy, pre, gh, out, copy)

    def act(f, carry):
        hidden, slope = gelu_parts(pre[f])
        hid[f] = hidden.astype(jnp.bfloat16)
        gp[f] = (slope * gh[f]).astype(jnp.bfloat16)
        return carry

    lax.fori_loop(0, blocks_f, act, 0)
    for copy in range(2):
        section_close(pat, w, wt, hid, gp, out, copy, 0)

    def store(i, carry):
        cols = wide_columns(i)
        value = jnp.concatenate([out[2 * i], out[2 * i + 1]], axis=0).astype(jnp.bfloat16).T
        send_up[0:32, cols] = value[0:32]
        send_up[32:64, cols] = value[96:128]
        send_down[:, cols] = value[32:96]
        return carry

    lax.fori_loop(0, blocks_d // 2, store, 0)


def second_kernel(
    sections, pat, acts, cot, stash, entering, sent_up, sent_down, got_up, got_down, hid1, gp1, w, wt,
    forward, backward, xs, gys, hid, gp, x, gy, pre, gh, out,
):
    blocks_d, blocks_f = out.shape[0], pre.shape[0]
    me = lax.axis_index("pipe")
    at_entry, at_exit = me == 0, me == sections - 1
    clear(pre)
    clear(gh)
    row = lax.broadcasted_iota(jnp.int32, (BLOCK, BLOCK), 0)
    col = lax.broadcasted_iota(jnp.int32, (BLOCK, BLOCK), 1)
    source = jnp.where(row < BLOCK // 2, 2 * row, 2 * row - BLOCK + 1)
    evens_first = (col == source).astype(jnp.float32).astype(jnp.bfloat16)
    masks = [copy_mask(copy, 128) for copy in range(2)]
    half_masks = [copy_mask(copy, BLOCK) for copy in range(2)]
    late = lax.broadcasted_iota(jnp.int32, (128, 128), 1) < 64
    late_half = lax.broadcasted_iota(jnp.int32, (BLOCK, 128), 1) < 64
    late_only = late.astype(jnp.float32).astype(jnp.bfloat16)

    def rearranged(value):
        return mul(evens_first, value).astype(jnp.bfloat16)

    def merged(first, second, mask):
        return jnp.where(mask, first.astype(jnp.float32), second.astype(jnp.float32))

    def load(i, carry):
        cols = wide_columns(i)
        x0 = jnp.where(at_entry, entering[0, :, cols], got_up[0:32, cols])
        x1 = jnp.where(at_exit, entering[1, :, cols], got_down[0:32, cols])
        g0 = jnp.where(at_exit, sent_up[0:32, cols], got_down[32:64, cols])
        g1 = jnp.where(at_entry, sent_down[0:32, cols], got_up[32:64, cols])
        s0 = jnp.where(at_exit, acts[0, :, cols], stash[0, 1, :, cols])
        s1 = jnp.where(at_entry, acts[1, :, cols], stash[1, 1, :, cols])
        inputs = stack_tokens([s0, s1, x0, x1])
        cots = stack_tokens([g0, g1, cot[0, :, cols], cot[1, :, cols]])
        saved = stack_tokens([s0, s1, stash[0, 0, :, cols], stash[1, 0, :, cols]])
        put(out, i, merged(cots, inputs, late))
        for copy in range(2):
            put(x, i, inputs * masks[copy], copy)
            put(gys, i, cots * masks[copy], copy)
            put(gy, i, cots * (masks[copy] * late_only), copy)
        for part in range(2):
            piece = rearranged(saved[part * BLOCK : (part + 1) * BLOCK])
            for copy in range(2):
                xs[copy, 2 * i + part] = piece * half_masks[copy]
        return carry

    lax.fori_loop(0, blocks_d // 2, load, 0)
    for copy in range(2):
        section_pass(pat, w, wt, x, gy, pre, gh, out, copy)

    def act(f, carry):
        hidden, slope = gelu_parts(pre[f])
        hid[f] = hidden.astype(jnp.bfloat16)
        gp[f] = (slope * gh[f]).astype(jnp.bfloat16)
        return carry

    lax.fori_loop(0, blocks_f, act, 0)
    for copy in range(2):
        section_close(pat, w, wt, hid, gp, out, copy, 2)

    def store(i, carry):
        cols = wide_columns(i)
        value = jnp.concatenate([out[2 * i], out[2 * i + 1]], axis=0).astype(jnp.bfloat16).T
        for copy in range(2):
            backward[copy, :, cols] = value[32 * copy : 32 * copy + 32]
            forward[copy, :, cols] = value[64 + 32 * copy : 96 + 32 * copy]
        return carry

    lax.fori_loop(0, blocks_d // 2, store, 0)

    def join(f, carry):
        gp[f] = merged(gp[f], gp1[f], late_half).astype(jnp.bfloat16)
        hid[f] = rearranged(merged(hid[f], hid1[f], late_half).astype(jnp.bfloat16))
        return carry

    lax.fori_loop(0, blocks_f, join, 0)


def two_wide(value):
    return jnp.concatenate([value[: BLOCK // 2], value[BLOCK // 2 :]], axis=1).astype(jnp.bfloat16)


def sum_kernel(
    sections, quarter, pat, xs, gys, hid, gp, total, grads, got_core, to_side, got_side, share, got_own, got_far, wide, *sems
):
    core_sent, core_got, side_sent, side_got, own_sent, own_got, far_sent, far_got = sems
    blocks_d, blocks_f = xs.shape[1], gp.shape[0]
    me, group = lax.axis_index("pipe"), lax.axis_index("dp")
    core, side = lax.rem(group, 2), group // 2
    near, over, far = group + 1 - 2 * core, group + 2 - 4 * side, sections - 1 - me
    barrier = pltpu.get_barrier_semaphore()
    for other in ((near, me), (over, me), (over, far)):
        pl.semaphore_signal(barrier, inc=1, device_id=other, device_id_type=pl.DeviceIdType.MESH)
    pl.semaphore_wait(barrier, 3)
    half = BLOCK // 2

    def compute(j):
        copy, proj = divmod(j, 2)
        for q in range(4):

            def step(i, carry, q=q):
                for u in range(6):
                    n = i * 6 + u
                    d, f = place(pat, copy, proj, q * quarter + n, blocks_d, blocks_f)
                    if proj == 0:
                        value = mul_nt(xs[copy, d], gp[f])
                    else:
                        value = mul_nt(hid[f], gys[copy, d])
                    grads[j, q // 2, q % 2, pl.ds(pl.multiple_of(n * half, half), half)] = two_wide(value)
                return carry

            lax.fori_loop(0, quarter // 6, step, 0)

    def copies(j):
        def remote(source, target, sent, got, to):
            return pltpu.make_async_remote_copy(
                src_ref=source, dst_ref=target, send_sem=sent.at[j], recv_sem=got.at[j],
                device_id=to, device_id_type=pl.DeviceIdType.MESH,
            )

        return (
            remote(grads.at[j, :, 1 - core], got_core.at[j], core_sent, core_got, (near, me)),
            remote(to_side.at[j], got_side.at[j], side_sent, side_got, (over, me)),
            remote(share.at[j], got_far.at[j], far_sent, far_got, (over, far)),
            remote(share.at[j], got_own.at[j], own_sent, own_got, (over, me)),
        )

    wires = [copies(j) for j in range(4)]

    def pieces(body):
        def step(i, carry):
            body(pl.ds(pl.multiple_of(i * 64, 64), 64))
            return carry

        lax.fori_loop(0, quarter * half // 64, step, 0)

    def after_core(j):
        wires[j][0].wait_recv()

        def body(rows):
            value = grads[j, side, core, rows].astype(jnp.float32) + got_core[j, side, rows].astype(jnp.float32)
            to_side[j, rows] = value.astype(jnp.bfloat16)

        pieces(body)
        wires[j][1].start()

    def after_side(j):
        wires[j][1].wait_recv()

        def body(rows):
            value = grads[j, 1 - side, core, rows].astype(jnp.float32) + got_core[j, 1 - side, rows].astype(jnp.float32)
            share[j, rows] = (value + got_side[j, rows].astype(jnp.float32)).astype(jnp.bfloat16)

        pieces(body)
        wires[j][2].start()
        wires[j][3].start()

    def after_far(copy, proj):
        own, other = copy * 2 + proj, (1 - copy) * 2 + proj
        wires[own][3].wait_recv()
        wires[other][2].wait_recv()

        def body(i, carry):
            rows = pl.ds(pl.multiple_of(i * 64, 64), 64)
            value = got_own[own, rows].astype(jnp.float32) + got_far[other, rows].astype(jnp.float32)
            wide[pl.ds(i * 128 + proj, 64, stride=2), :] = value
            return carry

        lax.fori_loop(0, quarter * half // 64, body, 0)

    def finish(copy):
        def body(n, carry):
            for t in range(half):
                total[copy, n, :, t * 128 : (t + 1) * 128] = wide[pl.ds((n * half + t) * 2, 2), :]
            return carry

        lax.fori_loop(0, quarter, body, 0)

    for step in range(6):
        if step < 4:
            compute(step)
            wires[step][0].start()
        if 1 <= step < 5:
            after_core(step - 1)
        if 2 <= step:
            after_side(step - 2)
    for copy in (1, 0):
        for proj in range(2):
            after_far(copy, proj)
        finish(copy)
    for j in range(4):
        for wire in wires[j]:
            wire.wait_send()


def call(kernel, args, outs, scratch):
    smem, vmem = pl.BlockSpec(memory_space=pltpu.SMEM), pl.BlockSpec(memory_space=pltpu.VMEM)
    return pl.pallas_call(
        kernel,
        out_shape=[jax.ShapeDtypeStruct(*out) for out in outs],
        in_specs=[smem] + [vmem] * (len(args) - 1),
        out_specs=[vmem] * len(outs),
        scratch_shapes=[pltpu.VMEM(*one) for one in scratch],
        compiler_params=pltpu.CompilerParams(vmem_limit_bytes=VMEM_BYTES),
    )(*args)


def shards(acts_in, cot_in, stash, entering, pattern, weights, momentum):
    bf16, f32 = jnp.bfloat16, jnp.float32
    me, sections = lax.axis_index("pipe"), lax.axis_size("pipe")
    group = lax.axis_index("dp")
    acts, cot, saved, fresh = (jnp.swapaxes(one, -1, -2) for one in (acts_in[0, 0], cot_in[0, 0], stash[0, 0], entering[0]))
    pat = jnp.stack(
        [
            lax.dynamic_index_in_dim(pattern, me, 0, keepdims=False),
            lax.dynamic_index_in_dim(pattern, sections - 1 - me, 0, keepdims=False),
        ]
    ).reshape(-1)
    tokens, width = acts.shape[1:]
    count = weights.shape[3]
    blocks_d, blocks_f = width // BLOCK, FF // BLOCK
    w = weights[0].reshape(2, 2, count, BLOCK, BLOCK)
    wt = jnp.swapaxes(w, 3, 4)
    d_block, f_block = (blocks_d, BLOCK, 128), (blocks_f, BLOCK, 128)
    send_up, send_down, hid, gp = call(
        first_kernel,
        (pat, acts, cot, saved, w, wt),
        [((2 * tokens, width), bf16), ((2 * tokens, width), bf16), (f_block, bf16), (f_block, bf16)],
        [((2, *d_block), bf16), ((2, *d_block), bf16), (f_block, f32), (f_block, f32), (d_block, f32)],
    )
    got_up = lax.ppermute(send_up, "pipe", [(i, i + 1) for i in range(sections - 1)])
    got_down = lax.ppermute(send_down, "pipe", [(i + 1, i) for i in range(sections - 1)])
    forward, backward, xs, gys, hid, gp = call(
        lambda *refs: second_kernel(sections, *refs),
        (pat, acts, cot, saved, fresh, send_up, send_down, got_up, got_down, hid, gp, w, wt),
        [(acts.shape, bf16)] * 2 + [((2, *d_block), bf16)] * 2 + [(f_block, bf16)] * 2,
        [((2, *d_block), bf16)] * 2 + [(f_block, f32)] * 2 + [(d_block, f32)],
    )
    quarter = count // 4
    chunk = (4, quarter * BLOCK // 2, 128)
    smem, vmem = pl.BlockSpec(memory_space=pltpu.SMEM), pl.BlockSpec(memory_space=pltpu.VMEM)
    total = pl.pallas_call(
        lambda *refs: sum_kernel(sections, quarter, *refs),
        out_shape=jax.ShapeDtypeStruct((2, quarter, 2, weights.shape[4]), f32),
        in_specs=[smem] + [vmem] * 4,
        out_specs=vmem,
        scratch_shapes=[
            pltpu.VMEM((4, 2, 2, *chunk[1:]), bf16),
            pltpu.VMEM((4, 2, *chunk[1:]), bf16),
            pltpu.VMEM(chunk, bf16),
            pltpu.VMEM(chunk, bf16),
            pltpu.VMEM(chunk, bf16),
            pltpu.VMEM(chunk, bf16),
            pltpu.VMEM(chunk, bf16),
            pltpu.VMEM((2 * chunk[1], 128), f32),
        ]
        + [pltpu.SemaphoreType.DMA((4,))] * 8,
        compiler_params=pltpu.CompilerParams(collective_id=0, has_side_effects=True, vmem_limit_bytes=VMEM_BYTES),
    )(pat, xs, gys, hid, gp)
    total = jnp.swapaxes(total, 1, 2)
    momentum_next = BETA * momentum[0] + total / (2 * tokens)
    own = lax.dynamic_slice_in_dim(weights[0], group * quarter, quarter, axis=2)
    weights_next = (own.astype(f32) - STEP * momentum_next).astype(bf16)
    forward, backward = jnp.swapaxes(forward, 1, 2), jnp.swapaxes(backward, 1, 2)
    return forward[None, None], backward[None, None], weights_next[None], momentum_next[None]


def solution(mesh):
    placed = (
        P("dp", "pipe"),
        P("dp", "pipe"),
        P("dp", "pipe"),
        P("dp"),
        P(),
        P("pipe"),
        P("pipe", None, None, "dp"),
    )
    return jax.shard_map(
        shards,
        mesh=mesh,
        in_specs=placed,
        out_specs=(P("dp", "pipe"), P("dp", "pipe"), P("pipe", None, None, "dp"), P("pipe", None, None, "dp")),
        check_vma=False,
    )
```

time: 177 us -> 154 us (0.87); the launches traced: 173 us -> 152 us
  local copies, waits for them, and re-layouts: 29.3 us -> 17.8 us
  Pallas kernels: 127 us -> 116 us
  other arithmetic: 2.41 us -> 4.24 us
    unnamed x20 -> x6, local copies, waits for them, and re-layouts: 15.2 us -> 0.68 us
    pallas_call x2, Pallas kernels: 75.5 us -> 66.7 us  [call(): pl.pallas_call(kernel, out_shape=[jax.ShapeDtypeStruct(*out) for out in o...]
    pallas_call x1, Pallas kernels: 51.8 us -> 49.7 us  [shards(): pl.pallas_call(lambda *refs: sum_kernel(sections, quarter, *refs), out_sh...]
    broadcast_in_dim x1, other arithmetic: 2.4 us -> 4.23 us  [shards(): momentum_next[None]]
where the time goes in v3:
time: 154 us; the launch traced here: 152 us
  Pallas kernels  116 us (75%)
  local copies, waits for them, and re-layouts  17.8 us (12%)
  starting transfers between devices  6.95 us (5%)
  waiting for transfers between devices  6.3 us (4%)
  other arithmetic  4.24 us (3%)
    pallas_call x2, Pallas kernels, call(): pl.pallas_call(kernel, out_shape=[jax.ShapeDtypeStruct(*out) for out in o...  66.7 us
    pallas_call x1, Pallas kernels, shards(): pl.pallas_call(lambda *refs: sum_kernel(sections, quarter, *refs), out_sh...  49.7 us
    another operation x2, local copies, waits for them, and re-layouts, shards(): w = weights[0].reshape(2, 2, count, BLOCK, BLOCK)  14.3 us
    ppermute x1, starting transfers between devices, shards(): lax.ppermute(send_up, 'pipe', [(i, i + 1) for i in range(sections - 1)])  5.66 us
    ppermute x1, waiting for transfers between devices, shards(): lax.ppermute(send_down, 'pipe', [(i + 1, i) for i in range(sections - 1)])  5.2 us
    broadcast_in_dim x1, other arithmetic, shards(): momentum_next[None]  4.23 us
  transfers between devices with their start and end apart: 2, of which 2 were waited for; matrix products, arithmetic and copies ran while one was open for 1% of the time, Pallas kernels for 0%

profile of v3, /device:TPU:1, one launch (start us, length us, event | category | flops | bytes accessed | tf_op | source)
XLA Modules:
  0.0 152.4 jit_solution(15801312534020451383)
XLA Ops:
  0.6 0.7 constant_dynamic-slice_fusion.2
  1.3 0.7 reshape.16.pat.refs_0_
  2.0 7.6 %reshape_squeeze.3.w.refs_11_ = bf16[2,2,72,64,64]{4,3,2,1,0:T(8,128)(2,1)} reshape(bf16[1,2,2,72,4096]{4,3,2,1,0:T(8,128)(2,1)} %param.12) | data formatting | bytes 4718592 | tf_op jit(solution)/shard_map/reshape;squeeze | solution.py:391
  9.6 6.7 %copy.14 = bf16[2,2,72,64,64]{3,4,2,1,0:T(8,128)(2,1)} copy(bf16[2,2,72,64,64]{4,3,2,1,0:T(8,128)(2,1)} %reshape_squeeze.3.w.refs_11_) | data formatting | bytes 4718592 | tf_op jit(solution)/shard_map/reshape;squeeze | solution.py:391
  16.3 25.2 %shard_map.102 = (bf16[64,1536]{1,0:T(8,128)(2,1)}, bf16[64,1536]{1,0:T(8,128)(2,1)}, bf16[96,64,128]{2,1,0:T(8,128)(2,1)}, bf16[96,64,128]{2,1,0:T(8,128)(2,1)}) custom-call(s32[288]{0:T(512)} %reshape.16.pat.refs_0_, bf16[2,32,1536]{2,1,0:T(8,128)(2,1)} %bitcast.46, bf16[2,32,1536]{2,1,0:T(8,128)(2,1)} %bitcast.48, bf16[2,2,32,1536]{3,2,1,0:T(8,128)(2,1)} %bitcast.44, ...), custom_call_target="tpu_custom_call" | custom-call | tf_op jit(solution)/shard_map/pallas_call | solution.py:367
  41.5 5.7 %collective-permute-start = (bf16[64,1536]{1,0:T(8,128)(2,1)}, bf16[64,1536]{1,0:T(8,128)(2,1)S(1)}, u32[]{:S(2)}, u32[]{:S(2)}) collective-permute-start(bf16[64,1536]{1,0:T(8,128)(2,1)} %get-tuple-element.14.refs_5_), channel_id=1, source_target_pairs={{0,1},{1,2},{2,3},{3,4},{4,5},{5,6},{6,7},{7,8},{8,9},{9,10},{10,1... | collective-permute-start | bytes 589832 | tf_op jit(solution)/shard_map/ppermute | solution.py:400
  47.2 1.3 collective-permute-start.1
  48.5 1.4 constant_dynamic-slice_fusion
  49.9 1.1 collective-permute-done.refs_7_
  51.0 0.0 copy-start.1
  51.0 5.2 %collective-permute-done.1.refs_8_ = bf16[64,1536]{1,0:T(8,128)(2,1)S(1)} collective-permute-done((bf16[64,1536]{1,0:T(8,128)(2,1)}, bf16[64,1536]{1,0:T(8,128)(2,1)S(1)}, u32[]{:S(2)}, u32[]{:S(2)}) %collective-permute-start.1) | collective-permute-done | bytes 196640 | tf_op jit(solution)/shard_map/ppermute | solution.py:401
  56.2 0.0 copy-start.2
  56.2 0.0 copy-done.1
  56.2 0.7 copy-done.2
  56.9 41.5 %shard_map.103 = (bf16[2,32,1536]{2,1,0:T(8,128)(2,1)}, bf16[2,32,1536]{2,1,0:T(8,128)(2,1)}, bf16[2,24,64,128]{3,2,1,0:T(8,128)(2,1)}, bf16[2,24,64,128]{3,2,1,...) custom-call(s32[288]{0:T(512)} %reshape.16.pat.refs_0_, bf16[2,32,1536]{2,1,0:T(8,128)(2,1)} %bitcast.47, ...), custom_call_target="tpu_custom_call" | custom-call | tf_op jit(solution)/shard_map/pallas_call | solution.py:367
  98.4 0.0 copy-start
  98.4 49.7 %shard_map.104 = f32[2,18,2,4096]{3,2,1,0:T(2,128)} custom-call(s32[288]{0:T(512)} %reshape.16.pat.refs_0_, bf16[2,24,64,128]{3,2,1,0:T(8,128)(2,1)} %get-tuple-element.20.refs_1_, bf16[2,24,64,128]{3,2,1,0:T(8,128)(2,1)} %get-tuple-element.21.refs_2_, bf16[96,64,128]{2,1,0:T(8,128)(2,1)} %get-tuple-element.22.refs_3_, ...), custom_call_target="tpu_custom_call" | custom-call | tf_op jit(solution)/shard_map/pallas_call | solution.py:411
  148.1 0.0 copy-done
  148.1 4.2 %fusion.2 = (f32[1,2,2,18,4096]{4,2,3,1,0:T(2,128)}, bf16[1,2,2,18,4096]{4,2,3,1,0:T(2,128)(2,1)}) fusion(f32[2,18,2,4096]{3,2,1,0:T(2,128)} %shard_map.104, f32[1,2,2,18,4096]{4,2,3,1,0:T(2,128)S(1)} %copy-done, bf16[1,2,2,18,4096]{4,3,2,1,0:T(8,128)(2,1)S(1)} %constant_dynamic-slice_fusion), kind=kLoop, calls=%fused_computation.9 | loop fusion | flops 2064384 | bytes 4718592 | tf_op jit(solution)/shard_map/broadcast_in_dim | solution.py:434
  (1 shorter events, 0.0 us)
Async XLA Ops:
  41.5 9.5 %collective-permute-start = (bf16[64,1536]{1,0:T(8,128)(2,1)}, bf16[64,1536]{1,0:T(8,128)(2,1)S(1)}, u32[]{:S(2)}, u32[]{:S(2)}) collective-permute-start(bf16[64,1536]{1,0:T(8,128)(2,1)} %get-tuple-element.14.refs_5_), channel_id=1, source_target_pairs={{0,1},{1,2},{2,3},{3,4},{4,5},{5,6},{6,7},{7,8},{8,9},{9,10},{10,1... | collective-permute-start | bytes 589832 | tf_op jit(solution)/shard_map/ppermute | solution.py:400
  47.2 9.1 %collective-permute-start.1 = (bf16[64,1536]{1,0:T(8,128)(2,1)}, bf16[64,1536]{1,0:T(8,128)(2,1)S(1)}, u32[]{:S(2)}, u32[]{:S(2)}) collective-permute-start(bf16[64,1536]{1,0:T(8,128)(2,1)} %get-tuple-element.15.refs_6_), channel_id=1, source_target_pairs={{1,0},{2,1},{3,2},{4,3},{5,4},{6,5},{7,6},{8,7},{9,8},{10,9},{11,1... | collective-permute-start | bytes 589832 | tf_op jit(solution)/shard_map/ppermute | solution.py:401
  51.0 5.2 %copy-start.1 = (bf16[64,1536]{1,0:T(8,128)(2,1)}, bf16[64,1536]{1,0:T(8,128)(2,1)S(1)}, u32[]{:S(2)}) copy-start(bf16[64,1536]{1,0:T(8,128)(2,1)S(1)} %collective-permute-done.refs_7_) | copy-start | bytes 589828
  56.2 0.7 copy-start.2
  98.4 49.7 %copy-start = (f32[1,2,2,18,4096]{4,2,3,1,0:T(2,128)S(1)}, f32[1,2,2,18,4096]{4,2,3,1,0:T(2,128)}, u32[]{:S(2)}) copy-start(f32[1,2,2,18,4096]{4,2,3,1,0:T(2,128)} %param.13) | copy-start | bytes 3538948

commit v4 on v3

--- a/solution.py
+++ b/solution.py
@@ -9,7 +9,9 @@
 BLOCK = 64
 BETA = 0.9
 STEP = 0.2
-UNROLL = 8
+PER = 6
+ACTS = 2
+SLOTS = 96
 VMEM_BYTES = 56 * 2**20
 
 
@@ -58,75 +60,161 @@
     return value - r * blocks_d, r
 
 
-def each_block(count, body):
+def entry(lists, which, i):
+    value = lists[which * SLOTS + i]
+    return value % 128, (value // 128) % 32, value // 4096
+
+
+def batched(trips, width, body):
     def step(i, carry):
-        body([i * UNROLL + u for u in range(UNROLL)])
-        return carry
-
-    lax.fori_loop(0, count // UNROLL, step, 0)
-
-
-def section_pass(pat, w, wt, x, gy, pre, gh, out, copy):
-    blocks_d, blocks_f, count = x.shape[1], pre.shape[0], w.shape[2]
-
-    def up(ns):
+        body(i * width)
+        return carry
+
+    lax.fori_loop(0, trips, step, 0)
+
+
+def build_lists(pat, lists, flags, count, blocks_d, blocks_f):
+    dummy = blocks_d * 128 + blocks_f * 4096
+
+    def wipe(i, carry):
+        for u in range(8):
+            flags[i * 8 + u] = 0
+        return carry
+
+    lax.fori_loop(0, 2 * blocks_f // 8, wipe, 0)
+
+    def fill(i, carry):
+        for which in range(4):
+            lists[which * SLOTS + i] = dummy
+        lists[4 * SLOTS + i] = blocks_f
+        return carry
+
+    lax.fori_loop(0, SLOTS, fill, 0)
+
+    def mark(n, carry):
+        for copy in range(2):
+            _, f = place(pat, copy, 0, n, blocks_d, blocks_f)
+            flags[copy * blocks_f + f] = 1
+        return carry
+
+    lax.fori_loop(0, count, mark, 0)
+
+    def mark_both(n, carry):
+        for copy in range(2):
+            _, f = place(pat, copy, 1, n, blocks_d, blocks_f)
+            at = copy * blocks_f + f
+            flags[at] = jnp.where(flags[at] > 0, 2, 0)
+        return carry
+
+    lax.fori_loop(0, count, mark_both, 0)
+
+    def collect(n, found):
+        after = []
+        for which in range(4):
+            copy, proj = divmod(which, 2)
+            d, f = place(pat, copy, proj, n, blocks_d, blocks_f)
+            active = flags[copy * blocks_f + f] == 2
+            at = which * SLOTS + found[which]
+            lists[at] = jnp.where(active, n + d * 128 + f * 4096, dummy)
+            after.append(found[which] + jnp.where(active, 1, 0))
+        return tuple(after)
+
+    zero = jnp.int32(0)
+    found = lax.fori_loop(0, count, collect, (zero,) * 4)
+
+    def gather(f, number):
+        active = jnp.maximum(flags[f], flags[blocks_f + f]) == 2
+        lists[4 * SLOTS + number] = jnp.where(active, f, blocks_f)
+        return number + jnp.where(active, 1, 0)
+
+    number = lax.fori_loop(0, blocks_f, gather, zero)
+    most = jnp.maximum(jnp.maximum(found[0], found[1]), jnp.maximum(found[2], found[3]))
+    lists[5 * SLOTS] = (most + PER - 1) // PER
+    lists[5 * SLOTS + 1] = (number + ACTS - 1) // ACTS
+
+
+def prepare_weights(lists, raw, wide, w):
+    count, half = raw.shape[2], BLOCK // 2
+
+    def spread(t, carry):
+        for which in range(4):
+            copy, proj = divmod(which, 2)
+            value = raw[copy, proj, :, pl.ds(pl.multiple_of(t * 128, 128), 128)].astype(jnp.float32)
+            wide[which, pl.ds(t, count, stride=half), :] = value
+        return carry
+
+    lax.fori_loop(0, half, spread, 0)
+    row = lax.broadcasted_iota(jnp.int32, (BLOCK, BLOCK), 0)
+    col = lax.broadcasted_iota(jnp.int32, (BLOCK, BLOCK), 1)
+    back = (row == jnp.where(col < half, 2 * col, 2 * col - BLOCK + 1)).astype(jnp.float32).astype(jnp.bfloat16)
+    eye = (row == col).astype(jnp.float32).astype(jnp.bfloat16)
+
+    def body(i):
+        done = []
+        for which in range(4):
+            for u in range(3):
+                n = entry(lists, which, i + u)[0]
+                value = wide[which, pl.ds(pl.multiple_of(n * half, half), half), :]
+                split = jnp.concatenate([value[:, :BLOCK], value[:, BLOCK:]], axis=0).astype(jnp.bfloat16)
+                done.append((which, n, mul(back, split).astype(jnp.bfloat16)))
+        for which, n, block in done:
+            w[0, which // 2, which % 2, n] = block
+            w[1, which // 2, which % 2, n] = mul_nt(eye, block).astype(jnp.bfloat16)
+
+    batched(lists[5 * SLOTS] * (PER // 3), 3, body)
+
+
+def section_pass(lists, w, x, gy, pre, gh):
+    def body(i):
         terms = []
-        for n in ns:
-            d, f = place(pat, copy, 0, n, blocks_d, blocks_f)
-            terms.append((f, mul(wt[copy, 0, n], x[copy, d])))
-        for f, term in terms:
-            pre[f] += term
-
-    def down(ns):
+        for copy in range(2):
+            for u in range(PER):
+                n, d, f = entry(lists, 2 * copy, i + u)
+                terms.append((pre, f, mul(w[1, copy, 0, n], x[copy, d])))
+                n, d, f = entry(lists, 2 * copy + 1, i + u)
+                terms.append((gh, f, mul(w[0, copy, 1, n], gy[copy, d])))
+        for ref, f, term in terms:
+            ref[f] += term
+
+    batched(lists[5 * SLOTS], PER, body)
+
+
+def section_close(lists, w, hid, gp, out, first_fwd, first_bwd):
+    lane = lax.broadcasted_iota(jnp.int32, (BLOCK, 128), 1) // 32
+    fwd = [(lane == first_fwd + copy).astype(jnp.float32).astype(jnp.bfloat16) for copy in range(2)]
+    bwd = [(lane == first_bwd + copy).astype(jnp.float32).astype(jnp.bfloat16) for copy in range(2)]
+
+    def body(i):
         terms = []
-        for n in ns:
-            d, f = place(pat, copy, 1, n, blocks_d, blocks_f)
-            terms.append((f, mul(w[copy, 1, n], gy[copy, d])))
-        for f, term in terms:
-            gh[f] += term
-
-    each_block(count, up)
-    each_block(count, down)
-
-
-def section_close(pat, w, wt, hid, gp, out, copy, fwd_lanes):
-    blocks_d, blocks_f, count = out.shape[0], hid.shape[0], w.shape[2]
-    lane = lax.broadcasted_iota(jnp.int32, (BLOCK, 128), 1) // 32
-    fwd = (lane == fwd_lanes + copy).astype(jnp.float32).astype(jnp.bfloat16)
-    own = (lane % 2 == copy).astype(jnp.float32).astype(jnp.bfloat16)
-
-    def down(ns):
-        terms = []
-        for n in ns:
-            d, f = place(pat, copy, 1, n, blocks_d, blocks_f)
-            terms.append((d, mul(wt[copy, 1, n], hid[f] * fwd)))
+        for copy in range(2):
+            for u in range(PER):
+                n, d, f = entry(lists, 2 * copy + 1, i + u)
+                terms.append((d, mul(w[1, copy, 1, n], hid[f] * fwd[copy])))
+                n, d, f = entry(lists, 2 * copy, i + u)
+                terms.append((d, mul(w[0, copy, 0, n], gp[f] * bwd[copy])))
         for d, term in terms:
             out[d] += term
 
-    def up(ns):
-        terms = []
-        for n in ns:
-            d, f = place(pat, copy, 0, n, blocks_d, blocks_f)
-            terms.append((d, mul(w[copy, 0, n], gp[f] * own)))
-        for d, term in terms:
-            out[d] += term
-
-    each_block(count, down)
-    each_block(count, up)
-
-
-def clear(ref):
-    def step(i, carry):
-        ref[i] = jnp.zeros(ref.shape[1:], ref.dtype)
-        return carry
-
-    lax.fori_loop(0, ref.shape[0], step, 0)
-
-
-def first_kernel(pat, acts, cot, stash, w, wt, send_up, send_down, hid, gp, x, gy, pre, gh, out):
-    blocks_d, blocks_f = out.shape[0], pre.shape[0]
-    clear(pre)
-    clear(gh)
+    batched(lists[5 * SLOTS], PER, body)
+
+
+def clear(lists, refs):
+    def body(i):
+        for u in range(ACTS):
+            f = lists[4 * SLOTS + i + u]
+            for ref in refs:
+                ref[f] = jnp.zeros(ref.shape[1:], ref.dtype)
+
+    batched(lists[5 * SLOTS + 1], ACTS, body)
+
+
+def first_kernel(pat, acts, cot, stash, raw, send_up, send_down, hid, gp, lists, w_out, flags, wide, w, x, gy, pre, gh, out, sem):
+    blocks_d, blocks_f = out.shape[0] - 1, pre.shape[0] - 1
+    build_lists(pat, lists, flags, raw.shape[2], blocks_d, blocks_f)
+    prepare_weights(lists, raw, wide, w)
+    keep = pltpu.make_async_copy(w, w_out, sem)
+    keep.start()
+    clear(lists, (pre, gh))
     masks = [copy_mask(copy, 128) for copy in range(2)]
     backward = lax.broadcasted_iota(jnp.int32, (128, 128), 1) >= 64
 
@@ -142,18 +230,17 @@
         return carry
 
     lax.fori_loop(0, blocks_d // 2, load, 0)
-    for copy in range(2):
-        section_pass(pat, w, wt, x, gy, pre, gh, out, copy)
-
-    def act(f, carry):
-        hidden, slope = gelu_parts(pre[f])
-        hid[f] = hidden.astype(jnp.bfloat16)
-        gp[f] = (slope * gh[f]).astype(jnp.bfloat16)
-        return carry
-
-    lax.fori_loop(0, blocks_f, act, 0)
-    for copy in range(2):
-        section_close(pat, w, wt, hid, gp, out, copy, 0)
+    section_pass(lists, w, x, gy, pre, gh)
+
+    def act(i):
+        for u in range(ACTS):
+            f = lists[4 * SLOTS + i + u]
+            hidden, slope = gelu_parts(pre[f])
+            hid[f] = hidden.astype(jnp.bfloat16)
+            gp[f] = (slope * gh[f]).astype(jnp.bfloat16)
+
+    batched(lists[5 * SLOTS + 1], ACTS, act)
+    section_close(lists, w, hid, gp, out, 0, 2)
 
     def store(i, carry):
         cols = wide_columns(i)
@@ -164,17 +251,26 @@
         return carry
 
     lax.fori_loop(0, blocks_d // 2, store, 0)
+    keep.wait()
 
 
 def second_kernel(
-    sections, pat, acts, cot, stash, entering, sent_up, sent_down, got_up, got_down, hid1, gp1, w, wt,
-    forward, backward, xs, gys, hid, gp, x, gy, pre, gh, out,
+    sections, lists, acts, cot, stash, entering, sent_up, sent_down, got_up, got_down, hid1, gp1, w_in,
+    forward, backward, xs, gys, hid_both, gp_both, w, hid, x, gy, pre, gh, out, sem,
 ):
-    blocks_d, blocks_f = out.shape[0], pre.shape[0]
+    fetch = pltpu.make_async_copy(w_in, w, sem)
+    fetch.start()
+    blocks_d, blocks_f = out.shape[0] - 1, pre.shape[0] - 1
     me = lax.axis_index("pipe")
     at_entry, at_exit = me == 0, me == sections - 1
-    clear(pre)
-    clear(gh)
+    clear(lists, (pre, gh))
+
+    def wipe(f, carry):
+        hid_both[f] = jnp.zeros(hid_both.shape[1:], hid_both.dtype)
+        gp_both[f] = jnp.zeros(gp_both.shape[1:], gp_both.dtype)
+        return carry
+
+    lax.fori_loop(0, blocks_f, wipe, 0, unroll=4)
     row = lax.broadcasted_iota(jnp.int32, (BLOCK, BLOCK), 0)
     col = lax.broadcasted_iota(jnp.int32, (BLOCK, BLOCK), 1)
     source = jnp.where(row < BLOCK // 2, 2 * row, 2 * row - BLOCK + 1)
@@ -214,18 +310,19 @@
         return carry
 
     lax.fori_loop(0, blocks_d // 2, load, 0)
-    for copy in range(2):
-        section_pass(pat, w, wt, x, gy, pre, gh, out, copy)
-
-    def act(f, carry):
-        hidden, slope = gelu_parts(pre[f])
-        hid[f] = hidden.astype(jnp.bfloat16)
-        gp[f] = (slope * gh[f]).astype(jnp.bfloat16)
-        return carry
-
-    lax.fori_loop(0, blocks_f, act, 0)
-    for copy in range(2):
-        section_close(pat, w, wt, hid, gp, out, copy, 2)
+    fetch.wait()
+    section_pass(lists, w, x, gy, pre, gh)
+
+    def act(i):
+        for u in range(ACTS):
+            f = lists[4 * SLOTS + i + u]
+            hidden, slope = gelu_parts(pre[f])
+            hid[f] = hidden.astype(jnp.bfloat16)
+            gp_both[f] = merged(slope * gh[f], gp1[f], late_half).astype(jnp.bfloat16)
+            hid_both[f] = rearranged(merged(hidden, hid1[f], late_half).astype(jnp.bfloat16))
+
+    batched(lists[5 * SLOTS + 1], ACTS, act)
+    section_close(lists, w, hid, gp_both, out, 2, 0)
 
     def store(i, carry):
         cols = wide_columns(i)
@@ -236,13 +333,6 @@
         return carry
 
     lax.fori_loop(0, blocks_d // 2, store, 0)
-
-    def join(f, carry):
-        gp[f] = merged(gp[f], gp1[f], late_half).astype(jnp.bfloat16)
-        hid[f] = rearranged(merged(hid[f], hid1[f], late_half).astype(jnp.bfloat16))
-        return carry
-
-    lax.fori_loop(0, blocks_f, join, 0)
 
 
 def two_wide(value):
@@ -253,7 +343,7 @@
     sections, quarter, pat, xs, gys, hid, gp, total, grads, got_core, to_side, got_side, share, got_own, got_far, wide, *sems
 ):
     core_sent, core_got, side_sent, side_got, own_sent, own_got, far_sent, far_got = sems
-    blocks_d, blocks_f = xs.shape[1], gp.shape[0]
+    blocks_d, blocks_f = xs.shape[1], gp.shape[0] - 1
     me, group = lax.axis_index("pipe"), lax.axis_index("dp")
     core, side = lax.rem(group, 2), group // 2
     near, over, far = group + 1 - 2 * core, group + 2 - 4 * side, sections - 1 - me
@@ -268,8 +358,8 @@
         for q in range(4):
 
             def step(i, carry, q=q):
-                for u in range(6):
-                    n = i * 6 + u
+                for u in range(9):
+                    n = i * 9 + u
                     d, f = place(pat, copy, proj, q * quarter + n, blocks_d, blocks_f)
                     if proj == 0:
                         value = mul_nt(xs[copy, d], gp[f])
@@ -278,7 +368,7 @@
                     grads[j, q // 2, q % 2, pl.ds(pl.multiple_of(n * half, half), half)] = two_wide(value)
                 return carry
 
-            lax.fori_loop(0, quarter // 6, step, 0)
+            lax.fori_loop(0, quarter // 9, step, 0)
 
     def copies(j):
         def remote(source, target, sent, got, to):
@@ -363,15 +453,15 @@
 
 
 def call(kernel, args, outs, scratch):
-    smem, vmem = pl.BlockSpec(memory_space=pltpu.SMEM), pl.BlockSpec(memory_space=pltpu.VMEM)
+    space = {"s": pltpu.SMEM, "v": pltpu.VMEM, "a": pl.ANY}
     return pl.pallas_call(
         kernel,
-        out_shape=[jax.ShapeDtypeStruct(*out) for out in outs],
-        in_specs=[smem] + [vmem] * (len(args) - 1),
-        out_specs=[vmem] * len(outs),
-        scratch_shapes=[pltpu.VMEM(*one) for one in scratch],
+        out_shape=[jax.ShapeDtypeStruct(*out[1:]) for out in outs],
+        in_specs=[pl.BlockSpec(memory_space=space[kind]) for kind, _ in args],
+        out_specs=[pl.BlockSpec(memory_space=space[out[0]]) for out in outs],
+        scratch_shapes=[space[one[0]](*one[1:]) for one in scratch] + [pltpu.SemaphoreType.DMA],
         compiler_params=pltpu.CompilerParams(vmem_limit_bytes=VMEM_BYTES),
-    )(*args)
+    )(*(value for _, value in args))
 
 
 def shards(acts_in, cot_in, stash, entering, pattern, weights, momentum):
@@ -388,22 +478,48 @@
     tokens, width = acts.shape[1:]
     count = weights.shape[3]
     blocks_d, blocks_f = width // BLOCK, FF // BLOCK
-    w = weights[0].reshape(2, 2, count, BLOCK, BLOCK)
-    wt = jnp.swapaxes(w, 3, 4)
-    d_block, f_block = (blocks_d, BLOCK, 128), (blocks_f, BLOCK, 128)
-    send_up, send_down, hid, gp = call(
+    raw = weights[0]
+    d_block, f_block = (blocks_d, BLOCK, 128), (blocks_f + 1, BLOCK, 128)
+    x_block, out_block = (2, blocks_d + 1, BLOCK, 128), (blocks_d + 1, BLOCK, 128)
+    w_shape = (2, 2, 2, count, BLOCK, BLOCK)
+    send_up, send_down, hid, gp, lists, w = call(
         first_kernel,
-        (pat, acts, cot, saved, w, wt),
-        [((2 * tokens, width), bf16), ((2 * tokens, width), bf16), (f_block, bf16), (f_block, bf16)],
-        [((2, *d_block), bf16), ((2, *d_block), bf16), (f_block, f32), (f_block, f32), (d_block, f32)],
+        [("s", pat), ("v", acts), ("v", cot), ("v", saved), ("v", raw)],
+        [
+            ("v", (2 * tokens, width), bf16),
+            ("v", (2 * tokens, width), bf16),
+            ("v", f_block, bf16),
+            ("v", f_block, bf16),
+            ("s", (5 * SLOTS + 8,), jnp.int32),
+            ("a", w_shape, bf16),
+        ],
+        [
+            ("s", (2 * blocks_f,), jnp.int32),
+            ("v", (4, count * BLOCK // 2, 128), f32),
+            ("v", w_shape, bf16),
+            ("v", x_block, bf16),
+            ("v", x_block, bf16),
+            ("v", f_block, f32),
+            ("v", f_block, f32),
+            ("v", out_block, f32),
+        ],
     )
     got_up = lax.ppermute(send_up, "pipe", [(i, i + 1) for i in range(sections - 1)])
     got_down = lax.ppermute(send_down, "pipe", [(i + 1, i) for i in range(sections - 1)])
+    vectors = (acts, cot, saved, fresh, send_up, send_down, got_up, got_down, hid, gp)
     forward, backward, xs, gys, hid, gp = call(
         lambda *refs: second_kernel(sections, *refs),
-        (pat, acts, cot, saved, fresh, send_up, send_down, got_up, got_down, hid, gp, w, wt),
-        [(acts.shape, bf16)] * 2 + [((2, *d_block), bf16)] * 2 + [(f_block, bf16)] * 2,
-        [((2, *d_block), bf16)] * 2 + [(f_block, f32)] * 2 + [(d_block, f32)],
+        [("s", lists)] + [("v", one) for one in vectors] + [("a", w)],
+        [("v", acts.shape, bf16)] * 2 + [("v", (2, *d_block), bf16)] * 2 + [("v", f_block, bf16)] * 2,
+        [
+            ("v", w_shape, bf16),
+            ("v", f_block, bf16),
+            ("v", x_block, bf16),
+            ("v", x_block, bf16),
+            ("v", f_block, f32),
+            ("v", f_block, f32),
+            ("v", out_block, f32),
+        ],
     )
     quarter = count // 4
     chunk = (4, quarter * BLOCK // 2, 128)

time: 154 us -> 127 us (0.82)
  local copies, waits for them, and re-layouts: 17.8 us -> 3.5 us
  Pallas kernels: 116 us -> 109 us
  starting transfers between devices: 6.95 us -> 3.18 us
    another operation x2 -> x0, local copies, waits for them, and re-layouts: 14.3 us -> none  [shards(): w = weights[0].reshape(2, 2, count, BLOCK, BLOCK)]
    pallas_call x2, Pallas kernels: 66.7 us -> 57.7 us  [call(): pl.pallas_call(kernel, out_shape=[jax.ShapeDtypeStruct(*out[1:]) for out...]
    ppermute x1, starting transfers between devices: 5.66 us -> 1.89 us  [shards(): lax.ppermute(send_up, 'pipe', [(i, i + 1) for i in range(sections - 1)])]
    pallas_call x1, Pallas kernels: 49.7 us -> 51.7 us  [shards(): pl.pallas_call(lambda *refs: sum_kernel(sections, quarter, *refs), out_sh...]
where the time goes in v4:
time: 127 us; the launch traced here: 126 us
  Pallas kernels  109 us (86%)
  waiting for transfers between devices  5.44 us (4%)
  other arithmetic  4.24 us (3%)
  local copies, waits for them, and re-layouts  3.5 us (3%)
  starting transfers between devices  3.18 us (3%)
    pallas_call x2, Pallas kernels, call(): pl.pallas_call(kernel, out_shape=[jax.ShapeDtypeStruct(*out[1:]) for out...  57.7 us
    pallas_call x1, Pallas kernels, shards(): pl.pallas_call(lambda *refs: sum_kernel(sections, quarter, *refs), out_sh...  51.7 us
    ppermute x1, waiting for transfers between devices, shards(): lax.ppermute(send_down, 'pipe', [(i + 1, i) for i in range(sections - 1)])  5.3 us
    broadcast_in_dim x1, other arithmetic, shards(): momentum_next[None]  4.23 us
  transfers between devices with their start and end apart: 2, of which 2 were waited for; matrix products, arithmetic and copies ran while one was open for 1% of the time, Pallas kernels for 0%

profile of v4, /device:TPU:1, one launch (start us, length us, event | category | flops | bytes accessed | tf_op | source)
XLA Modules:
  0.0 126.4 jit_solution(458030974341169451)
XLA Ops:
  0.6 0.7 constant_dynamic-slice_fusion.2
  1.3 0.7 reshape.16.pat.refs_0_
  2.0 36.5 %shard_map.102 = (bf16[64,1536]{1,0:T(8,128)(2,1)}, bf16[64,1536]{1,0:T(8,128)(2,1)}, bf16[97,64,128]{2,1,0:T(8,128)(2,1)}, bf16[97,64,128]{2,1,0:T(8,128)(2,1)}...) custom-call(s32[288]{0:T(512)} %reshape.16.pat.refs_0_, bf16[2,32,1536]{2,1,0:T(8,128)(2,1)} %bitcast.43, ...), custom_call_target="tpu_custom_call" | custom-call | tf_op jit(solution)/shard_map/pallas_call | solution.py:457
  38.6 1.9 %collective-permute-start = (bf16[64,1536]{1,0:T(8,128)(2,1)}, bf16[64,1536]{1,0:T(8,128)(2,1)S(1)}, u32[]{:S(2)}, u32[]{:S(2)}) collective-permute-start(bf16[64,1536]{1,0:T(8,128)(2,1)} %get-tuple-element.17.refs_5_), channel_id=1, source_target_pairs={{0,1},{1,2},{2,3},{3,4},{4,5},{5,6},{6,7},{7,8},{8,9},{9,10},{10,1... | collective-permute-start | bytes 589832 | tf_op jit(solution)/shard_map/ppermute | solution.py:507
  40.5 1.3 %collective-permute-start.1 = (bf16[64,1536]{1,0:T(8,128)(2,1)}, bf16[64,1536]{1,0:T(8,128)(2,1)S(1)}, u32[]{:S(2)}, u32[]{:S(2)}) collective-permute-start(bf16[64,1536]{1,0:T(8,128)(2,1)} %get-tuple-element.18.refs_6_), channel_id=1, source_target_pairs={{1,0},{2,1},{3,2},{4,3},{5,4},{6,5},{7,6},{8,7},{9,8},{10,9},{11,1... | collective-permute-start | bytes 589832 | tf_op jit(solution)/shard_map/ppermute | solution.py:508
  41.8 1.4 %constant_dynamic-slice_fusion = bf16[1,2,2,18,4096]{4,3,2,1,0:T(8,128)(2,1)S(1)} fusion(bf16[1,2,2,72,4096]{4,3,2,1,0:T(8,128)(2,1)} %param.12, s32[]{:T(128)S(6)} %select_n.12), kind=kLoop, calls=%fused_computation.6 | loop fusion | bytes 1179652 | tf_op jit(solution)/shard_map/dynamic_slice | solution.py:547
  43.2 0.1 collective-permute-done.refs_7_
  43.4 0.0 copy-start.1
  43.4 5.3 %collective-permute-done.1.refs_8_ = bf16[64,1536]{1,0:T(8,128)(2,1)S(1)} collective-permute-done((bf16[64,1536]{1,0:T(8,128)(2,1)}, bf16[64,1536]{1,0:T(8,128)(2,1)S(1)}, u32[]{:S(2)}, u32[]{:S(2)}) %collective-permute-start.1) | collective-permute-done | bytes 196640 | tf_op jit(solution)/shard_map/ppermute | solution.py:508
  48.7 0.0 copy-start.2
  48.7 0.0 copy-done.1
  48.7 0.7 copy-done.2
  49.3 21.1 %shard_map.103 = (bf16[2,32,1536]{2,1,0:T(8,128)(2,1)}, bf16[2,32,1536]{2,1,0:T(8,128)(2,1)}, bf16[2,24,64,128]{3,2,1,0:T(8,128)(2,1)}, bf16[2,24,64,128]{3,2,1,...) custom-call(s32[488]{0:T(512)} %get-tuple-element.16.refs_0_, bf16[2,32,1536]{2,1,0:T(8,128)(2,1)} %bitcast.44, ...), custom_call_target="tpu_custom_call" | custom-call | tf_op jit(solution)/shard_map/pallas_call | solution.py:457
  70.5 0.0 copy-start
  70.5 51.7 %shard_map.104 = f32[2,18,2,4096]{3,2,1,0:T(2,128)} custom-call(s32[288]{0:T(512)} %reshape.16.pat.refs_0_, bf16[2,24,64,128]{3,2,1,0:T(8,128)(2,1)} %get-tuple-element.24.refs_1_, bf16[2,24,64,128]{3,2,1,0:T(8,128)(2,1)} %get-tuple-element.25.refs_2_, bf16[97,64,128]{2,1,0:T(8,128)(2,1)} %get-tuple-element.26.refs_3_, ...), custom_call_target="tpu_custom_call" | custom-call | tf_op jit(solution)/shard_map/pallas_call | solution.py:527
  122.2 0.0 copy-done
  122.2 4.2 %fusion.2 = (f32[1,2,2,18,4096]{4,2,3,1,0:T(2,128)}, bf16[1,2,2,18,4096]{4,2,3,1,0:T(2,128)(2,1)}) fusion(f32[2,18,2,4096]{3,2,1,0:T(2,128)} %shard_map.104, f32[1,2,2,18,4096]{4,2,3,1,0:T(2,128)S(1)} %copy-done, bf16[1,2,2,18,4096]{4,3,2,1,0:T(8,128)(2,1)S(1)} %constant_dynamic-slice_fusion), kind=kLoop, calls=%fused_computation.9 | loop fusion | flops 2064384 | bytes 4718592 | tf_op jit(solution)/shard_map/broadcast_in_dim | solution.py:550
  (1 shorter events, 0.0 us)
Async XLA Ops:
  38.6 4.8 %collective-permute-start = (bf16[64,1536]{1,0:T(8,128)(2,1)}, bf16[64,1536]{1,0:T(8,128)(2,1)S(1)}, u32[]{:S(2)}, u32[]{:S(2)}) collective-permute-start(bf16[64,1536]{1,0:T(8,128)(2,1)} %get-tuple-element.17.refs_5_), channel_id=1, source_target_pairs={{0,1},{1,2},{2,3},{3,4},{4,5},{5,6},{6,7},{7,8},{8,9},{9,10},{10,1... | collective-permute-start | bytes 589832 | tf_op jit(solution)/shard_map/ppermute | solution.py:507
  40.5 8.2 %collective-permute-start.1 = (bf16[64,1536]{1,0:T(8,128)(2,1)}, bf16[64,1536]{1,0:T(8,128)(2,1)S(1)}, u32[]{:S(2)}, u32[]{:S(2)}) collective-permute-start(bf16[64,1536]{1,0:T(8,128)(2,1)} %get-tuple-element.18.refs_6_), channel_id=1, source_target_pairs={{1,0},{2,1},{3,2},{4,3},{5,4},{6,5},{7,6},{8,7},{9,8},{10,9},{11,1... | collective-permute-start | bytes 589832 | tf_op jit(solution)/shard_map/ppermute | solution.py:508
  43.4 5.3 %copy-start.1 = (bf16[64,1536]{1,0:T(8,128)(2,1)}, bf16[64,1536]{1,0:T(8,128)(2,1)S(1)}, u32[]{:S(2)}) copy-start(bf16[64,1536]{1,0:T(8,128)(2,1)S(1)} %collective-permute-done.refs_7_) | copy-start | bytes 589828
  48.7 0.7 copy-start.2
  70.5 51.7 %copy-start = (f32[1,2,2,18,4096]{4,2,3,1,0:T(2,128)S(1)}, f32[1,2,2,18,4096]{4,2,3,1,0:T(2,128)}, u32[]{:S(2)}) copy-start(f32[1,2,2,18,4096]{4,2,3,1,0:T(2,128)} %param.13) | copy-start | bytes 3538948

commit v5 on v4

--- a/solution.py
+++ b/solution.py
@@ -10,8 +10,9 @@
 BETA = 0.9
 STEP = 0.2
 PER = 6
-ACTS = 2
-SLOTS = 96
+ACTS = 4
+PITCH = 72
+PARTS = 2
 VMEM_BYTES = 56 * 2**20
 
 
@@ -52,7 +53,7 @@
 
 
 def place(pat, copy, proj, n, blocks_d, blocks_f):
-    value = pat[(copy * 2 + proj) * 72 + n]
+    value = pat[copy * 2 + proj, n]
     if proj == 0:
         r = value // blocks_f
         return r, value - r * blocks_f
@@ -61,107 +62,97 @@
 
 
 def entry(lists, which, i):
-    value = lists[which * SLOTS + i]
+    value = lists[which, i]
     return value % 128, (value // 128) % 32, value // 4096
 
 
-def batched(trips, width, body):
+def batched(number, width, body):
     def step(i, carry):
         body(i * width)
         return carry
 
-    lax.fori_loop(0, trips, step, 0)
-
-
-def build_lists(pat, lists, flags, count, blocks_d, blocks_f):
+    lax.fori_loop(0, number, step, 0)
+
+
+def build_lists(pat, lists, blocks_d, blocks_f):
+    f32 = jnp.float32
     dummy = blocks_d * 128 + blocks_f * 4096
-
-    def wipe(i, carry):
-        for u in range(8):
-            flags[i * 8 + u] = 0
-        return carry
-
-    lax.fori_loop(0, 2 * blocks_f // 8, wipe, 0)
-
-    def fill(i, carry):
-        for which in range(4):
-            lists[which * SLOTS + i] = dummy
-        lists[4 * SLOTS + i] = blocks_f
-        return carry
-
-    lax.fori_loop(0, SLOTS, fill, 0)
-
-    def mark(n, carry):
-        for copy in range(2):
-            _, f = place(pat, copy, 0, n, blocks_d, blocks_f)
-            flags[copy * blocks_f + f] = 1
-        return carry
-
-    lax.fori_loop(0, count, mark, 0)
-
-    def mark_both(n, carry):
-        for copy in range(2):
-            _, f = place(pat, copy, 1, n, blocks_d, blocks_f)
-            at = copy * blocks_f + f
-            flags[at] = jnp.where(flags[at] > 0, 2, 0)
-        return carry
-
-    lax.fori_loop(0, count, mark_both, 0)
-
-    def collect(n, found):
-        after = []
-        for which in range(4):
-            copy, proj = divmod(which, 2)
-            d, f = place(pat, copy, proj, n, blocks_d, blocks_f)
-            active = flags[copy * blocks_f + f] == 2
-            at = which * SLOTS + found[which]
-            lists[at] = jnp.where(active, n + d * 128 + f * 4096, dummy)
-            after.append(found[which] + jnp.where(active, 1, 0))
-        return tuple(after)
-
-    zero = jnp.int32(0)
-    found = lax.fori_loop(0, count, collect, (zero,) * 4)
-
-    def gather(f, number):
-        active = jnp.maximum(flags[f], flags[blocks_f + f]) == 2
-        lists[4 * SLOTS + number] = jnp.where(active, f, blocks_f)
-        return number + jnp.where(active, 1, 0)
-
-    number = lax.fori_loop(0, blocks_f, gather, zero)
-    most = jnp.maximum(jnp.maximum(found[0], found[1]), jnp.maximum(found[2], found[3]))
-    lists[5 * SLOTS] = (most + PER - 1) // PER
-    lists[5 * SLOTS + 1] = (number + ACTS - 1) // ACTS
+    value = pat[...].astype(f32)
+    which = lax.broadcasted_iota(jnp.int32, (8, 128), 0)
+    lane = lax.broadcasted_iota(jnp.int32, (8, 128), 1).astype(f32)
+    width = jnp.where(which % 2 == 0, f32(blocks_f), f32(blocks_d))
+    high = jnp.floor((value + 0.5) / width)
+    low = value - high * width
+    d_of, f_of = jnp.where(which % 2 == 0, high, low), jnp.where(which % 2 == 0, low, high)
+    valid = value >= 0
+    f_of = jnp.where(valid, f_of, -1.0 - which.astype(f32))
+    f_down = jnp.transpose(jnp.concatenate([f_of] * 16, axis=0))
+    square = (128, 128)
+    along = lax.broadcasted_iota(jnp.int32, square, 1).astype(f32)
+    down = lax.broadcasted_iota(jnp.int32, square, 0).astype(f32)
+    found, touched = [], []
+    for w in range(4):
+        column = jnp.broadcast_to(f_down[:, (w ^ 1) : (w ^ 1) + 1], square)
+        same = column == jnp.broadcast_to(f_of[w : w + 1], square)
+        found.append(jnp.max(jnp.where(same, 1.0, 0.0), axis=0, keepdims=True))
+        own = jnp.broadcast_to(f_down[:, w : w + 1], square) == along
+        touched.append(jnp.max(jnp.where(own, 1.0, 0.0), axis=0, keepdims=True))
+    both = jnp.maximum(touched[0] * touched[1], touched[2] * touched[3])
+    zero = jnp.zeros((3, 128), f32)
+    active = jnp.concatenate(found + [both, zero], axis=0)
+    before = (down < along).astype(f32).astype(jnp.bfloat16)
+    place_of = mul(active.astype(jnp.bfloat16), before)
+    entries = lane + d_of * 128.0 + f_of * 4096.0 - float(dummy)
+    entries = jnp.where(which < 4, entries, lane - float(blocks_f))
+    spots = jnp.where(active > 0, place_of, -1.0)
+    turned = jnp.transpose(jnp.concatenate([spots, entries] * 8, axis=0))
+    rows = []
+    for w in range(5):
+        here = jnp.broadcast_to(turned[:, w : w + 1], square) == along
+        given = jnp.broadcast_to(turned[:, 8 + w : 9 + w], square)
+        rest = float(dummy if w < 4 else blocks_f)
+        rows.append(jnp.sum(jnp.where(here, given, 0.0), axis=0, keepdims=True) + rest)
+    lists[0:8, :] = jnp.concatenate(rows + [zero], axis=0).astype(jnp.int32)
+    lists[8:16, :] = place_of.astype(jnp.int32)
+
+
+def trips(lists):
+    most = jnp.maximum(jnp.maximum(lists[8, 127], lists[9, 127]), jnp.maximum(lists[10, 127], lists[11, 127]))
+    return (most + PER - 1) // PER
+
+
+def act_trips(lists):
+    return (lists[12, 127] + ACTS - 1) // ACTS
 
 
 def prepare_weights(lists, raw, wide, w):
-    count, half = raw.shape[2], BLOCK // 2
+    count = raw.shape[2]
 
     def spread(t, carry):
         for which in range(4):
             copy, proj = divmod(which, 2)
             value = raw[copy, proj, :, pl.ds(pl.multiple_of(t * 128, 128), 128)].astype(jnp.float32)
-            wide[which, pl.ds(t, count, stride=half), :] = value
-        return carry
-
-    lax.fori_loop(0, half, spread, 0)
+            wide[which, pl.ds(2 * t, count, stride=PITCH), :] = value
+            wide[which, pl.ds(2 * t + 1, count, stride=PITCH), :] = pltpu.roll(value, BLOCK, 1)
+        return carry
+
+    lax.fori_loop(0, BLOCK // 2, spread, 0)
     row = lax.broadcasted_iota(jnp.int32, (BLOCK, BLOCK), 0)
     col = lax.broadcasted_iota(jnp.int32, (BLOCK, BLOCK), 1)
-    back = (row == jnp.where(col < half, 2 * col, 2 * col - BLOCK + 1)).astype(jnp.float32).astype(jnp.bfloat16)
     eye = (row == col).astype(jnp.float32).astype(jnp.bfloat16)
 
     def body(i):
         done = []
         for which in range(4):
-            for u in range(3):
+            for u in range(PER):
                 n = entry(lists, which, i + u)[0]
-                value = wide[which, pl.ds(pl.multiple_of(n * half, half), half), :]
-                split = jnp.concatenate([value[:, :BLOCK], value[:, BLOCK:]], axis=0).astype(jnp.bfloat16)
-                done.append((which, n, mul(back, split).astype(jnp.bfloat16)))
-        for which, n, block in done:
+                block = wide[which, pl.ds(pl.multiple_of(n * PITCH, 8), BLOCK), :][:, :BLOCK].astype(jnp.bfloat16)
+                done.append((which, n, block, mul_nt(eye, block)))
+        for which, n, block, turned in done:
             w[0, which // 2, which % 2, n] = block
-            w[1, which // 2, which % 2, n] = mul_nt(eye, block).astype(jnp.bfloat16)
-
-    batched(lists[5 * SLOTS] * (PER // 3), 3, body)
+            w[1, which // 2, which % 2, n] = turned.astype(jnp.bfloat16)
+
+    batched(trips(lists), PER, body)
 
 
 def section_pass(lists, w, x, gy, pre, gh):
@@ -176,7 +167,7 @@
         for ref, f, term in terms:
             ref[f] += term
 
-    batched(lists[5 * SLOTS], PER, body)
+    batched(trips(lists), PER, body)
 
 
 def section_close(lists, w, hid, gp, out, first_fwd, first_bwd):
@@ -195,22 +186,25 @@
         for d, term in terms:
             out[d] += term
 
-    batched(lists[5 * SLOTS], PER, body)
+    batched(trips(lists), PER, body)
 
 
 def clear(lists, refs):
     def body(i):
         for u in range(ACTS):
-            f = lists[4 * SLOTS + i + u]
+            f = lists[4, i + u]
             for ref in refs:
                 ref[f] = jnp.zeros(ref.shape[1:], ref.dtype)
 
-    batched(lists[5 * SLOTS + 1], ACTS, body)
-
-
-def first_kernel(pat, acts, cot, stash, raw, send_up, send_down, hid, gp, lists, w_out, flags, wide, w, x, gy, pre, gh, out, sem):
+    batched(act_trips(lists), ACTS, body)
+
+
+def first_kernel(pat, acts, cot, stash, raw, send_up, send_down, hid, gp, lists_out, w_out, lists, wide, w, x, gy, pre, gh, out, sem):
     blocks_d, blocks_f = out.shape[0] - 1, pre.shape[0] - 1
-    build_lists(pat, lists, flags, raw.shape[2], blocks_d, blocks_f)
+    build_lists(pat, lists_out, blocks_d, blocks_f)
+    read = pltpu.make_async_copy(lists_out, lists, sem)
+    read.start()
+    read.wait()
     prepare_weights(lists, raw, wide, w)
     keep = pltpu.make_async_copy(w, w_out, sem)
     keep.start()
@@ -234,12 +228,12 @@
 
     def act(i):
         for u in range(ACTS):
-            f = lists[4 * SLOTS + i + u]
+            f = lists[4, i + u]
             hidden, slope = gelu_parts(pre[f])
             hid[f] = hidden.astype(jnp.bfloat16)
             gp[f] = (slope * gh[f]).astype(jnp.bfloat16)
 
-    batched(lists[5 * SLOTS + 1], ACTS, act)
+    batched(act_trips(lists), ACTS, act)
     section_close(lists, w, hid, gp, out, 0, 2)
 
     def store(i, carry):
@@ -315,13 +309,13 @@
 
     def act(i):
         for u in range(ACTS):
-            f = lists[4 * SLOTS + i + u]
+            f = lists[4, i + u]
             hidden, slope = gelu_parts(pre[f])
             hid[f] = hidden.astype(jnp.bfloat16)
             gp_both[f] = merged(slope * gh[f], gp1[f], late_half).astype(jnp.bfloat16)
             hid_both[f] = rearranged(merged(hidden, hid1[f], late_half).astype(jnp.bfloat16))
 
-    batched(lists[5 * SLOTS + 1], ACTS, act)
+    batched(act_trips(lists), ACTS, act)
     section_close(lists, w, hid, gp_both, out, 2, 0)
 
     def store(i, carry):
@@ -340,7 +334,7 @@
 
 
 def sum_kernel(
-    sections, quarter, pat, xs, gys, hid, gp, total, grads, got_core, to_side, got_side, share, got_own, got_far, wide, *sems
+    sections, quarter, pat, xs, gys, hid, gp, total, grads, got_core, to_side, got_side, share, got_own, got_far, *sems
 ):
     core_sent, core_got, side_sent, side_got, own_sent, own_got, far_sent, far_got = sems
     blocks_d, blocks_f = xs.shape[1], gp.shape[0] - 1
@@ -353,22 +347,23 @@
     pl.semaphore_wait(barrier, 3)
     half = BLOCK // 2
 
+    share_rows = quarter * half // PARTS
+
     def compute(j):
-        copy, proj = divmod(j, 2)
-        for q in range(4):
-
-            def step(i, carry, q=q):
-                for u in range(9):
-                    n = i * 9 + u
-                    d, f = place(pat, copy, proj, q * quarter + n, blocks_d, blocks_f)
-                    if proj == 0:
-                        value = mul_nt(xs[copy, d], gp[f])
-                    else:
-                        value = mul_nt(hid[f], gys[copy, d])
-                    grads[j, q // 2, q % 2, pl.ds(pl.multiple_of(n * half, half), half)] = two_wide(value)
-                return carry
-
-            lax.fori_loop(0, quarter // 9, step, 0)
+        copy, proj, part = j // (2 * PARTS), j // PARTS % 2, j % PARTS
+
+        def step(q, carry):
+            for u in range(quarter // PARTS):
+                n = part * (quarter // PARTS) + u
+                d, f = place(pat, copy, proj, q * quarter + n, blocks_d, blocks_f)
+                if proj == 0:
+                    value = mul_nt(xs[copy, d], gp[f])
+                else:
+                    value = mul_nt(hid[f], gys[copy, d])
+                grads[j, q // 2, q % 2, u * half : (u + 1) * half] = two_wide(value)
+            return carry
+
+        lax.fori_loop(0, 4, step, 0)
 
     def copies(j):
         def remote(source, target, sent, got, to):
@@ -384,14 +379,14 @@
             remote(share.at[j], got_own.at[j], own_sent, own_got, (over, me)),
         )
 
-    wires = [copies(j) for j in range(4)]
+    wires = [copies(j) for j in range(4 * PARTS)]
 
     def pieces(body):
         def step(i, carry):
-            body(pl.ds(pl.multiple_of(i * 64, 64), 64))
+            body(pl.ds(pl.multiple_of(i * 96, 96), 96))
             return carry
 
-        lax.fori_loop(0, quarter * half // 64, step, 0)
+        lax.fori_loop(0, share_rows // 96, step, 0)
 
     def after_core(j):
         wires[j][0].wait_recv()
@@ -414,40 +409,33 @@
         wires[j][2].start()
         wires[j][3].start()
 
-    def after_far(copy, proj):
-        own, other = copy * 2 + proj, (1 - copy) * 2 + proj
+    def after_far(copy, proj, part):
+        own, other = (copy * 2 + proj) * PARTS + part, ((1 - copy) * 2 + proj) * PARTS + part
         wires[own][3].wait_recv()
         wires[other][2].wait_recv()
 
         def body(i, carry):
-            rows = pl.ds(pl.multiple_of(i * 64, 64), 64)
+            rows = pl.ds(pl.multiple_of(i * 96, 96), 96)
             value = got_own[own, rows].astype(jnp.float32) + got_far[other, rows].astype(jnp.float32)
-            wide[pl.ds(i * 128 + proj, 64, stride=2), :] = value
+            total[copy, pl.ds((part * share_rows + i * 96) * 2 + proj, 96, stride=2), :] = value
             return carry
 
-        lax.fori_loop(0, quarter * half // 64, body, 0)
-
-    def finish(copy):
-        def body(n, carry):
-            for t in range(half):
-                total[copy, n, :, t * 128 : (t + 1) * 128] = wide[pl.ds((n * half + t) * 2, 2), :]
-            return carry
-
-        lax.fori_loop(0, quarter, body, 0)
-
-    for step in range(6):
-        if step < 4:
+        lax.fori_loop(0, share_rows // 96, body, 0)
+
+    number = 4 * PARTS
+    for step in range(number + 2):
+        if step < number:
             compute(step)
             wires[step][0].start()
-        if 1 <= step < 5:
+        if 1 <= step < number + 1:
             after_core(step - 1)
         if 2 <= step:
             after_side(step - 2)
     for copy in (1, 0):
         for proj in range(2):
-            after_far(copy, proj)
-        finish(copy)
-    for j in range(4):
+            for part in range(PARTS):
+                after_far(copy, proj, part)
+    for j in range(number):
         for wire in wires[j]:
             wire.wait_send()
 
@@ -464,17 +452,30 @@
     )(*(value for _, value in args))
 
 
+def dense(value):
+    copies, projs, count, size = value.shape
+    value = jnp.swapaxes(value, 1, 2).reshape(copies, count, projs, size // 128, 128)
+    return jnp.swapaxes(value, 2, 3).reshape(copies, -1, 128)
+
+
+def spread_out(value):
+    value = value.reshape(2, -1, BLOCK // 2, 2, 128)
+    count = value.shape[1]
+    return jnp.swapaxes(jnp.swapaxes(value, 2, 3).reshape(2, count, 2, -1), 1, 2)
+
+
 def shards(acts_in, cot_in, stash, entering, pattern, weights, momentum):
     bf16, f32 = jnp.bfloat16, jnp.float32
     me, sections = lax.axis_index("pipe"), lax.axis_size("pipe")
     group = lax.axis_index("dp")
     acts, cot, saved, fresh = (jnp.swapaxes(one, -1, -2) for one in (acts_in[0, 0], cot_in[0, 0], stash[0, 0], entering[0]))
-    pat = jnp.stack(
+    pat = jnp.concatenate(
         [
             lax.dynamic_index_in_dim(pattern, me, 0, keepdims=False),
             lax.dynamic_index_in_dim(pattern, sections - 1 - me, 0, keepdims=False),
         ]
-    ).reshape(-1)
+    )
+    pat = jnp.pad(pat, ((0, 4), (0, 128 - pat.shape[1])), constant_values=-1)
     tokens, width = acts.shape[1:]
     count = weights.shape[3]
     blocks_d, blocks_f = width // BLOCK, FF // BLOCK
@@ -484,18 +485,18 @@
     w_shape = (2, 2, 2, count, BLOCK, BLOCK)
     send_up, send_down, hid, gp, lists, w = call(
         first_kernel,
-        [("s", pat), ("v", acts), ("v", cot), ("v", saved), ("v", raw)],
+        [("v", pat), ("v", acts), ("v", cot), ("v", saved), ("v", raw)],
         [
             ("v", (2 * tokens, width), bf16),
             ("v", (2 * tokens, width), bf16),
             ("v", f_block, bf16),
             ("v", f_block, bf16),
-            ("s", (5 * SLOTS + 8,), jnp.int32),
+            ("v", (16, 128), jnp.int32),
             ("a", w_shape, bf16),
         ],
         [
-            ("s", (2 * blocks_f,), jnp.int32),
-            ("v", (4, count * BLOCK // 2, 128), f32),
+            ("s", (16, 128), jnp.int32),
+            ("v", (4, count * PITCH, 128), f32),
             ("v", w_shape, bf16),
             ("v", x_block, bf16),
             ("v", x_block, bf16),
@@ -522,30 +523,29 @@
         ],
     )
     quarter = count // 4
-    chunk = (4, quarter * BLOCK // 2, 128)
+    chunk = (4 * PARTS, quarter * BLOCK // 2 // PARTS, 128)
     smem, vmem = pl.BlockSpec(memory_space=pltpu.SMEM), pl.BlockSpec(memory_space=pltpu.VMEM)
     total = pl.pallas_call(
         lambda *refs: sum_kernel(sections, quarter, *refs),
-        out_shape=jax.ShapeDtypeStruct((2, quarter, 2, weights.shape[4]), f32),
+        out_shape=jax.ShapeDtypeStruct((2, quarter * BLOCK, 128), f32),
         in_specs=[smem] + [vmem] * 4,
         out_specs=vmem,
         scratch_shapes=[
-            pltpu.VMEM((4, 2, 2, *chunk[1:]), bf16),
-            pltpu.VMEM((4, 2, *chunk[1:]), bf16),
+            pltpu.VMEM((4 * PARTS, 2, 2, *chunk[1:]), bf16),
+            pltpu.VMEM((4 * PARTS, 2, *chunk[1:]), bf16),
             pltpu.VMEM(chunk, bf16),
             pltpu.VMEM(chunk, bf16),
             pltpu.VMEM(chunk, bf16),
             pltpu.VMEM(chunk, bf16),
             pltpu.VMEM(chunk, bf16),
-            pltpu.VMEM((2 * chunk[1], 128), f32),
         ]
-        + [pltpu.SemaphoreType.DMA((4,))] * 8,
+        + [pltpu.SemaphoreType.DMA((4 * PARTS,))] * 8,
         compiler_params=pltpu.CompilerParams(collective_id=0, has_side_effects=True, vmem_limit_bytes=VMEM_BYTES),
     )(pat, xs, gys, hid, gp)
-    total = jnp.swapaxes(total, 1, 2)
-    momentum_next = BETA * momentum[0] + total / (2 * tokens)
     own = lax.dynamic_slice_in_dim(weights[0], group * quarter, quarter, axis=2)
-    weights_next = (own.astype(f32) - STEP * momentum_next).astype(bf16)
+    momentum_next = BETA * dense(momentum[0]) + total / (2 * tokens)
+    weights_next = spread_out((dense(own).astype(f32) - STEP * momentum_next).astype(bf16))
+    momentum_next = spread_out(momentum_next)
     forward, backward = jnp.swapaxes(forward, 1, 2), jnp.swapaxes(backward, 1, 2)
     return forward[None, None], backward[None, None], weights_next[None], momentum_next[None]
 

time: 127 us -> 109 us (0.86); the launches traced: 126 us -> 107 us
  Pallas kernels: 109 us -> 86.7 us
  starting transfers between devices: 3.18 us -> 7.06 us
  waiting for transfers between devices: 5.44 us -> 1.8 us
  local copies, waits for them, and re-layouts: 3.5 us -> 5.44 us
    pallas_call x2, Pallas kernels: 57.7 us -> 40.2 us  [call(): pl.pallas_call(kernel, out_shape=[jax.ShapeDtypeStruct(*out[1:]) for out...]
    pallas_call x1, Pallas kernels: 51.7 us -> 46.5 us  [shards(): pl.pallas_call(lambda *refs: sum_kernel(sections, quarter, *refs), out_sh...]
    broadcast_in_dim x1 -> x0, other arithmetic: 4.23 us -> none  [shards(): momentum_next[None]]
    convert_element_type x0 -> x2, other arithmetic: none -> 4.15 us  [the longest x1 2.7 us: shards(): (dense(own).astype(f32) - STEP * momentum_next).astype(bf16)]
    ppermute x1, starting transfers between devices: 1.89 us -> 5.77 us  [shards(): lax.ppermute(send_up, 'pipe', [(i, i + 1) for i in range(sections - 1)])]
    ppermute x1, waiting for transfers between devices: 5.3 us -> 1.8 us  [shards(): lax.ppermute(send_down, 'pipe', [(i + 1, i) for i in range(sections - 1)])]
    convert_element_type x0 -> x2, local copies, waits for them, and re-layouts: none -> 3.46 us  [shards(): dense(own).astype(f32) - STEP * momentum_next]
    dynamic_slice x2 -> x0, local copies, waits for them, and re-layouts: 2.15 us -> none  [the longest x1 1.45 us: shards(): own = lax.dynamic_slice_in_dim(weights[0], group * quarter, quarter, axis=2)]
  transfers between devices with their start and end apart: 2 -> 2, of which waited for: 2 -> 1; matrix products, arithmetic and copies ran while one was open for 1% -> 6% of each run, Pallas kernels for 0% -> 0%
where the time goes in v5:
time: 109 us; the launch traced here: 107 us
  Pallas kernels  86.7 us (80%)
  starting transfers between devices  7.06 us (6%)
  local copies, waits for them, and re-layouts  5.44 us (5%)
  other arithmetic  5.16 us (5%)
  waiting for transfers between devices  1.8 us (2%)
    pallas_call x1, Pallas kernels, shards(): pl.pallas_call(lambda *refs: sum_kernel(sections, quarter, *refs), out_sh...  46.5 us
    pallas_call x2, Pallas kernels, call(): pl.pallas_call(kernel, out_shape=[jax.ShapeDtypeStruct(*out[1:]) for out...  40.2 us
    ppermute x1, starting transfers between devices, shards(): lax.ppermute(send_up, 'pipe', [(i, i + 1) for i in range(sections - 1)])  5.77 us
    convert_element_type x2, local copies, waits for them, and re-layouts, shards(): dense(own).astype(f32) - STEP * momentum_next  3.46 us
    convert_element_type x1, other arithmetic, shards(): (dense(own).astype(f32) - STEP * momentum_next).astype(bf16)  2.7 us
  transfers between devices with their start and end apart: 2, of which 1 were waited for; matrix products, arithmetic and copies ran while one was open for 6% of the time, Pallas kernels for 0%

profile of v5, /device:TPU:1, one launch (start us, length us, event | category | flops | bytes accessed | tf_op | source)
XLA Modules:
  0.0 106.8 jit_solution(16900172925367878459)
XLA Ops:
  0.6 0.7 dynamic-slice_bitcast_fusion.1
  1.3 0.6 pad.4.pat.refs_0_
  1.9 0.0 copy-start
  1.9 21.6 %shard_map.102 = (bf16[64,1536]{1,0:T(8,128)(2,1)}, bf16[64,1536]{1,0:T(8,128)(2,1)}, bf16[97,64,128]{2,1,0:T(8,128)(2,1)}, bf16[97,64,128]{2,1,0:T(8,128)(2,1)}...) custom-call(s32[8,128]{1,0:T(8,128)} %pad.4.pat.refs_0_, bf16[2,32,1536]{2,1,0:T(8,128)(2,1)} %bitcast.67, ...), custom_call_target="tpu_custom_call" | custom-call | tf_op jit(solution)/shard_map/pallas_call | solution.py:445
  23.5 5.8 %collective-permute-start = (bf16[64,1536]{1,0:T(8,128)(2,1)}, bf16[64,1536]{1,0:T(8,128)(2,1)S(1)}, u32[]{:S(2)}, u32[]{:S(2)}) collective-permute-start(bf16[64,1536]{1,0:T(8,128)(2,1)} %get-tuple-element.17.refs_5_), channel_id=1, source_target_pairs={{0,1},{1,2},{2,3},{3,4},{4,5},{5,6},{6,7},{7,8},{8,9},{9,10},{10,1... | collective-permute-start | bytes 589832 | tf_op jit(solution)/shard_map/ppermute | solution.py:508
  29.3 1.3 %collective-permute-start.1 = (bf16[64,1536]{1,0:T(8,128)(2,1)}, bf16[64,1536]{1,0:T(8,128)(2,1)S(1)}, u32[]{:S(2)}, u32[]{:S(2)}) collective-permute-start(bf16[64,1536]{1,0:T(8,128)(2,1)} %get-tuple-element.18.refs_6_), channel_id=1, source_target_pairs={{1,0},{2,1},{3,2},{4,3},{5,4},{6,5},{7,6},{8,7},{9,8},{10,9},{11,1... | collective-permute-start | bytes 589832 | tf_op jit(solution)/shard_map/ppermute | solution.py:509
  30.6 0.0 copy-done
  30.6 1.0 broadcast_multiply_fusion
  31.6 1.4 %convert_bitcast_fusion = f32[2,18,2,4096]{3,1,2,0:T(8,128)S(1)} fusion(bf16[1,2,2,72,4096]{4,3,2,1,0:T(8,128)(2,1)} %param.12, s32[]{:T(128)S(6)} %select_n.12), kind=kLoop, calls=%fused_computation | loop fusion | flops 294912 | bytes 1769476 | tf_op jit(solution)/shard_map/convert_element_type | solution.py:547
  33.1 1.2 %reshape.42 = f32[2,18,2,32,128]{4,3,1,2,0:T(8,128)} reshape(f32[2,18,2,4096]{3,1,2,0:T(8,128)S(1)} %convert_bitcast_fusion) | data formatting | bytes 2359296 | tf_op jit(solution)/shard_map/convert_element_type | solution.py:547
  34.3 2.2 %copy.14 = f32[2,18,32,2,128]{4,3,2,1,0:T(2,128)S(1)} copy(f32[2,18,32,2,128]{4,2,1,3,0:T(8,128)} %bitcast.62) | data formatting | bytes 2359296 | tf_op jit(solution)/shard_map/convert_element_type | solution.py:547
  36.5 0.0 collective-permute-done.refs_7_
  36.5 0.0 copy-start.1
  36.5 1.8 %collective-permute-done.1.refs_8_ = bf16[64,1536]{1,0:T(8,128)(2,1)S(1)} collective-permute-done((bf16[64,1536]{1,0:T(8,128)(2,1)}, bf16[64,1536]{1,0:T(8,128)(2,1)S(1)}, u32[]{:S(2)}, u32[]{:S(2)}) %collective-permute-start.1) | collective-permute-done | bytes 196640 | tf_op jit(solution)/shard_map/ppermute | solution.py:509
  38.3 0.0 copy-start.2
  38.4 0.0 copy-done.1
  38.4 0.7 copy-done.2
  39.0 18.6 %shard_map.103 = (bf16[2,32,1536]{2,1,0:T(8,128)(2,1)}, bf16[2,32,1536]{2,1,0:T(8,128)(2,1)}, bf16[2,24,64,128]{3,2,1,0:T(8,128)(2,1)}, bf16[2,24,64,128]{3,2,1,...) custom-call(s32[16,128]{1,0:T(8,128)} %get-tuple-element.16.refs_0_, ...), custom_call_target="tpu_custom_call" | custom-call | tf_op jit(solution)/shard_map/pallas_call | solution.py:445
  57.7 46.5 %shard_map.104 = f32[2,1152,128]{2,1,0:T(8,128)} custom-call(s32[8,128]{1,0:T(8,128)} %pad.4.pat.refs_0_, bf16[2,24,64,128]{3,2,1,0:T(8,128)(2,1)} %get-tuple-element.24.refs_1_, bf16[2,24,64,128]{3,2,1,0:T(8,128)(2,1)} %get-tuple-element.25.refs_2_, bf16[97,64,128]{2,1,0:T(8,128)(2,1)} %get-tuple-element.26.refs_3_, ...), custom_call_target="tpu_custom_call" | custom-call | tf_op jit(solution)/shard_map/pallas_call | solution.py:528
  104.1 2.7 %subtract_convert_fusion = (bf16[2,1152,128]{2,1,0:T(8,128)(2,1)}, f32[2,1152,128]{2,1,0:T(8,128)}) fusion(f32[2,1152,128]{2,1,0:T(8,128)S(1)} %bitcast.61, f32[2,1152,128]{2,1,0:T(8,128)S(1)} %bitcast.60, f32[2,1152,128]{2,1,0:T(8,128)} %shard_map.104), kind=kLoop, calls=%fused_computation.1 | loop fusion | flops 1474560 | bytes 5308416 | tf_op jit(solution)/shard_map/convert_element_type | solution.py:547
  (1 shorter events, 0.0 us)
Async XLA Ops:
  1.9 28.6 %copy-start = (f32[1,2,2,18,4096]{4,2,3,1,0:T(2,128)S(1)}, f32[1,2,2,18,4096]{4,2,3,1,0:T(2,128)}, u32[]{:S(2)}) copy-start(f32[1,2,2,18,4096]{4,2,3,1,0:T(2,128)} %param.13) | copy-start | bytes 3538948
  23.5 13.0 %collective-permute-start = (bf16[64,1536]{1,0:T(8,128)(2,1)}, bf16[64,1536]{1,0:T(8,128)(2,1)S(1)}, u32[]{:S(2)}, u32[]{:S(2)}) collective-permute-start(bf16[64,1536]{1,0:T(8,128)(2,1)} %get-tuple-element.17.refs_5_), channel_id=1, source_target_pairs={{0,1},{1,2},{2,3},{3,4},{4,5},{5,6},{6,7},{7,8},{8,9},{9,10},{10,1... | collective-permute-start | bytes 589832 | tf_op jit(solution)/shard_map/ppermute | solution.py:508
  29.3 9.1 %collective-permute-start.1 = (bf16[64,1536]{1,0:T(8,128)(2,1)}, bf16[64,1536]{1,0:T(8,128)(2,1)S(1)}, u32[]{:S(2)}, u32[]{:S(2)}) collective-permute-start(bf16[64,1536]{1,0:T(8,128)(2,1)} %get-tuple-element.18.refs_6_), channel_id=1, source_target_pairs={{1,0},{2,1},{3,2},{4,3},{5,4},{6,5},{7,6},{8,7},{9,8},{10,9},{11,1... | collective-permute-start | bytes 589832 | tf_op jit(solution)/shard_map/ppermute | solution.py:509
  36.5 1.8 %copy-start.1 = (bf16[64,1536]{1,0:T(8,128)(2,1)}, bf16[64,1536]{1,0:T(8,128)(2,1)S(1)}, u32[]{:S(2)}) copy-start(bf16[64,1536]{1,0:T(8,128)(2,1)S(1)} %collective-permute-done.refs_7_) | copy-start | bytes 589828
  38.3 0.7 copy-start.2

commit v6 on v5

--- a/solution.py
+++ b/solution.py
@@ -9,8 +9,8 @@
 BLOCK = 64
 BETA = 0.9
 STEP = 0.2
-PER = 6
-ACTS = 4
+PER = 12
+ACTS = 8
 PITCH = 72
 PARTS = 2
 VMEM_BYTES = 56 * 2**20
@@ -72,6 +72,12 @@
         return carry
 
     lax.fori_loop(0, number, step, 0)
+
+
+def begin(source, target, sem):
+    copy = pltpu.make_async_copy(source, target, sem)
+    copy.start()
+    return copy
 
 
 def build_lists(pat, lists, blocks_d, blocks_f):
@@ -136,7 +142,7 @@
             wide[which, pl.ds(2 * t + 1, count, stride=PITCH), :] = pltpu.roll(value, BLOCK, 1)
         return carry
 
-    lax.fori_loop(0, BLOCK // 2, spread, 0)
+    lax.fori_loop(0, BLOCK // 2, spread, 0, unroll=4)
     row = lax.broadcasted_iota(jnp.int32, (BLOCK, BLOCK), 0)
     col = lax.broadcasted_iota(jnp.int32, (BLOCK, BLOCK), 1)
     eye = (row == col).astype(jnp.float32).astype(jnp.bfloat16)
@@ -199,16 +205,19 @@
     batched(act_trips(lists), ACTS, body)
 
 
-def first_kernel(pat, acts, cot, stash, raw, send_up, send_down, hid, gp, lists_out, w_out, lists, wide, w, x, gy, pre, gh, out, sem):
+def first_kernel(
+    pat, acts_in, cot_in, stash_in, raw, send_up, send_down, hid_out, gp_out, lists_out, w_out,
+    acts, cot, stash, hid, gp, lists, wide, w, x, gy, pre, gh, out, sem,
+):
     blocks_d, blocks_f = out.shape[0] - 1, pre.shape[0] - 1
+    reads = [begin(acts_in, acts, sem.at[0]), begin(cot_in, cot, sem.at[1]), begin(stash_in, stash, sem.at[2])]
     build_lists(pat, lists_out, blocks_d, blocks_f)
-    read = pltpu.make_async_copy(lists_out, lists, sem)
-    read.start()
-    read.wait()
+    begin(lists_out, lists, sem.at[3]).wait()
     prepare_weights(lists, raw, wide, w)
-    keep = pltpu.make_async_copy(w, w_out, sem)
-    keep.start()
+    writes = [begin(w, w_out, sem.at[4])]
     clear(lists, (pre, gh))
+    for read in reads:
+        read.wait()
     masks = [copy_mask(copy, 128) for copy in range(2)]
     backward = lax.broadcasted_iota(jnp.int32, (128, 128), 1) >= 64
 
@@ -223,7 +232,7 @@
         put(out, i, jnp.where(backward, cots.astype(jnp.float32), inputs.astype(jnp.float32)))
         return carry
 
-    lax.fori_loop(0, blocks_d // 2, load, 0)
+    lax.fori_loop(0, blocks_d // 2, load, 0, unroll=2)
     section_pass(lists, w, x, gy, pre, gh)
 
     def act(i):
@@ -234,6 +243,7 @@
             gp[f] = (slope * gh[f]).astype(jnp.bfloat16)
 
     batched(act_trips(lists), ACTS, act)
+    writes += [begin(hid, hid_out, sem.at[5]), begin(gp, gp_out, sem.at[6])]
     section_close(lists, w, hid, gp, out, 0, 2)
 
     def store(i, carry):
@@ -244,16 +254,18 @@
         send_down[:, cols] = value[32:96]
         return carry
 
-    lax.fori_loop(0, blocks_d // 2, store, 0)
-    keep.wait()
+    lax.fori_loop(0, blocks_d // 2, store, 0, unroll=4)
+    for write in writes:
+        write.wait()
 
 
 def second_kernel(
-    sections, lists, acts, cot, stash, entering, sent_up, sent_down, got_up, got_down, hid1, gp1, w_in,
-    forward, backward, xs, gys, hid_both, gp_both, w, hid, x, gy, pre, gh, out, sem,
+    sections, lists, acts, cot, stash, entering, sent_up, sent_down, got_up, got_down, hid1_in, gp1_in, w_in,
+    forward, backward, xs_out, gys_out, hid_out, gp_out,
+    hid1, gp1, xs, gys, hid_both, gp_both, w, hid, x, gy, pre, gh, out, sem,
 ):
-    fetch = pltpu.make_async_copy(w_in, w, sem)
-    fetch.start()
+    fetch = begin(w_in, w, sem.at[0])
+    early = [begin(hid1_in, hid1, sem.at[1]), begin(gp1_in, gp1, sem.at[2])]
     blocks_d, blocks_f = out.shape[0] - 1, pre.shape[0] - 1
     me = lax.axis_index("pipe")
     at_entry, at_exit = me == 0, me == sections - 1
@@ -303,9 +315,12 @@
                 xs[copy, 2 * i + part] = piece * half_masks[copy]
         return carry
 
-    lax.fori_loop(0, blocks_d // 2, load, 0)
+    lax.fori_loop(0, blocks_d // 2, load, 0, unroll=2)
+    writes = [begin(xs, xs_out, sem.at[3]), begin(gys, gys_out, sem.at[4])]
     fetch.wait()
     section_pass(lists, w, x, gy, pre, gh)
+    for read in early:
+        read.wait()
 
     def act(i):
         for u in range(ACTS):
@@ -316,6 +331,7 @@
             hid_both[f] = rearranged(merged(hidden, hid1[f], late_half).astype(jnp.bfloat16))
 
     batched(act_trips(lists), ACTS, act)
+    writes += [begin(hid_both, hid_out, sem.at[5]), begin(gp_both, gp_out, sem.at[6])]
     section_close(lists, w, hid, gp_both, out, 2, 0)
 
     def store(i, carry):
@@ -326,7 +342,9 @@
             forward[copy, :, cols] = value[64 + 32 * copy : 96 + 32 * copy]
         return carry
 
-    lax.fori_loop(0, blocks_d // 2, store, 0)
+    lax.fori_loop(0, blocks_d // 2, store, 0, unroll=4)
+    for write in writes:
+        write.wait()
 
 
 def two_wide(value):
@@ -334,17 +352,17 @@
 
 
 def sum_kernel(
-    sections, quarter, pat, xs, gys, hid, gp, total, grads, got_core, to_side, got_side, share, got_own, got_far, *sems
+    sections, quarter, pat, xs, gys_in, hid_in, gp, total, gys, hid, local, grads, got_core, to_side, got_side, share, got_own, got_far, *sems
 ):
     core_sent, core_got, side_sent, side_got, own_sent, own_got, far_sent, far_got = sems
     blocks_d, blocks_f = xs.shape[1], gp.shape[0] - 1
     me, group = lax.axis_index("pipe"), lax.axis_index("dp")
     core, side = lax.rem(group, 2), group // 2
     near, over, far = group + 1 - 2 * core, group + 2 - 4 * side, sections - 1 - me
+    reads = [begin(gys_in, gys, local.at[0]), begin(hid_in, hid, local.at[1])]
     barrier = pltpu.get_barrier_semaphore()
     for other in ((near, me), (over, me), (over, far)):
         pl.semaphore_signal(barrier, inc=1, device_id=other, device_id_type=pl.DeviceIdType.MESH)
-    pl.semaphore_wait(barrier, 3)
     half = BLOCK // 2
 
     share_rows = quarter * half // PARTS
@@ -424,8 +442,13 @@
 
     number = 4 * PARTS
     for step in range(number + 2):
+        if step == PARTS:
+            for read in reads:
+                read.wait()
         if step < number:
             compute(step)
+            if step == 0:
+                pl.semaphore_wait(barrier, 3)
             wires[step][0].start()
         if 1 <= step < number + 1:
             after_core(step - 1)
@@ -447,7 +470,7 @@
         out_shape=[jax.ShapeDtypeStruct(*out[1:]) for out in outs],
         in_specs=[pl.BlockSpec(memory_space=space[kind]) for kind, _ in args],
         out_specs=[pl.BlockSpec(memory_space=space[out[0]]) for out in outs],
-        scratch_shapes=[space[one[0]](*one[1:]) for one in scratch] + [pltpu.SemaphoreType.DMA],
+        scratch_shapes=[space[one[0]](*one[1:]) for one in scratch] + [pltpu.SemaphoreType.DMA((8,))],
         compiler_params=pltpu.CompilerParams(vmem_limit_bytes=VMEM_BYTES),
     )(*(value for _, value in args))
 
@@ -485,16 +508,21 @@
     w_shape = (2, 2, 2, count, BLOCK, BLOCK)
     send_up, send_down, hid, gp, lists, w = call(
         first_kernel,
-        [("v", pat), ("v", acts), ("v", cot), ("v", saved), ("v", raw)],
+        [("v", pat), ("a", acts), ("a", cot), ("a", saved), ("v", raw)],
         [
             ("v", (2 * tokens, width), bf16),
             ("v", (2 * tokens, width), bf16),
-            ("v", f_block, bf16),
-            ("v", f_block, bf16),
+            ("a", f_block, bf16),
+            ("a", f_block, bf16),
             ("v", (16, 128), jnp.int32),
             ("a", w_shape, bf16),
         ],
         [
+            ("v", acts.shape, bf16),
+            ("v", cot.shape, bf16),
+            ("v", saved.shape, bf16),
+            ("v", f_block, bf16),
+            ("v", f_block, bf16),
             ("s", (16, 128), jnp.int32),
             ("v", (4, count * PITCH, 128), f32),
             ("v", w_shape, bf16),
@@ -507,12 +535,15 @@
     )
     got_up = lax.ppermute(send_up, "pipe", [(i, i + 1) for i in range(sections - 1)])
     got_down = lax.ppermute(send_down, "pipe", [(i + 1, i) for i in range(sections - 1)])
-    vectors = (acts, cot, saved, fresh, send_up, send_down, got_up, got_down, hid, gp)
+    vectors = (acts, cot, saved, fresh, send_up, send_down, got_up, got_down)
     forward, backward, xs, gys, hid, gp = call(
         lambda *refs: second_kernel(sections, *refs),
-        [("s", lists)] + [("v", one) for one in vectors] + [("a", w)],
-        [("v", acts.shape, bf16)] * 2 + [("v", (2, *d_block), bf16)] * 2 + [("v", f_block, bf16)] * 2,
-        [
+        [("s", lists)] + [("v", one) for one in vectors] + [("a", hid), ("a", gp), ("a", w)],
+        [("v", acts.shape, bf16)] * 2 + [("a", (2, *d_block), bf16)] * 2 + [("a", f_block, bf16)] * 2,
+        [("v", f_block, bf16)] * 2
+        + [("v", (2, *d_block), bf16)] * 2
+        + [("v", f_block, bf16)] * 2
+        + [
             ("v", w_shape, bf16),
             ("v", f_block, bf16),
             ("v", x_block, bf16),
@@ -525,12 +556,16 @@
     quarter = count // 4
     chunk = (4 * PARTS, quarter * BLOCK // 2 // PARTS, 128)
     smem, vmem = pl.BlockSpec(memory_space=pltpu.SMEM), pl.BlockSpec(memory_space=pltpu.VMEM)
+    hbm = pl.BlockSpec(memory_space=pl.ANY)
     total = pl.pallas_call(
         lambda *refs: sum_kernel(sections, quarter, *refs),
         out_shape=jax.ShapeDtypeStruct((2, quarter * BLOCK, 128), f32),
-        in_specs=[smem] + [vmem] * 4,
+        in_specs=[smem, vmem, hbm, hbm, vmem],
         out_specs=vmem,
         scratch_shapes=[
+            pltpu.VMEM((2, *d_block), bf16),
+            pltpu.VMEM(f_block, bf16),
+            pltpu.SemaphoreType.DMA((2,)),
             pltpu.VMEM((4 * PARTS, 2, 2, *chunk[1:]), bf16),
             pltpu.VMEM((4 * PARTS, 2, *chunk[1:]), bf16),
             pltpu.VMEM(chunk, bf16),

time: 109 us -> 98.7 us (0.906)
  the two profiles are of different devices: /device:TPU:1 before, /device:TPU:32 now
where the time goes in v6:
time: 98.7 us; the launch traced here: 98.4 us
  Pallas kernels  75.6 us (77%)
  starting transfers between devices  10.4 us (11%)
  local copies, waits for them, and re-layouts  5.44 us (6%)
  other arithmetic  5.16 us (5%)
  waiting for transfers between devices  1.15 us (1%)
    pallas_call x1, Pallas kernels, shards(): pl.pallas_call(lambda *refs: sum_kernel(sections, quarter, *refs), out_sh...  43 us
    pallas_call x2, Pallas kernels, call(): pl.pallas_call(kernel, out_shape=[jax.ShapeDtypeStruct(*out[1:]) for out...  32.6 us
    ppermute x1, starting transfers between devices, shards(): lax.ppermute(send_down, 'pipe', [(i + 1, i) for i in range(sections - 1)])  5.26 us
    ppermute x1, starting transfers between devices, shards(): lax.ppermute(send_up, 'pipe', [(i, i + 1) for i in range(sections - 1)])  5.1 us
    convert_element_type x2, local copies, waits for them, and re-layouts, shards(): dense(own).astype(f32) - STEP * momentum_next  3.46 us
    convert_element_type x1, other arithmetic, shards(): (dense(own).astype(f32) - STEP * momentum_next).astype(bf16)  2.7 us
  transfers between devices with their start and end apart: 2, of which 1 were waited for; matrix products, arithmetic and copies ran while one was open for 6% of the time, Pallas kernels for 0%

profile of v6, /device:TPU:32, one launch (start us, length us, event | category | flops | bytes accessed | tf_op | source)
XLA Modules:
  0.0 98.4 jit_solution(6369298572616042458)
XLA Ops:
  0.6 0.7 dynamic-slice_bitcast_fusion.1
  1.3 0.6 pad.4.pat.refs_0_
  1.9 0.0 copy-start
  1.9 17.5 %shard_map.102 = (bf16[64,1536]{1,0:T(8,128)(2,1)}, bf16[64,1536]{1,0:T(8,128)(2,1)}, bf16[97,64,128]{2,1,0:T(8,128)(2,1)}, bf16[97,64,128]{2,1,0:T(8,128)(2,1)}...) custom-call(s32[8,128]{1,0:T(8,128)} %pad.4.pat.refs_0_, bf16[2,32,1536]{2,1,0:T(8,128)(2,1)} %bitcast.67, ...), custom_call_target="tpu_custom_call" | custom-call | tf_op jit(solution)/shard_map/pallas_call | solution.py:468
  19.4 5.1 %collective-permute-start = (bf16[64,1536]{1,0:T(8,128)(2,1)}, bf16[64,1536]{1,0:T(8,128)(2,1)S(1)}, u32[]{:S(2)}, u32[]{:S(2)}) collective-permute-start(bf16[64,1536]{1,0:T(8,128)(2,1)} %get-tuple-element.17.refs_5_), channel_id=1, source_target_pairs={{0,1},{1,2},{2,3},{3,4},{4,5},{5,6},{6,7},{7,8},{8,9},{9,10},{10,1... | collective-permute-start | bytes 589832 | tf_op jit(solution)/shard_map/ppermute | solution.py:536
  24.5 5.3 %collective-permute-start.1 = (bf16[64,1536]{1,0:T(8,128)(2,1)}, bf16[64,1536]{1,0:T(8,128)(2,1)S(1)}, u32[]{:S(2)}, u32[]{:S(2)}) collective-permute-start(bf16[64,1536]{1,0:T(8,128)(2,1)} %get-tuple-element.18.refs_6_), channel_id=1, source_target_pairs={{1,0},{2,1},{3,2},{4,3},{5,4},{6,5},{7,6},{8,7},{9,8},{10,9},{11,1... | collective-permute-start | bytes 589832 | tf_op jit(solution)/shard_map/ppermute | solution.py:537
  29.8 0.0 copy-done
  29.8 1.0 %broadcast_multiply_fusion = f32[1,2,2,18,4096]{4,2,3,1,0:T(2,128)S(1)} fusion(f32[1,2,2,18,4096]{4,2,3,1,0:T(2,128)S(1)} %copy-done), kind=kLoop, calls=%fused_computation.3 | loop fusion | flops 294912 | bytes 2359296 | tf_op jit(solution)/shard_map/mul | solution.py:581
  30.8 1.4 %convert_bitcast_fusion = f32[2,18,2,4096]{3,1,2,0:T(8,128)S(1)} fusion(bf16[1,2,2,72,4096]{4,3,2,1,0:T(8,128)(2,1)} %param.12, s32[]{:T(128)S(6)} %select_n.12), kind=kLoop, calls=%fused_computation | loop fusion | flops 294912 | bytes 1769476 | tf_op jit(solution)/shard_map/convert_element_type | solution.py:582
  32.3 1.2 %reshape.42 = f32[2,18,2,32,128]{4,3,1,2,0:T(8,128)} reshape(f32[2,18,2,4096]{3,1,2,0:T(8,128)S(1)} %convert_bitcast_fusion) | data formatting | bytes 2359296 | tf_op jit(solution)/shard_map/convert_element_type | solution.py:582
  33.5 2.2 %copy.14 = f32[2,18,32,2,128]{4,3,2,1,0:T(2,128)S(1)} copy(f32[2,18,32,2,128]{4,2,1,3,0:T(8,128)} %bitcast.62) | data formatting | bytes 2359296 | tf_op jit(solution)/shard_map/convert_element_type | solution.py:582
  35.7 0.0 collective-permute-done.refs_7_
  35.7 0.0 copy-start.1
  35.8 1.1 %collective-permute-done.1.refs_8_ = bf16[64,1536]{1,0:T(8,128)(2,1)S(1)} collective-permute-done((bf16[64,1536]{1,0:T(8,128)(2,1)}, bf16[64,1536]{1,0:T(8,128)(2,1)S(1)}, u32[]{:S(2)}, u32[]{:S(2)}) %collective-permute-start.1) | collective-permute-done | bytes 196640 | tf_op jit(solution)/shard_map/ppermute | solution.py:537
  36.9 0.0 copy-start.2
  36.9 0.0 copy-done.1
  36.9 0.7 copy-done.2
  37.6 15.1 %shard_map.103 = (bf16[2,32,1536]{2,1,0:T(8,128)(2,1)}, bf16[2,32,1536]{2,1,0:T(8,128)(2,1)}, bf16[2,24,64,128]{3,2,1,0:T(8,128)(2,1)}, bf16[2,24,64,128]{3,2,1,...) custom-call(s32[16,128]{1,0:T(8,128)} %get-tuple-element.16.refs_0_, ...), custom_call_target="tpu_custom_call" | custom-call | tf_op jit(solution)/shard_map/pallas_call | solution.py:468
  52.7 43.0 %shard_map.104 = f32[2,1152,128]{2,1,0:T(8,128)} custom-call(s32[8,128]{1,0:T(8,128)} %pad.4.pat.refs_0_, bf16[2,24,64,128]{3,2,1,0:T(8,128)(2,1)} %get-tuple-element.24.refs_1_, bf16[2,24,64,128]{3,2,1,0:T(8,128)(2,1)} %get-tuple-element.25.refs_2_, bf16[97,64,128]{2,1,0:T(8,128)(2,1)} %get-tuple-element.26.refs_3_, ...), custom_call_target="tpu_custom_call" | custom-call | tf_op jit(solution)/shard_map/pallas_call | solution.py:560
  95.7 2.7 %subtract_convert_fusion = (bf16[2,1152,128]{2,1,0:T(8,128)(2,1)}, f32[2,1152,128]{2,1,0:T(8,128)}) fusion(f32[2,1152,128]{2,1,0:T(8,128)S(1)} %bitcast.61, f32[2,1152,128]{2,1,0:T(8,128)S(1)} %bitcast.60, f32[2,1152,128]{2,1,0:T(8,128)} %shard_map.104), kind=kLoop, calls=%fused_computation.1 | loop fusion | flops 1474560 | bytes 5308416 | tf_op jit(solution)/shard_map/convert_element_type | solution.py:582
  (1 shorter events, 0.0 us)
Async XLA Ops:
  1.9 27.9 %copy-start = (f32[1,2,2,18,4096]{4,2,3,1,0:T(2,128)S(1)}, f32[1,2,2,18,4096]{4,2,3,1,0:T(2,128)}, u32[]{:S(2)}) copy-start(f32[1,2,2,18,4096]{4,2,3,1,0:T(2,128)} %param.13) | copy-start | bytes 3538948
  19.4 16.3 %collective-permute-start = (bf16[64,1536]{1,0:T(8,128)(2,1)}, bf16[64,1536]{1,0:T(8,128)(2,1)S(1)}, u32[]{:S(2)}, u32[]{:S(2)}) collective-permute-start(bf16[64,1536]{1,0:T(8,128)(2,1)} %get-tuple-element.17.refs_5_), channel_id=1, source_target_pairs={{0,1},{1,2},{2,3},{3,4},{4,5},{5,6},{6,7},{7,8},{8,9},{9,10},{10,1... | collective-permute-start | bytes 589832 | tf_op jit(solution)/shard_map/ppermute | solution.py:536
  24.5 12.4 %collective-permute-start.1 = (bf16[64,1536]{1,0:T(8,128)(2,1)}, bf16[64,1536]{1,0:T(8,128)(2,1)S(1)}, u32[]{:S(2)}, u32[]{:S(2)}) collective-permute-start(bf16[64,1536]{1,0:T(8,128)(2,1)} %get-tuple-element.18.refs_6_), channel_id=1, source_target_pairs={{1,0},{2,1},{3,2},{4,3},{5,4},{6,5},{7,6},{8,7},{9,8},{10,9},{11,1... | collective-permute-start | bytes 589832 | tf_op jit(solution)/shard_map/ppermute | solution.py:537
  35.7 1.2 %copy-start.1 = (bf16[64,1536]{1,0:T(8,128)(2,1)}, bf16[64,1536]{1,0:T(8,128)(2,1)S(1)}, u32[]{:S(2)}) copy-start(bf16[64,1536]{1,0:T(8,128)(2,1)S(1)} %collective-permute-done.refs_7_) | copy-start | bytes 589828
  36.9 0.7 copy-start.2

commit v7 on v6

--- a/solution.py
+++ b/solution.py
@@ -53,7 +53,7 @@
 
 
 def place(pat, copy, proj, n, blocks_d, blocks_f):
-    value = pat[copy * 2 + proj, n]
+    value = pat[16 + copy * 2 + proj, n]
     if proj == 0:
         r = value // blocks_f
         return r, value - r * blocks_f
@@ -83,7 +83,7 @@
 def build_lists(pat, lists, blocks_d, blocks_f):
     f32 = jnp.float32
     dummy = blocks_d * 128 + blocks_f * 4096
-    value = pat[...].astype(f32)
+    value = pat.astype(f32)
     which = lax.broadcasted_iota(jnp.int32, (8, 128), 0)
     lane = lax.broadcasted_iota(jnp.int32, (8, 128), 1).astype(f32)
     width = jnp.where(which % 2 == 0, f32(blocks_f), f32(blocks_d))
@@ -161,6 +161,19 @@
     batched(trips(lists), PER, body)
 
 
+def keep_own(wide, own, quarter):
+    first, half = lax.axis_index("dp") * quarter, BLOCK // 2
+
+    def step(n, carry):
+        for which in range(4):
+            copy, proj = divmod(which, 2)
+            rows = wide[which, pl.ds(pl.multiple_of((first + n) * PITCH, 8), half, stride=2), :]
+            own[copy, pl.ds(n * BLOCK + proj, half, stride=2), :] = rows
+        return carry
+
+    lax.fori_loop(0, quarter, step, 0, unroll=2)
+
+
 def section_pass(lists, w, x, gy, pre, gh):
     def body(i):
         terms = []
@@ -206,15 +219,22 @@
 
 
 def first_kernel(
-    pat, acts_in, cot_in, stash_in, raw, send_up, send_down, hid_out, gp_out, lists_out, w_out,
-    acts, cot, stash, hid, gp, lists, wide, w, x, gy, pre, gh, out, sem,
+    sections, pattern, acts_in, cot_in, stash_in, raw_in, send_up, send_down, hid_out, gp_out, lists_out, w_out, own,
+    acts, cot, stash, raw, hid, gp, lists, wide, w, x, gy, pre, gh, out, sem,
 ):
     blocks_d, blocks_f = out.shape[0] - 1, pre.shape[0] - 1
     reads = [begin(acts_in, acts, sem.at[0]), begin(cot_in, cot, sem.at[1]), begin(stash_in, stash, sem.at[2])]
-    build_lists(pat, lists_out, blocks_d, blocks_f)
+    fetch = begin(raw_in, raw, sem.at[7])
+    me, count = lax.axis_index("pipe"), raw.shape[2]
+    lists_out[16:24, :] = jnp.full((8, 128), -1, jnp.int32)
+    lists_out[16:18, 0:count] = pattern[me]
+    lists_out[18:20, 0:count] = pattern[sections - 1 - me]
+    build_lists(lists_out[16:24, :], lists_out, blocks_d, blocks_f)
     begin(lists_out, lists, sem.at[3]).wait()
+    fetch.wait()
     prepare_weights(lists, raw, wide, w)
     writes = [begin(w, w_out, sem.at[4])]
+    keep_own(wide, own, count // 4)
     clear(lists, (pre, gh))
     for read in reads:
         read.wait()
@@ -345,6 +365,26 @@
     lax.fori_loop(0, blocks_d // 2, store, 0, unroll=4)
     for write in writes:
         write.wait()
+
+
+def swap_kernel(sections, up, down, got_up, got_down, sent, got):
+    me, group = lax.axis_index("pipe"), lax.axis_index("dp")
+    after, before = lax.rem(me + 1, sections), lax.rem(me + sections - 1, sections)
+    barrier = pltpu.get_barrier_semaphore()
+    for other in (after, before):
+        pl.semaphore_signal(barrier, inc=1, device_id=(group, other), device_id_type=pl.DeviceIdType.MESH)
+    pl.semaphore_wait(barrier, 2)
+    wires = [
+        pltpu.make_async_remote_copy(
+            src_ref=source, dst_ref=target, send_sem=sent.at[i], recv_sem=got.at[i],
+            device_id=(group, to), device_id_type=pl.DeviceIdType.MESH,
+        )
+        for i, (source, target, to) in enumerate(((up, got_up, after), (down, got_down, before)))
+    ]
+    for wire in wires:
+        wire.start()
+    for wire in wires:
+        wire.wait()
 
 
 def two_wide(value):
@@ -489,16 +529,8 @@
 
 def shards(acts_in, cot_in, stash, entering, pattern, weights, momentum):
     bf16, f32 = jnp.bfloat16, jnp.float32
-    me, sections = lax.axis_index("pipe"), lax.axis_size("pipe")
-    group = lax.axis_index("dp")
+    sections = lax.axis_size("pipe")
     acts, cot, saved, fresh = (jnp.swapaxes(one, -1, -2) for one in (acts_in[0, 0], cot_in[0, 0], stash[0, 0], entering[0]))
-    pat = jnp.concatenate(
-        [
-            lax.dynamic_index_in_dim(pattern, me, 0, keepdims=False),
-            lax.dynamic_index_in_dim(pattern, sections - 1 - me, 0, keepdims=False),
-        ]
-    )
-    pat = jnp.pad(pat, ((0, 4), (0, 128 - pat.shape[1])), constant_values=-1)
     tokens, width = acts.shape[1:]
     count = weights.shape[3]
     blocks_d, blocks_f = width // BLOCK, FF // BLOCK
@@ -506,24 +538,26 @@
     d_block, f_block = (blocks_d, BLOCK, 128), (blocks_f + 1, BLOCK, 128)
     x_block, out_block = (2, blocks_d + 1, BLOCK, 128), (blocks_d + 1, BLOCK, 128)
     w_shape = (2, 2, 2, count, BLOCK, BLOCK)
-    send_up, send_down, hid, gp, lists, w = call(
-        first_kernel,
-        [("v", pat), ("a", acts), ("a", cot), ("a", saved), ("v", raw)],
+    send_up, send_down, hid, gp, lists, w, own = call(
+        lambda *refs: first_kernel(sections, *refs),
+        [("v", pattern), ("a", acts), ("a", cot), ("a", saved), ("a", raw)],
         [
             ("v", (2 * tokens, width), bf16),
             ("v", (2 * tokens, width), bf16),
             ("a", f_block, bf16),
             ("a", f_block, bf16),
-            ("v", (16, 128), jnp.int32),
+            ("v", (24, 128), jnp.int32),
             ("a", w_shape, bf16),
+            ("v", (2, count // 4 * BLOCK, 128), f32),
         ],
         [
             ("v", acts.shape, bf16),
             ("v", cot.shape, bf16),
             ("v", saved.shape, bf16),
+            ("v", raw.shape, bf16),
             ("v", f_block, bf16),
             ("v", f_block, bf16),
-            ("s", (16, 128), jnp.int32),
+            ("s", (24, 128), jnp.int32),
             ("v", (4, count * PITCH, 128), f32),
             ("v", w_shape, bf16),
             ("v", x_block, bf16),
@@ -533,8 +567,14 @@
             ("v", out_block, f32),
         ],
     )
-    got_up = lax.ppermute(send_up, "pipe", [(i, i + 1) for i in range(sections - 1)])
-    got_down = lax.ppermute(send_down, "pipe", [(i + 1, i) for i in range(sections - 1)])
+    got_up, got_down = pl.pallas_call(
+        lambda *refs: swap_kernel(sections, *refs),
+        out_shape=[jax.ShapeDtypeStruct(send_up.shape, bf16)] * 2,
+        in_specs=[pl.BlockSpec(memory_space=pltpu.VMEM)] * 2,
+        out_specs=[pl.BlockSpec(memory_space=pltpu.VMEM)] * 2,
+        scratch_shapes=[pltpu.SemaphoreType.DMA((2,))] * 2,
+        compiler_params=pltpu.CompilerParams(collective_id=1, has_side_effects=True),
+    )(send_up, send_down)
     vectors = (acts, cot, saved, fresh, send_up, send_down, got_up, got_down)
     forward, backward, xs, gys, hid, gp = call(
         lambda *refs: second_kernel(sections, *refs),
@@ -576,10 +616,9 @@
         ]
         + [pltpu.SemaphoreType.DMA((4 * PARTS,))] * 8,
         compiler_params=pltpu.CompilerParams(collective_id=0, has_side_effects=True, vmem_limit_bytes=VMEM_BYTES),
-    )(pat, xs, gys, hid, gp)
-    own = lax.dynamic_slice_in_dim(weights[0], group * quarter, quarter, axis=2)
+    )(lists, xs, gys, hid, gp)
     momentum_next = BETA * dense(momentum[0]) + total / (2 * tokens)
-    weights_next = spread_out((dense(own).astype(f32) - STEP * momentum_next).astype(bf16))
+    weights_next = spread_out((own - STEP * momentum_next).astype(bf16))
     momentum_next = spread_out(momentum_next)
     forward, backward = jnp.swapaxes(forward, 1, 2), jnp.swapaxes(backward, 1, 2)
     return forward[None, None], backward[None, None], weights_next[None], momentum_next[None]

time: 98.7 us -> 97.3 us (0.986)
  the two profiles are of different devices: /device:TPU:32 before, /device:TPU:1 now
where the time goes in v7:
time: 97.3 us; the launch traced here: 97.1 us
  Pallas kernels  93.3 us (96%)
  other arithmetic  2.04 us (2%)
  local copies, waits for them, and re-layouts  1 us (1%)
    pallas_call x1, Pallas kernels, shards(): pl.pallas_call(lambda *refs: sum_kernel(sections, quarter, *refs), out_sh...  42.9 us
    pallas_call x2, Pallas kernels, call(): pl.pallas_call(kernel, out_shape=[jax.ShapeDtypeStruct(*out[1:]) for out...  32.8 us
    pallas_call x1, Pallas kernels, shards(): pl.pallas_call(lambda *refs: swap_kernel(sections, *refs), out_shape=[jax...  17.6 us

profile of v7, /device:TPU:1, one launch (start us, length us, event | category | flops | bytes accessed | tf_op | source)
XLA Modules:
  0.0 97.1 jit_solution(17095036689122775074)
XLA Ops:
  0.6 17.7 %shard_map.102 = (bf16[64,1536]{1,0:T(8,128)(2,1)}, bf16[64,1536]{1,0:T(8,128)(2,1)}, bf16[97,64,128]{2,1,0:T(8,128)(2,1)}, bf16[97,64,128]{2,1,0:T(8,128)(2,1)}...) custom-call(s32[64,2,72]{2,1,0:T(2,128)} %refs_0_.1, ...), custom_call_target="tpu_custom_call" | custom-call | tf_op jit(solution)/shard_map/pallas_call | solution.py:508
  18.3 17.6 %shard_map.103 = (bf16[64,1536]{1,0:T(8,128)(2,1)}, bf16[64,1536]{1,0:T(8,128)(2,1)}) custom-call(bf16[64,1536]{1,0:T(8,128)(2,1)} %get-tuple-element.20.refs_0_.refs_5_, bf16[64,1536]{1,0:T(8,128)(2,1)} %get-tuple-element.21.refs_1_.refs_6_), custom_call_target="tpu_custom_call" | custom-call | tf_op jit(solution)/shard_map/pallas_call | solution.py:570
  35.9 15.1 %shard_map.104 = (bf16[2,32,1536]{2,1,0:T(8,128)(2,1)}, bf16[2,32,1536]{2,1,0:T(8,128)(2,1)}, bf16[2,24,64,128]{3,2,1,0:T(8,128)(2,1)}, bf16[2,24,64,128]{3,2,1,...) custom-call(s32[24,128]{1,0:T(8,128)} %get-tuple-element.19.refs_0_, ...), custom_call_target="tpu_custom_call" | custom-call | tf_op jit(solution)/shard_map/pallas_call | solution.py:508
  51.1 0.0 copy-start.1
  51.1 42.9 %shard_map.105 = f32[2,1152,128]{2,1,0:T(8,128)} custom-call(s32[24,128]{1,0:T(8,128)} %get-tuple-element.19.refs_0_, bf16[2,24,64,128]{3,2,1,0:T(8,128)(2,1)} %get-tuple-element.30.refs_1_, bf16[2,24,64,128]{3,2,1,0:T(8,128)(2,1)} %get-tuple-element.31.refs_2_, bf16[97,64,128]{2,1,0:T(8,128)(2,1)} %get-tuple-element.32.refs_3_, ...), custom_call_target="tpu_custom_call" | custom-call | tf_op jit(solution)/shard_map/pallas_call | solution.py:600
  94.0 0.0 copy-done.1
  94.0 0.0 copy-start
  94.0 0.0 copy-start.2
  94.0 0.6 broadcast_multiply_fusion
  94.7 0.6 copy-done
  95.3 0.4 copy-done.2
  95.6 1.4 %subtract_convert_fusion = (bf16[2,1152,128]{2,1,0:T(8,128)(2,1)}, f32[2,1152,128]{2,1,0:T(8,128)}) fusion(f32[2,1152,128]{2,1,0:T(8,128)S(1)} %copy-done.2, f32[2,1152,128]{2,1,0:T(8,128)S(1)} %bitcast.46, f32[2,1152,128]{2,1,0:T(8,128)S(1)} %copy-done), kind=kLoop, calls=%fused_computation | loop fusion | flops 1474560 | bytes 5308416 | tf_op jit(solution)/shard_map/convert_element_type | solution.py:621
Async XLA Ops:
  51.1 42.9 %copy-start.1 = (f32[1,2,2,18,4096]{4,2,3,1,0:T(2,128)S(1)}, f32[1,2,2,18,4096]{4,2,3,1,0:T(2,128)}, u32[]{:S(2)}) copy-start(f32[1,2,2,18,4096]{4,2,3,1,0:T(2,128)} %param.13) | copy-start | bytes 3538948
  94.0 1.3 %copy-start = (f32[2,1152,128]{2,1,0:T(8,128)S(1)}, f32[2,1152,128]{2,1,0:T(8,128)}, u32[]{:S(2)}) copy-start(f32[2,1152,128]{2,1,0:T(8,128)} %shard_map.105) | copy-start | bytes 3538948
  94.0 1.6 %copy-start.2 = (f32[2,1152,128]{2,1,0:T(8,128)S(1)}, f32[2,1152,128]{2,1,0:T(8,128)}, u32[]{:S(2)}) copy-start(f32[2,1152,128]{2,1,0:T(8,128)} %get-tuple-element.29) | copy-start | bytes 3538948
